TPU v7x, 32 devices: a whole 2x2x4 slice. The times are simulated.
32 devices in a mesh: section: 2 (over core), dp: 2 (over y), tensor: 8 (over z, x).
Axes of the slice: x: 2, y: 2, z: 4, core: 2. Of those that a mesh axis runs over, the one named last changes fastest.
Arguments:
- boundary: bfloat16 [2, 4, 1024, 4, 1024], P('section', None, 'tensor', 'dp'), may hold values from -6 to 6
- segment_ids: int32 [4, 4, 1024], P(None, 'dp'), may hold values from -1 to 31, as said below
- project_weight: bfloat16 [2, 1024, 3, 1024], P('section', None, None, 'tensor'), may hold values from -0.1875 to 0.1875
- project_bias: bfloat16 [2, 3, 1024], P('section', None, 'tensor'), may hold values from -3 to 3
- output_weight: bfloat16 [2, 1024, 1024], P('section', 'tensor'), may hold values from -2 to 2
- output_biases: bfloat16 [2, 2, 1024], P('section'), may hold values from -3 to 3
- norm_gains: bfloat16 [2, 2, 1024], P('section'), may hold values from 0.5 to 1.5
- norm_shifts: bfloat16 [2, 2, 1024], P('section'), may hold values from -2 to 2
- up_weight: bfloat16 [2, 1024, 4096], P('section', None, 'tensor'), may hold values from -0.1875 to 0.1875
- up_bias: bfloat16 [2, 4096], P('section', 'tensor'), may hold values from -3 to 3
- down_weight: bfloat16 [2, 4096, 1024], P('section', 'tensor'), may hold values from -0.09375 to 0.09375
- prefix_keys: bfloat16 [2, 20, 1024], P('section', None, 'tensor'), may hold values from -6 to 6
- prefix_values: bfloat16 [2, 20, 1024], P('section', None, 'tensor'), may hold values from -6 to 6
Outputs:
- result: bfloat16 [2, 4, 1024, 4, 1024], P('section', None, 'tensor', 'dp')
- key_grad: float32 [2, 20, 1024], P('section', None, 'tensor')
- value_grad: float32 [2, 20, 1024], P('section', None, 'tensor')
Inputs may be any that keep to these rules, and one draw needn't show every extreme that they name: `segment_ids`: ids count a row's segments from 0 in order of position; each segment spans 1 to 96 slots, except in rows that are a single segment over all 1024 slots; -1 marks fewer than 128 padding slots at a row's end; in each micro-batch, one row of every aligned group of 2 rows is a single segment over all 1024 slots.
All inputs are finite; a program needn't handle non-finite values.
Results may differ from a plain program's by a relative error of at most 0.023.
Values may be sent and summed in bfloat16 or wider, within the bound.
No kernel may reach another device: no remote copies, remote signals or barrier semaphores. Data moves between devices by JAX's collectives and lax.ppermute only.
A program may use at most 192 MiB of HBM per device.

v0:
```python
from functools import partial
import math

import jax
import jax.numpy as jnp
from jax import lax
from jax.sharding import PartitionSpec as P

HEAD = 64


norm_epsilon = 1e-05
masked_fill = -1000000000.0


def shifted(block, axis, distance):
    devices = range(lax.axis_size(axis))
    route = [(i - distance, i) for i in devices if i - distance in devices]
    return lax.ppermute(block, axis, route)


def normalize(hidden, gain, shift):
    average = jnp.mean(hidden, axis=-1, keepdims=True)
    centered = hidden - average
    variance = jnp.mean(centered * centered, axis=-1, keepdims=True)
    inverse = lax.rsqrt(variance + norm_epsilon)
    normed = centered * inverse
    return (normed * gain + shift, normed, inverse)


def normalize_back(grad, normed, inverse, gain):
    scaled = grad * gain
    return inverse * (
        scaled
        - jnp.mean(scaled, axis=-1, keepdims=True)
        - normed * jnp.mean(scaled * normed, axis=-1, keepdims=True)
    )


def against(left, right):
    return lax.dot_general(
        left, right, (((1,), (1,)), ((), ())), preferred_element_type=jnp.float32
    )


def row_softmax(queries, key_rows, query_segments, key_segments):
    query_count = query_segments.shape[0]
    prefix_count = key_rows.shape[0] - key_segments.shape[0]
    scores = jnp.einsum("qhe,khe->hqk", queries, key_rows, preferred_element_type=jnp.float32) * (
        1.0 / math.sqrt(HEAD)
    )
    same = (query_segments[:, None] == key_segments[None, :]) & (key_segments[None, :] >= 0)
    allowed = jnp.concatenate(
        [jnp.ones((query_count, prefix_count), dtype=jnp.bool_), same], axis=1
    )
    scores = jnp.where(allowed[None], scores, masked_fill)
    largest = jnp.max(scores, axis=-1, keepdims=True)
    raised = jnp.exp(scores - largest)
    return raised / jnp.sum(raised, axis=-1, keepdims=True)


def split_rows(projected, rows):
    length = projected.shape[0] // rows
    heads_here = projected.shape[1] // (3 * HEAD)
    return jnp.transpose(projected.reshape(length, rows, 3, heads_here, HEAD), (1, 2, 0, 3, 4))


def prefix_tables(params):
    prefix_keys, prefix_values = (params[9], params[10])
    heads_here = prefix_keys.shape[1] // HEAD
    return (
        prefix_keys.reshape(prefix_keys.shape[0], heads_here, HEAD),
        prefix_values.reshape(prefix_values.shape[0], heads_here, HEAD),
    )


def layer_forward(tokens_in, segments, params):
    (
        project_weight,
        project_bias,
        output_weight,
        output_biases,
        norm_gains,
        norm_shifts,
        up_weight,
        up_bias,
        down_weight,
        prefix_keys,
        prefix_values,
    ) = params
    rows = segments.shape[0]
    project_flat = project_weight.reshape(project_weight.shape[0], -1)
    bias_flat = project_bias.reshape(-1).astype(jnp.float32)
    prefix_key_rows, prefix_value_rows = prefix_tables(params)
    projected = (
        jnp.dot(
            lax.all_gather(tokens_in, "tensor", axis=0, tiled=True),
            project_flat,
            preferred_element_type=jnp.float32,
        )
        + bias_flat
    ).astype(jnp.bfloat16)
    parts = split_rows(projected, rows)

    def attend(items):
        part, segment_row = items
        key_rows = jnp.concatenate([prefix_key_rows, part[1]], axis=0)
        value_rows = jnp.concatenate([prefix_value_rows, part[2]], axis=0)
        attention = row_softmax(part[0], key_rows, segment_row, segment_row).astype(jnp.bfloat16)
        return jnp.einsum(
            "hqk,khe->qhe", attention, value_rows, preferred_element_type=jnp.float32
        ).astype(jnp.bfloat16)

    mixed = lax.map(attend, (parts, segments))
    mixed = jnp.transpose(mixed, (1, 0, 2, 3)).reshape(projected.shape[0], -1)
    attended = lax.psum_scatter(
        jnp.dot(mixed, output_weight, preferred_element_type=jnp.float32),
        "tensor",
        scatter_dimension=0,
        tiled=True,
    )
    normed_first, unit_first, inverse_first = normalize(
        tokens_in.astype(jnp.float32) + attended + output_biases[0].astype(jnp.float32),
        norm_gains[0].astype(jnp.float32),
        norm_shifts[0].astype(jnp.float32),
    )
    pre_act = jnp.dot(
        lax.all_gather(normed_first.astype(jnp.bfloat16), "tensor", axis=0, tiled=True),
        up_weight,
        preferred_element_type=jnp.float32,
    ) + up_bias.astype(jnp.float32)
    activated = jax.nn.gelu(pre_act, approximate=False).astype(jnp.bfloat16)
    hidden_out = lax.psum_scatter(
        jnp.dot(activated, down_weight, preferred_element_type=jnp.float32),
        "tensor",
        scatter_dimension=0,
        tiled=True,
    )
    layer_out, unit_second, inverse_second = normalize(
        normed_first + hidden_out + output_biases[1].astype(jnp.float32),
        norm_gains[1].astype(jnp.float32),
        norm_shifts[1].astype(jnp.float32),
    )
    return (layer_out, (projected, pre_act, unit_first, inverse_first, unit_second, inverse_second))


def layer_backward(grad_in, segments, kept, params):
    (
        project_weight,
        project_bias,
        output_weight,
        output_biases,
        norm_gains,
        norm_shifts,
        up_weight,
        up_bias,
        down_weight,
        prefix_keys,
        prefix_values,
    ) = params
    projected, pre_act, unit_first, inverse_first, unit_second, inverse_second = kept
    rows = segments.shape[0]
    prefix_count = prefix_keys.shape[0]
    project_flat = project_weight.reshape(project_weight.shape[0], -1)
    prefix_key_rows, prefix_value_rows = prefix_tables(params)
    scale = 1.0 / math.sqrt(HEAD)
    d_second = normalize_back(
        grad_in.astype(jnp.float32), unit_second, inverse_second, norm_gains[1].astype(jnp.float32)
    )
    d_hidden = d_second.astype(jnp.bfloat16)
    d_act = against(lax.all_gather(d_hidden, "tensor", axis=0, tiled=True), down_weight)
    gelu_back = jax.vjp(partial(jax.nn.gelu, approximate=False), pre_act)[1]
    d_pre = gelu_back(d_act)[0].astype(jnp.bfloat16)
    d_normed = d_second + lax.psum_scatter(
        against(d_pre, up_weight).astype(jnp.bfloat16), "tensor", scatter_dimension=0, tiled=True
    ).astype(jnp.float32)
    d_first = normalize_back(d_normed, unit_first, inverse_first, norm_gains[0].astype(jnp.float32))
    d_attended = d_first.astype(jnp.bfloat16)
    d_mixed = against(
        lax.all_gather(d_attended, "tensor", axis=0, tiled=True), output_weight
    ).astype(jnp.bfloat16)
    parts = split_rows(projected, rows)
    length = projected.shape[0] // rows
    d_rows = jnp.transpose(d_mixed.reshape(length, rows, parts.shape[3], HEAD), (1, 0, 2, 3))

    def attend_back(items):
        part, d_out, segment_row = items
        key_rows = jnp.concatenate([prefix_key_rows, part[1]], axis=0)
        value_rows = jnp.concatenate([prefix_value_rows, part[2]], axis=0)
        attention = row_softmax(part[0], key_rows, segment_row, segment_row)
        rounded = attention.astype(jnp.bfloat16)
        d_prob = jnp.einsum("qhe,khe->hqk", d_out, value_rows, preferred_element_type=jnp.float32)
        delta = jnp.sum(attention * d_prob, axis=-1, keepdims=True)
        d_score = (attention * (d_prob - delta)).astype(jnp.bfloat16)
        d_query = (
            jnp.einsum("hqk,khe->qhe", d_score, key_rows, preferred_element_type=jnp.float32)
            * scale
        )
        d_key = (
            jnp.einsum("hqk,qhe->khe", d_score, part[0], preferred_element_type=jnp.float32) * scale
        )
        d_value = jnp.einsum("hqk,qhe->khe", rounded, d_out, preferred_element_type=jnp.float32)
        local_grad = jnp.stack([d_query, d_key[prefix_count:], d_value[prefix_count:]]).astype(
            jnp.bfloat16
        )
        return (local_grad, d_key[:prefix_count], d_value[:prefix_count])

    d_parts, key_rows_grad, value_rows_grad = lax.map(attend_back, (parts, d_rows, segments))
    key_part = jnp.sum(key_rows_grad, axis=0).reshape(prefix_count, -1)
    value_part = jnp.sum(value_rows_grad, axis=0).reshape(prefix_count, -1)
    d_projected = jnp.transpose(d_parts, (2, 0, 1, 3, 4)).reshape(projected.shape[0], -1)
    input_grad = d_first + lax.psum_scatter(
        against(d_projected, project_flat).astype(jnp.bfloat16),
        "tensor",
        scatter_dimension=0,
        tiled=True,
    ).astype(jnp.float32)
    return (input_grad, key_part, value_part)


def per_device(
    boundary,
    segment_ids,
    project_weight,
    project_bias,
    output_weight,
    output_biases,
    norm_gains,
    norm_shifts,
    up_weight,
    up_bias,
    down_weight,
    prefix_keys,
    prefix_values,
):
    section_index = lax.axis_index("section")
    first_section = section_index == 0
    micro_count = boundary.shape[1]
    shard_length, rows, width = (boundary.shape[2], boundary.shape[3], boundary.shape[4])
    count = shard_length * rows
    tick_count = micro_count + 2
    params = tuple(
        (
            entry[0]
            for entry in (
                project_weight,
                project_bias,
                output_weight,
                output_biases,
                norm_gains,
                norm_shifts,
                up_weight,
                up_bias,
                down_weight,
                prefix_keys,
                prefix_values,
            )
        )
    )
    run_forward = partial(layer_forward, params=params)
    run_backward = partial(layer_backward, params=params)
    prefix_width = params[9].shape[1]

    def slab(index):
        clipped = min(max(index, 0), micro_count - 1)
        return boundary[0, clipped].reshape(count, width)

    arrived = jnp.zeros((count, width), jnp.bfloat16)
    returned = jnp.zeros((count, width), jnp.bfloat16)
    key_total = jnp.zeros((prefix_keys.shape[1], prefix_width), jnp.float32)
    value_total = jnp.zeros((prefix_values.shape[1], prefix_width), jnp.float32)
    forward_out = []
    backward_out = []
    stored = []
    for moment in range(tick_count):
        forward_in = jnp.where(first_section, slab(moment), arrived)
        segments_clipped = jnp.clip(moment - section_index, 0, micro_count - 1)
        forward_segments = lax.dynamic_index_in_dim(
            segment_ids, segments_clipped, 0, keepdims=False
        )
        layer_out, kept = run_forward(forward_in, forward_segments)
        stored.append(kept + (forward_segments,))
        earlier = stored[max(moment - 2, 0)]
        chosen = tuple(
            (
                jnp.where(first_section, older, newer)
                for older, newer in zip(earlier, stored[moment])
            )
        )
        back_state = chosen[:-1]
        back_segments = chosen[-1]
        out_low = layer_out.astype(jnp.bfloat16)
        grad_in = jnp.where(first_section, returned, slab(moment - 1))
        input_grad, key_part, value_part = run_backward(grad_in, back_segments, back_state)
        grad_low = input_grad.astype(jnp.bfloat16)
        back_index = moment - 2 + section_index
        valid = ((back_index >= 0) & (back_index < micro_count)).astype(jnp.float32)
        key_part = key_part * valid
        value_part = value_part * valid
        key_part, value_part = lax.psum((key_part, value_part), "dp")
        key_total = key_total + key_part
        value_total = value_total + value_part
        if moment + 1 < tick_count:
            arrived = shifted(out_low, "section", 1)
            returned = shifted(grad_low, "section", -1)
        forward_out.append(out_low)
        backward_out.append(grad_low)
    pieces = [
        jnp.where(first_section, backward_out[index + 2], forward_out[index + 1])
        for index in range(micro_count)
    ]
    result = jnp.stack(pieces).reshape(1, micro_count, shard_length, rows, width)
    return (result, key_total[None], value_total[None])


def solution(mesh):
    in_specs = (
        P("section", None, "tensor", "dp", None),
        P(None, "dp", None),
        P("section", None, None, "tensor"),
        P("section", None, "tensor"),
        P("section", "tensor", None),
        P("section", None, None),
        P("section", None, None),
        P("section", None, None),
        P("section", None, "tensor"),
        P("section", "tensor"),
        P("section", "tensor", None),
        P("section", None, "tensor"),
        P("section", None, "tensor"),
    )
    out_specs = (
        P("section", None, "tensor", "dp", None),
        P("section", None, "tensor"),
        P("section", None, "tensor"),
    )
    return jax.shard_map(
        per_device, mesh=mesh, in_specs=in_specs, out_specs=out_specs, check_vma=False
    )
```

profile of v0, /device:TPU:0, one launch (start us, length us, event | category | flops | bytes accessed | tf_op | source)
XLA Modules:
  0.0 5625.2 jit_solution(12935964441329114780)
XLA Ops:
  14.8 73.4 %all-gather.25.cloned.1.call-done = bf16[2048,1024]{1,0:T(8,128)(2,1)} async-done(((bf16[256,1024]{1,0:T(8,128)(2,1)}), bf16[2048,1024]{1,0:T(8,128)(2,1)}) %all-gather.25.cloned.1.call-update) | async-done | bytes 4194320 | tf_op jit(solution)/shard_map/all_gather | solution.py:97
  147.3 146.6 %reduce-scatter.25.cloned.1.call-done = f32[256,1024]{1,0:T(8,128)} async-done(((f32[2048,1024]{1,0:T(8,128)}), f32[256,1024]{1,0:T(8,128)}) %reduce-scatter.25.cloned.1.call-update) | async-done | bytes 1048592 | tf_op jit(solution)/shard_map/reduce_scatter | solution.py:116
  299.4 72.5 %all-gather.27.cloned.1.call-done = bf16[2048,1024]{1,0:T(8,128)(2,1)} async-done(((bf16[256,1024]{1,0:T(8,128)(2,1)}), bf16[2048,1024]{1,0:T(8,128)(2,1)}) %all-gather.27.cloned.1.call-update) | async-done | bytes 4194320 | tf_op jit(solution)/shard_map/all_gather | solution.py:128
  393.3 145.4 %reduce-scatter.27.cloned.1.call-done = f32[256,1024]{1,0:T(8,128)} async-done(((f32[2048,1024]{1,0:T(8,128)}), f32[256,1024]{1,0:T(8,128)}) %reduce-scatter.27.cloned.1.call-update) | async-done | bytes 1048592 | tf_op jit(solution)/shard_map/reduce_scatter | solution.py:133
  547.5 68.0 %all-gather.37.cloned.1.call-done = bf16[2048,1024]{1,0:T(8,128)(2,1)} async-done(((bf16[256,1024]{1,0:T(8,128)(2,1)}), bf16[2048,1024]{1,0:T(8,128)(2,1)}) %all-gather.37.cloned.1.call-update) | async-done | bytes 4194320 | tf_op jit(solution)/shard_map/all_gather | solution.py:171
  634.1 55.1 all-gather.29.cloned.1.call-done
  780.4 151.5 %reduce-scatter.29.cloned.1.call-done = f32[256,1024]{1,0:T(8,128)} async-done(((f32[2048,1024]{1,0:T(8,128)}), f32[256,1024]{1,0:T(8,128)}) %reduce-scatter.29.cloned.1.call-update) | async-done | bytes 1048592 | tf_op jit(solution)/shard_map/reduce_scatter | solution.py:116
  938.1 71.9 %all-gather.39.cloned.1.call-done = bf16[2048,1024]{1,0:T(8,128)(2,1)} async-done(((bf16[256,1024]{1,0:T(8,128)(2,1)}), bf16[2048,1024]{1,0:T(8,128)(2,1)}) %all-gather.39.cloned.1.call-update) | async-done | bytes 4194320 | tf_op jit(solution)/shard_map/all_gather | solution.py:180
  1021.1 92.5 %while.147 = (s32[]{:T(128)}, bf16[2,3,1024,2,64]{2,4,3,1,0:T(8,128)(2,1)}, f32[2,20,2,64]{1,3,2,0:T(8,128)}, f32[2,20,2,64]{1,3,2,0:T(8,128)}, bf16[2,3,1024,2,...) while((s32[]{:T(128)}, ...), condition=%wide.region_39.40_spmd, body=%wide.region_35.39_spmd.sunk | while | flops 1683273216 | bytes 68641464 | solution.py:208
  1153.7 65.9 %reduce-scatter.39.cloned.1.call-done = bf16[256,1024]{1,0:T(8,128)(2,1)} async-done(((bf16[2048,1024]{1,0:T(8,128)(2,1)}), bf16[256,1024]{1,0:T(8,128)(2,1)}) %reduce-scatter.39.cloned.1.call-update) | async-done | bytes 524304 | tf_op jit(solution)/shard_map/reduce_scatter | solution.py:212
  1223.3 149.0 %reduce-scatter.31.cloned.1.call-done = f32[256,1024]{1,0:T(8,128)} async-done(((f32[2048,1024]{1,0:T(8,128)}), f32[256,1024]{1,0:T(8,128)}) %reduce-scatter.31.cloned.1.call-update) | async-done | bytes 1048592 | tf_op jit(solution)/shard_map/reduce_scatter | solution.py:133
  1382.2 68.5 %all-gather.41.cloned.1.call-done = bf16[2048,1024]{1,0:T(8,128)(2,1)} async-done(((bf16[256,1024]{1,0:T(8,128)(2,1)}), bf16[2048,1024]{1,0:T(8,128)(2,1)}) %all-gather.41.cloned.1.call-update) | async-done | bytes 4194320 | tf_op jit(solution)/shard_map/all_gather | solution.py:171
  1470.6 53.9 all-gather.33.cloned.1.call-done
  1616.2 151.0 %reduce-scatter.33.cloned.1.call-done = f32[256,1024]{1,0:T(8,128)} async-done(((f32[2048,1024]{1,0:T(8,128)}), f32[256,1024]{1,0:T(8,128)}) %reduce-scatter.33.cloned.1.call-update) | async-done | bytes 1048592 | tf_op jit(solution)/shard_map/reduce_scatter | solution.py:116
  1772.4 72.5 %all-gather.35.cloned.1.call-done = bf16[2048,1024]{1,0:T(8,128)(2,1)} async-done(((bf16[256,1024]{1,0:T(8,128)(2,1)}), bf16[2048,1024]{1,0:T(8,128)(2,1)}) %all-gather.35.cloned.1.call-update) | async-done | bytes 4194320 | tf_op jit(solution)/shard_map/all_gather | solution.py:128
  1864.3 147.4 %reduce-scatter.35.cloned.1.call-done = f32[256,1024]{1,0:T(8,128)} async-done(((f32[2048,1024]{1,0:T(8,128)}), f32[256,1024]{1,0:T(8,128)}) %reduce-scatter.35.cloned.1.call-update) | async-done | bytes 1048592 | tf_op jit(solution)/shard_map/reduce_scatter | solution.py:133
  2020.0 73.8 %all-gather.49.cloned.1.call-done = bf16[2048,1024]{1,0:T(8,128)(2,1)} async-done(((bf16[256,1024]{1,0:T(8,128)(2,1)}), bf16[2048,1024]{1,0:T(8,128)(2,1)}) %all-gather.49.cloned.1.call-update) | async-done | bytes 4194320 | tf_op jit(solution)/shard_map/all_gather | solution.py:97
  2150.1 147.4 %reduce-scatter.49.cloned.1.call-done = f32[256,1024]{1,0:T(8,128)} async-done(((f32[2048,1024]{1,0:T(8,128)}), f32[256,1024]{1,0:T(8,128)}) %reduce-scatter.49.cloned.1.call-update) | async-done | bytes 1048592 | tf_op jit(solution)/shard_map/reduce_scatter | solution.py:116
  2300.4 72.5 %all-gather.51.cloned.1.call-done = bf16[2048,1024]{1,0:T(8,128)(2,1)} async-done(((bf16[256,1024]{1,0:T(8,128)(2,1)}), bf16[2048,1024]{1,0:T(8,128)(2,1)}) %all-gather.51.cloned.1.call-update) | async-done | bytes 4194320 | tf_op jit(solution)/shard_map/all_gather | solution.py:128
  2392.3 147.3 %reduce-scatter.51.cloned.1.call-done = f32[256,1024]{1,0:T(8,128)} async-done(((f32[2048,1024]{1,0:T(8,128)}), f32[256,1024]{1,0:T(8,128)}) %reduce-scatter.51.cloned.1.call-update) | async-done | bytes 1048592 | tf_op jit(solution)/shard_map/reduce_scatter | solution.py:133
  2546.9 72.8 %all-gather.57.cloned.1.call-done = bf16[2048,1024]{1,0:T(8,128)(2,1)} async-done(((bf16[256,1024]{1,0:T(8,128)(2,1)}), bf16[2048,1024]{1,0:T(8,128)(2,1)}) %all-gather.57.cloned.1.call-update) | async-done | bytes 4194320 | tf_op jit(solution)/shard_map/all_gather | solution.py:97
  2675.9 147.4 %reduce-scatter.57.cloned.1.call-done = f32[256,1024]{1,0:T(8,128)} async-done(((f32[2048,1024]{1,0:T(8,128)}), f32[256,1024]{1,0:T(8,128)}) %reduce-scatter.57.cloned.1.call-update) | async-done | bytes 1048592 | tf_op jit(solution)/shard_map/reduce_scatter | solution.py:116
  2826.9 72.5 %all-gather.59.cloned.1.call-done = bf16[2048,1024]{1,0:T(8,128)(2,1)} async-done(((bf16[256,1024]{1,0:T(8,128)(2,1)}), bf16[2048,1024]{1,0:T(8,128)(2,1)}) %all-gather.59.cloned.1.call-update) | async-done | bytes 4194320 | tf_op jit(solution)/shard_map/all_gather | solution.py:128
  2919.3 146.8 %reduce-scatter.59.cloned.1.call-done = f32[256,1024]{1,0:T(8,128)} async-done(((f32[2048,1024]{1,0:T(8,128)}), f32[256,1024]{1,0:T(8,128)}) %reduce-scatter.59.cloned.1.call-update) | async-done | bytes 1048592 | tf_op jit(solution)/shard_map/reduce_scatter | solution.py:133
  3073.3 67.5 %all-gather.43.cloned.1.call-done = bf16[2048,1024]{1,0:T(8,128)(2,1)} async-done(((bf16[256,1024]{1,0:T(8,128)(2,1)}), bf16[2048,1024]{1,0:T(8,128)(2,1)}) %all-gather.43.cloned.1.call-update) | async-done | bytes 4194320 | tf_op jit(solution)/shard_map/all_gather | solution.py:180
  3147.0 67.8 %all-gather.65.cloned.1.call-done = bf16[2048,1024]{1,0:T(8,128)(2,1)} async-done(((bf16[256,1024]{1,0:T(8,128)(2,1)}), bf16[2048,1024]{1,0:T(8,128)(2,1)}) %all-gather.65.cloned.1.call-update) | async-done | bytes 4194320 | tf_op jit(solution)/shard_map/all_gather | solution.py:97
  3237.7 91.7 %while.148 = (s32[]{:T(128)}, bf16[2,3,1024,2,64]{2,4,3,1,0:T(8,128)(2,1)}, f32[2,20,2,64]{1,3,2,0:T(8,128)S(1)}, f32[2,20,2,64]{1,3,2,0:T(8,128)S(1)}, bf16[2,3...) while((s32[]{:T(128)}, ...), condition=%wide.region_50.51_spmd, body=%wide.region_46.50_spmd.sunk | while | flops 1683273216 | bytes 68598952 | solution.py:208
  3349.3 86.4 %reduce-scatter.43.cloned.1.call-done = bf16[256,1024]{1,0:T(8,128)(2,1)} async-done(((bf16[2048,1024]{1,0:T(8,128)(2,1)}), bf16[256,1024]{1,0:T(8,128)(2,1)}) %reduce-scatter.43.cloned.1.call-update) | async-done | bytes 524304 | tf_op jit(solution)/shard_map/reduce_scatter | solution.py:212
  3443.5 74.1 %all-gather.45.cloned.1.call-done = bf16[2048,1024]{1,0:T(8,128)(2,1)} async-done(((bf16[256,1024]{1,0:T(8,128)(2,1)}), bf16[2048,1024]{1,0:T(8,128)(2,1)}) %all-gather.45.cloned.1.call-update) | async-done | bytes 4194320 | tf_op jit(solution)/shard_map/all_gather | solution.py:171
  3537.3 86.3 %reduce-scatter.45.cloned.1.call-done = bf16[256,1024]{1,0:T(8,128)(2,1)} async-done(((bf16[2048,1024]{1,0:T(8,128)(2,1)}), bf16[256,1024]{1,0:T(8,128)(2,1)}) %reduce-scatter.45.cloned.1.call-update) | async-done | bytes 524304 | tf_op jit(solution)/shard_map/reduce_scatter | solution.py:174
  3643.2 58.2 %all-gather.47.cloned.1.call-done = bf16[2048,1024]{1,0:T(8,128)(2,1)} async-done(((bf16[256,1024]{1,0:T(8,128)(2,1)}), bf16[2048,1024]{1,0:T(8,128)(2,1)}) %all-gather.47.cloned.1.call-update) | async-done | bytes 4194320 | tf_op jit(solution)/shard_map/all_gather | solution.py:180
  3709.1 91.6 %while.149 = (s32[]{:T(128)}, bf16[2,3,1024,2,64]{2,4,3,1,0:T(8,128)(2,1)}, f32[2,20,2,64]{1,3,2,0:T(8,128)S(1)}, f32[2,20,2,64]{1,3,2,0:T(8,128)S(1)}, bf16[2,3...) while((s32[]{:T(128)}, ...), condition=%wide.region_61.62_spmd, body=%wide.region_57.61_spmd.sunk | while | flops 1683273216 | bytes 68598952 | solution.py:208
  3820.6 86.4 %reduce-scatter.47.cloned.1.call-done = bf16[256,1024]{1,0:T(8,128)(2,1)} async-done(((bf16[2048,1024]{1,0:T(8,128)(2,1)}), bf16[256,1024]{1,0:T(8,128)(2,1)}) %reduce-scatter.47.cloned.1.call-update) | async-done | bytes 524304 | tf_op jit(solution)/shard_map/reduce_scatter | solution.py:212
  4008.2 132.6 %reduce-scatter.65.cloned.1.call-done = f32[256,1024]{1,0:T(8,128)} async-done(((f32[2048,1024]{1,0:T(8,128)}), f32[256,1024]{1,0:T(8,128)}) %reduce-scatter.65.cloned.1.call-update) | async-done | bytes 1048592 | tf_op jit(solution)/shard_map/reduce_scatter | solution.py:116
  4144.2 87.4 %reduce-scatter.53.cloned.1.call-done = bf16[256,1024]{1,0:T(8,128)(2,1)} async-done(((bf16[2048,1024]{1,0:T(8,128)(2,1)}), bf16[256,1024]{1,0:T(8,128)(2,1)}) %reduce-scatter.53.cloned.1.call-update) | async-done | bytes 524304 | tf_op jit(solution)/shard_map/reduce_scatter | solution.py:174
  4251.4 58.4 %all-gather.55.cloned.1.call-done = bf16[2048,1024]{1,0:T(8,128)(2,1)} async-done(((bf16[256,1024]{1,0:T(8,128)(2,1)}), bf16[2048,1024]{1,0:T(8,128)(2,1)}) %all-gather.55.cloned.1.call-update) | async-done | bytes 4194320 | tf_op jit(solution)/shard_map/all_gather | solution.py:180
  4317.4 91.7 %while.151 = (s32[]{:T(128)}, bf16[2,3,1024,2,64]{2,4,3,1,0:T(8,128)(2,1)}, f32[2,20,2,64]{1,3,2,0:T(8,128)S(1)}, f32[2,20,2,64]{1,3,2,0:T(8,128)S(1)}, bf16[2,3...) while((s32[]{:T(128)}, ...), condition=%wide.region_82.83_spmd, body=%wide.region_78.82_spmd.sunk | while | flops 1683273216 | bytes 68598952 | solution.py:208
  4429.0 86.3 %reduce-scatter.55.cloned.1.call-done = bf16[256,1024]{1,0:T(8,128)(2,1)} async-done(((bf16[2048,1024]{1,0:T(8,128)(2,1)}), bf16[256,1024]{1,0:T(8,128)(2,1)}) %reduce-scatter.55.cloned.1.call-update) | async-done | bytes 524304 | tf_op jit(solution)/shard_map/reduce_scatter | solution.py:212
  4524.1 74.1 %all-gather.61.cloned.1.call-done = bf16[2048,1024]{1,0:T(8,128)(2,1)} async-done(((bf16[256,1024]{1,0:T(8,128)(2,1)}), bf16[2048,1024]{1,0:T(8,128)(2,1)}) %all-gather.61.cloned.1.call-update) | async-done | bytes 4194320 | tf_op jit(solution)/shard_map/all_gather | solution.py:171
  4617.9 86.4 %reduce-scatter.61.cloned.1.call-done = bf16[256,1024]{1,0:T(8,128)(2,1)} async-done(((bf16[2048,1024]{1,0:T(8,128)(2,1)}), bf16[256,1024]{1,0:T(8,128)(2,1)}) %reduce-scatter.61.cloned.1.call-update) | async-done | bytes 524304 | tf_op jit(solution)/shard_map/reduce_scatter | solution.py:174
  4724.8 58.1 %all-gather.63.cloned.1.call-done = bf16[2048,1024]{1,0:T(8,128)(2,1)} async-done(((bf16[256,1024]{1,0:T(8,128)(2,1)}), bf16[2048,1024]{1,0:T(8,128)(2,1)}) %all-gather.63.cloned.1.call-update) | async-done | bytes 4194320 | tf_op jit(solution)/shard_map/all_gather | solution.py:180
  4790.5 91.7 %while.153 = (s32[]{:T(128)}, bf16[2,3,1024,2,64]{2,4,3,1,0:T(8,128)(2,1)}, f32[2,20,2,64]{1,3,2,0:T(8,128)S(1)}, f32[2,20,2,64]{1,3,2,0:T(8,128)S(1)}, bf16[2,3...) while((s32[]{:T(128)}, ...), condition=%wide.region_103.104_spmd, body=%wide.region_99.103_spmd.sunk | while | flops 1683273216 | bytes 68598952 | solution.py:208
  4922.4 66.2 %reduce-scatter.63.cloned.1.call-done = bf16[256,1024]{1,0:T(8,128)(2,1)} async-done(((bf16[2048,1024]{1,0:T(8,128)(2,1)}), bf16[256,1024]{1,0:T(8,128)(2,1)}) %reduce-scatter.63.cloned.1.call-update) | async-done | bytes 524304 | tf_op jit(solution)/shard_map/reduce_scatter | solution.py:212
  4992.5 148.9 %reduce-scatter.67.cloned.1.call-done = f32[256,1024]{1,0:T(8,128)} async-done(((f32[2048,1024]{1,0:T(8,128)}), f32[256,1024]{1,0:T(8,128)}) %reduce-scatter.67.cloned.1.call-update) | async-done | bytes 1048592 | tf_op jit(solution)/shard_map/reduce_scatter | solution.py:133
  5147.0 72.5 %all-gather.69.cloned.1.call-done = bf16[2048,1024]{1,0:T(8,128)(2,1)} async-done(((bf16[256,1024]{1,0:T(8,128)(2,1)}), bf16[2048,1024]{1,0:T(8,128)(2,1)}) %all-gather.69.cloned.1.call-update) | async-done | bytes 4194320 | tf_op jit(solution)/shard_map/all_gather | solution.py:171
  5239.6 86.5 %reduce-scatter.69.cloned.1.call-done = bf16[256,1024]{1,0:T(8,128)(2,1)} async-done(((bf16[2048,1024]{1,0:T(8,128)(2,1)}), bf16[256,1024]{1,0:T(8,128)(2,1)}) %reduce-scatter.69.cloned.1.call-update) | async-done | bytes 524304 | tf_op jit(solution)/shard_map/reduce_scatter | solution.py:174
  5345.9 58.2 %all-gather.71.cloned.1.call-done = bf16[2048,1024]{1,0:T(8,128)(2,1)} async-done(((bf16[256,1024]{1,0:T(8,128)(2,1)}), bf16[2048,1024]{1,0:T(8,128)(2,1)}) %all-gather.71.cloned.1.call-update) | async-done | bytes 4194320 | tf_op jit(solution)/shard_map/all_gather | solution.py:180
  5411.8 91.5 %while.155 = (s32[]{:T(128)}, bf16[2,3,1024,2,64]{2,4,3,1,0:T(8,128)(2,1)}, f32[2,20,2,64]{1,3,2,0:T(8,128)S(1)}, f32[2,20,2,64]{1,3,2,0:T(8,128)S(1)}, bf16[2,3...) while((s32[]{:T(128)}, ...), condition=%wide.region_124.125_spmd, body=%wide.region_120.124_spmd.sunk | while | flops 1683273216 | bytes 68598952 | solution.py:208
  (1111 shorter events, 1854.4 us)
Async XLA Ops:
  12.0 281.9 %reduce-scatter.25.cloned.1.call-start = ((), (), s32[]{:S(2)}) async-start(), calls=%async_computation.25 | async-start | bytes 9437184 | tf_op jit(solution)/shard_map/reduce_scatter | solution.py:116
  146.5 225.4 %all-gather.27.cloned.1.call-start = ((), (), s32[]{:S(2)}) async-start(), calls=%async_computation.26 | async-start | bytes 4718592 | tf_op jit(solution)/shard_map/all_gather | solution.py:128
  299.4 239.4 %reduce-scatter.27.cloned.1.call-start = ((), (), s32[]{:S(2)}) async-start(), calls=%async_computation.27 | async-start | bytes 9437184 | tf_op jit(solution)/shard_map/reduce_scatter | solution.py:133
  391.3 224.2 %all-gather.37.cloned.1.call-start = ((), (), s32[]{:S(2)}) async-start(), calls=%async_computation.36 | async-start | bytes 4718592 | tf_op jit(solution)/shard_map/all_gather | solution.py:171
  547.5 231.6 %reduce-scatter.37.cloned.1.call-start = ((), (), s32[]{:S(2)}) async-start(), calls=%async_computation.37 | async-start | bytes 4718592 | tf_op jit(solution)/shard_map/reduce_scatter | solution.py:174
  634.1 297.9 %reduce-scatter.29.cloned.1.call-start = ((), (), s32[]{:S(2)}) async-start(), calls=%async_computation.29 | async-start | bytes 9437184 | tf_op jit(solution)/shard_map/reduce_scatter | solution.py:116
  749.2 260.8 %all-gather.39.cloned.1.call-start = ((), (), s32[]{:S(2)}) async-start(), calls=%async_computation.38 | async-start | bytes 4718592 | tf_op jit(solution)/shard_map/all_gather | solution.py:180
  937.4 196.0 %all-gather.31.cloned.1.call-start = ((), (), s32[]{:S(2)}) async-start(), calls=%async_computation.30 | async-start | bytes 4718592 | tf_op jit(solution)/shard_map/all_gather | solution.py:128
  938.0 281.6 %reduce-scatter.39.cloned.1.call-start = ((), (), s32[]{:S(2)}) async-start(), calls=%async_computation.39 | async-start | bytes 4718592 | tf_op jit(solution)/shard_map/reduce_scatter | solution.py:212
  1133.4 239.0 %reduce-scatter.31.cloned.1.call-start = ((), (), s32[]{:S(2)}) async-start(), calls=%async_computation.31 | async-start | bytes 9437184 | tf_op jit(solution)/shard_map/reduce_scatter | solution.py:133
  1153.6 297.2 %all-gather.41.cloned.1.call-start = ((), (), s32[]{:S(2)}) async-start(), calls=%async_computation.40 | async-start | bytes 4718592 | tf_op jit(solution)/shard_map/all_gather | solution.py:171
  1221.9 152.5 %collective-permute-start.2 = (bf16[256,1024]{1,0:T(8,128)(2,1)}, bf16[256,1024]{1,0:T(8,128)(2,1)}, u32[]{:S(2)}, u32[]{:S(2)}) collective-permute-start(bf16[256,1024]{1,0:T(8,128)(2,1)} %add_convert_fusion.16), channel_id=1, source_target_pairs={{16,0},{17,1},{18,2},{19,3},{20,4},{21,5},{22,6},{23,7},{24,8},{25... | collective-permute-start | bytes 1572872 | tf_op jit(solution)/shard_map/ppermute | solution.py:19
  1378.2 146.2 %all-gather.33.cloned.1.call-start = ((), (), s32[]{:S(2)}) async-start(), calls=%async_computation.32 | async-start | bytes 4718592 | tf_op jit(solution)/shard_map/all_gather | solution.py:97
  1382.2 232.2 %reduce-scatter.41.cloned.1.call-start = ((), (), s32[]{:S(2)}) async-start(), calls=%async_computation.41 | async-start | bytes 4718592 | tf_op jit(solution)/shard_map/reduce_scatter | solution.py:174
  1470.5 296.6 %reduce-scatter.33.cloned.1.call-start = ((), (), s32[]{:S(2)}) async-start(), calls=%async_computation.33 | async-start | bytes 9437184 | tf_op jit(solution)/shard_map/reduce_scatter | solution.py:116
  1584.8 260.1 %all-gather.35.cloned.1.call-start = ((), (), s32[]{:S(2)}) async-start(), calls=%async_computation.34 | async-start | bytes 4718592 | tf_op jit(solution)/shard_map/all_gather | solution.py:128
  1772.4 239.3 %reduce-scatter.35.cloned.1.call-start = ((), (), s32[]{:S(2)}) async-start(), calls=%async_computation.35 | async-start | bytes 9437184 | tf_op jit(solution)/shard_map/reduce_scatter | solution.py:133
  1864.2 229.5 %all-gather.49.cloned.1.call-start = ((), (), s32[]{:S(2)}) async-start(), calls=%async_computation.48 | async-start | bytes 4718592 | tf_op jit(solution)/shard_map/all_gather | solution.py:97
  2019.9 277.6 %reduce-scatter.49.cloned.1.call-start = ((), (), s32[]{:S(2)}) async-start(), calls=%async_computation.49 | async-start | bytes 9437184 | tf_op jit(solution)/shard_map/reduce_scatter | solution.py:116
  2150.0 222.9 %all-gather.51.cloned.1.call-start = ((), (), s32[]{:S(2)}) async-start(), calls=%async_computation.50 | async-start | bytes 4718592 | tf_op jit(solution)/shard_map/all_gather | solution.py:128
  2300.3 239.4 %reduce-scatter.51.cloned.1.call-start = ((), (), s32[]{:S(2)}) async-start(), calls=%async_computation.51 | async-start | bytes 9437184 | tf_op jit(solution)/shard_map/reduce_scatter | solution.py:133
  2392.3 227.3 %all-gather.57.cloned.1.call-start = ((), (), s32[]{:S(2)}) async-start(), calls=%async_computation.56 | async-start | bytes 4718592 | tf_op jit(solution)/shard_map/all_gather | solution.py:97
  2546.8 276.5 %reduce-scatter.57.cloned.1.call-start = ((), (), s32[]{:S(2)}) async-start(), calls=%async_computation.57 | async-start | bytes 9437184 | tf_op jit(solution)/shard_map/reduce_scatter | solution.py:116
  2675.9 223.5 %all-gather.59.cloned.1.call-start = ((), (), s32[]{:S(2)}) async-start(), calls=%async_computation.58 | async-start | bytes 4718592 | tf_op jit(solution)/shard_map/all_gather | solution.py:128
  2826.8 239.3 %reduce-scatter.59.cloned.1.call-start = ((), (), s32[]{:S(2)}) async-start(), calls=%async_computation.59 | async-start | bytes 9437184 | tf_op jit(solution)/shard_map/reduce_scatter | solution.py:133
  2918.7 222.1 %all-gather.43.cloned.1.call-start = ((), (), s32[]{:S(2)}) async-start(), calls=%async_computation.42 | async-start | bytes 4718592 | tf_op jit(solution)/shard_map/all_gather | solution.py:180
  2919.3 295.5 %all-gather.65.cloned.1.call-start = ((), (), s32[]{:S(2)}) async-start(), calls=%async_computation.64 | async-start | bytes 4718592 | tf_op jit(solution)/shard_map/all_gather | solution.py:97
  3073.2 362.5 %reduce-scatter.43.cloned.1.call-start = ((), (), s32[]{:S(2)}) async-start(), calls=%async_computation.43 | async-start | bytes 4718592 | tf_op jit(solution)/shard_map/reduce_scatter | solution.py:212
  3349.3 168.3 %all-gather.45.cloned.1.call-start = ((), (), s32[]{:S(2)}) async-start(), calls=%async_computation.44 | async-start | bytes 4718592 | tf_op jit(solution)/shard_map/all_gather | solution.py:171
  3443.5 180.1 %reduce-scatter.45.cloned.1.call-start = ((), (), s32[]{:S(2)}) async-start(), calls=%async_computation.45 | async-start | bytes 4718592 | tf_op jit(solution)/shard_map/reduce_scatter | solution.py:174
  3537.2 164.2 %all-gather.47.cloned.1.call-start = ((), (), s32[]{:S(2)}) async-start(), calls=%async_computation.46 | async-start | bytes 4718592 | tf_op jit(solution)/shard_map/all_gather | solution.py:180
  3628.2 278.9 %reduce-scatter.47.cloned.1.call-start = ((), (), s32[]{:S(2)}) async-start(), calls=%async_computation.47 | async-start | bytes 4718592 | tf_op jit(solution)/shard_map/reduce_scatter | solution.py:212
  3820.6 169.2 %all-gather.53.cloned.1.call-start = ((), (), s32[]{:S(2)}) async-start(), calls=%async_computation.52 | async-start | bytes 4718592 | tf_op jit(solution)/shard_map/all_gather | solution.py:171
  3915.7 225.1 %reduce-scatter.65.cloned.1.call-start = ((), (), s32[]{:S(2)}) async-start(), calls=%async_computation.65 | async-start | bytes 9437184 | tf_op jit(solution)/shard_map/reduce_scatter | solution.py:116
  3962.2 269.4 %reduce-scatter.53.cloned.1.call-start = ((), (), s32[]{:S(2)}) async-start(), calls=%async_computation.53 | async-start | bytes 4718592 | tf_op jit(solution)/shard_map/reduce_scatter | solution.py:174
  4008.1 301.7 %all-gather.55.cloned.1.call-start = ((), (), s32[]{:S(2)}) async-start(), calls=%async_computation.54 | async-start | bytes 4718592 | tf_op jit(solution)/shard_map/all_gather | solution.py:180
  4236.5 278.8 %reduce-scatter.55.cloned.1.call-start = ((), (), s32[]{:S(2)}) async-start(), calls=%async_computation.55 | async-start | bytes 4718592 | tf_op jit(solution)/shard_map/reduce_scatter | solution.py:212
  4428.9 169.3 %all-gather.61.cloned.1.call-start = ((), (), s32[]{:S(2)}) async-start(), calls=%async_computation.60 | async-start | bytes 4718592 | tf_op jit(solution)/shard_map/all_gather | solution.py:171
  4524.1 180.3 %reduce-scatter.61.cloned.1.call-start = ((), (), s32[]{:S(2)}) async-start(), calls=%async_computation.61 | async-start | bytes 4718592 | tf_op jit(solution)/shard_map/reduce_scatter | solution.py:174
  4617.8 165.1 %all-gather.63.cloned.1.call-start = ((), (), s32[]{:S(2)}) async-start(), calls=%async_computation.62 | async-start | bytes 4718592 | tf_op jit(solution)/shard_map/all_gather | solution.py:180
  4709.6 192.3 %all-gather.67.cloned.1.call-start = ((), (), s32[]{:S(2)}) async-start(), calls=%async_computation.66 | async-start | bytes 4718592 | tf_op jit(solution)/shard_map/all_gather | solution.py:128
  4724.7 263.8 %reduce-scatter.63.cloned.1.call-start = ((), (), s32[]{:S(2)}) async-start(), calls=%async_computation.63 | async-start | bytes 4718592 | tf_op jit(solution)/shard_map/reduce_scatter | solution.py:212
  4901.9 239.6 %reduce-scatter.67.cloned.1.call-start = ((), (), s32[]{:S(2)}) async-start(), calls=%async_computation.67 | async-start | bytes 9437184 | tf_op jit(solution)/shard_map/reduce_scatter | solution.py:133
  4922.3 297.2 %all-gather.69.cloned.1.call-start = ((), (), s32[]{:S(2)}) async-start(), calls=%async_computation.68 | async-start | bytes 4718592 | tf_op jit(solution)/shard_map/all_gather | solution.py:171
  4991.3 152.2 %collective-permute-start.9 = (bf16[256,1024]{1,0:T(8,128)(2,1)}, bf16[256,1024]{1,0:T(8,128)(2,1)}, u32[]{:S(2)}, u32[]{:S(2)}) collective-permute-start(bf16[256,1024]{1,0:T(8,128)(2,1)} %get-tuple-element.926), channel_id=1, source_target_pairs={{16,0},{17,1},{18,2},{19,3},{20,4},{21,5},{22,6},{23,7},{24,8},{25... | collective-permute-start | bytes 1572872 | tf_op jit(solution)/shard_map/ppermute | solution.py:19
  5147.0 179.1 %reduce-scatter.69.cloned.1.call-start = ((), (), s32[]{:S(2)}) async-start(), calls=%async_computation.69 | async-start | bytes 4718592 | tf_op jit(solution)/shard_map/reduce_scatter | solution.py:174
  5239.6 164.6 %all-gather.71.cloned.1.call-start = ((), (), s32[]{:S(2)}) async-start(), calls=%async_computation.70 | async-start | bytes 4718592 | tf_op jit(solution)/shard_map/all_gather | solution.py:180
  5330.9 278.2 %reduce-scatter.71.cloned.1.call-start = ((), (), s32[]{:S(2)}) async-start(), calls=%async_computation.71 | async-start | bytes 4718592 | tf_op jit(solution)/shard_map/reduce_scatter | solution.py:212
  (248 other events, 25886.9 us)
Sparse Core Ops, SparseCore 0:
  12.1 76.0 all-gather.24
  146.6 147.2 reduce-scatter.24
  299.5 72.3 all-gather.26
  391.4 147.2 reduce-scatter.26
  543.1 72.3 all-gather.36
  617.5 71.6 all-gather.28
  692.8 86.1 reduce-scatter.36
  783.1 148.7 reduce-scatter.28
  937.5 72.3 all-gather.38
  1012.0 71.6 all-gather.30
  1133.5 86.0 reduce-scatter.38
  1223.5 148.7 reduce-scatter.30
  1378.3 72.3 all-gather.40
  1452.8 71.6 all-gather.32
  1527.9 86.3 reduce-scatter.40
  1618.3 148.8 reduce-scatter.32
  1772.5 72.3 all-gather.34
  1864.3 147.2 reduce-scatter.34
  2020.0 73.6 all-gather.48
  2150.1 147.2 reduce-scatter.48
  2300.5 72.3 all-gather.50
  2392.4 147.2 reduce-scatter.50
  2546.9 72.6 all-gather.56
  2676.0 147.2 reduce-scatter.56
  2826.9 72.3 all-gather.58
  2918.8 147.2 reduce-scatter.58
  3068.3 72.3 all-gather.42
  3143.1 71.6 all-gather.64
  3349.4 86.2 reduce-scatter.42
  3443.6 73.9 all-gather.44
  3537.4 86.1 reduce-scatter.44
  3628.3 73.1 all-gather.46
  3820.7 86.3 reduce-scatter.46
  3915.8 73.9 all-gather.52
  3993.4 147.2 reduce-scatter.64
  4144.7 86.9 reduce-scatter.52
  4236.6 73.1 all-gather.54
  4429.0 86.1 reduce-scatter.54
  4524.2 73.9 all-gather.60
  4618.0 86.3 reduce-scatter.60
  4709.8 73.1 all-gather.62
  4785.1 71.6 all-gather.66
  4902.0 86.5 reduce-scatter.62
  4992.6 148.7 reduce-scatter.66
  5147.1 72.3 all-gather.68
  5239.7 86.3 reduce-scatter.68
  5331.0 73.1 all-gather.70
  5522.7 86.3 reduce-scatter.70
where the time goes:
time: 5640 us; the launch traced here: 5630 us
  waiting for transfers between devices  4070 us (72%)
  matrix products  819 us (15%)
  local copies, waits for them, and re-layouts  407 us (7%)
  other arithmetic  280 us (5%)
    reduce_scatter x6, waiting for transfers between devices, layer_forward(): lax.psum_scatter(jnp.dot(activated, down_weight, preferred_element_type=j...  885 us
    reduce_scatter x6, waiting for transfers between devices, layer_forward(): lax.psum_scatter(jnp.dot(mixed, output_weight, preferred_element_type=jnp...  877 us
    reduce_scatter x6, waiting for transfers between devices, layer_backward(): lax.psum_scatter(against(d_projected, project_flat).astype(jnp.bfloat16),...  444 us
    reduce_scatter x6, waiting for transfers between devices, layer_backward(): lax.psum_scatter(against(d_pre, up_weight).astype(jnp.bfloat16), 'tensor'...  406 us
    all_gather x6, waiting for transfers between devices, layer_forward(): lax.all_gather(tokens_in, 'tensor', axis=0, tiled=True)  397 us
    all_gather x6, waiting for transfers between devices, layer_backward(): lax.all_gather(d_hidden, 'tensor', axis=0, tiled=True)  385 us
    all_gather x6, waiting for transfers between devices, layer_backward(): lax.all_gather(d_attended, 'tensor', axis=0, tiled=True)  372 us
    all_gather x6, waiting for transfers between devices, layer_forward(): lax.all_gather(normed_first.astype(jnp.bfloat16), 'tensor', axis=0, tiled...  290 us
  transfers between devices with their start and end apart: 58, of which 54 were waited for; matrix products, arithmetic and copies ran while one was open for 11% of the time, Pallas kernels for 0%

commit v1 on v0

v1 whole, which is shorter than its diff:
```python
import functools
import math

import jax
import jax.numpy as jnp
from jax import lax
from jax.experimental import pallas as pl
from jax.experimental.pallas import tpu as pltpu
from jax.sharding import PartitionSpec as P

HEAD = 64
PAIR = 2 * HEAD
EPSILON = 1e-05
MASKED = -1000000000.0
VMEM = 56 * 1024 * 1024
SECTIONS = 2

bf16 = jnp.bfloat16
f32 = jnp.float32


def dot_nn(left, right):
    return lax.dot_general(left, right, (((1,), (0,)), ((), ())), preferred_element_type=f32)


def dot_nt(left, right):
    return lax.dot_general(left, right, (((1,), (1,)), ((), ())), preferred_element_type=f32)


def dot_tn(left, right):
    return lax.dot_general(left, right, (((0,), (0,)), ((), ())), preferred_element_type=f32)


def unit(hidden):
    average = jnp.mean(hidden, axis=-1, keepdims=True)
    centered = hidden - average
    variance = jnp.mean(centered * centered, axis=-1, keepdims=True)
    inverse = lax.rsqrt(variance + EPSILON)
    return centered * inverse, inverse


def unit_back(grad, normed, inverse, gain):
    scaled = grad * gain
    return inverse * (
        scaled
        - jnp.mean(scaled, axis=-1, keepdims=True)
        - normed * jnp.mean(scaled * normed, axis=-1, keepdims=True)
    )


def call(kernel, grid, in_specs, out_specs, out_shape, scratch=(), flops=0, moved=0, exps=0):
    return pl.pallas_call(
        kernel,
        grid=grid,
        in_specs=in_specs,
        out_specs=out_specs,
        out_shape=out_shape,
        scratch_shapes=list(scratch),
        compiler_params=pltpu.CompilerParams(
            vmem_limit_bytes=VMEM, dimension_semantics=("arbitrary",) * len(grid)
        ),
        cost_estimate=pl.CostEstimate(flops=flops, bytes_accessed=moved, transcendentals=exps),
    )


def whole(shape):
    return pl.BlockSpec(shape, lambda i: (0,) * len(shape))


def struct(shape, dtype):
    return jax.ShapeDtypeStruct(shape, dtype)


def table_pair(table, width):
    array, first, rows = table
    return pl.BlockSpec((2, 1, rows, width), lambda i: (0, i, first // rows, 0))


def table_all(table, width):
    array, first, rows = table
    return pl.BlockSpec(
        (2, array.shape[1], rows, width), lambda i: (0, 0, first // rows, 0)
    )


def table_piece(table, width):
    array, first, rows = table
    pairs = array.shape[1]
    return pl.BlockSpec((1, 1, rows, width), lambda i: (i // pairs, i % pairs, first // rows, 0))


def pair_rows(ref):
    parts = []
    for part in range(3):
        for half in range(2):
            parts.append(ref[half, 0, part * HEAD : (part + 1) * HEAD, :])
    return jnp.concatenate(parts, axis=0)


def project_kernel(x_ref, w_ref, b_ref, q_ref, kv_ref):
    out = (dot_nt(x_ref[...], pair_rows(w_ref)) + b_ref[0]).astype(bf16)
    q_ref[0] = out[:, :PAIR] * bf16(1.0 / math.sqrt(HEAD))
    kv_ref[0, 0] = out[:, PAIR : 2 * PAIR]
    kv_ref[1, 0] = out[:, 2 * PAIR :]


def project(x, table, bias):
    count, width = x.shape
    pairs = table[0].shape[1]
    return call(
        project_kernel,
        (pairs,),
        [
            whole((count, width)),
            table_pair(table, width),
            pl.BlockSpec((1, 1, 3 * PAIR), lambda i: (i, 0, 0)),
        ],
        [
            pl.BlockSpec((1, count, PAIR), lambda i: (i, 0, 0)),
            pl.BlockSpec((2, 1, count, PAIR), lambda i: (0, i, 0, 0)),
        ],
        [struct((pairs, count, PAIR), bf16), struct((2, pairs, count, PAIR), bf16)],
        flops=2 * count * width * 3 * PAIR * pairs,
        moved=2 * (count * width * 4 + 3 * width * PAIR * pairs),
    )(x, table[0], bias)


def attend_kernel(
    prefix_count, q_ref, own_ref, other_ref, pk_ref, pv_ref, sq_ref, sk_ref,
    mixed_ref, raised_ref, inverse_ref, bias_ref,
):
    pad = pk_ref.shape[1]
    others = other_ref.shape[0]

    @pl.when(pl.program_id(0) == 0)
    def _():
        row = lax.broadcasted_iota(jnp.int32, (pad, bias_ref.shape[1]), 0)
        bias_ref[:pad] = jnp.where(row < prefix_count, 0.0, MASKED)
        keys = sk_ref[...]
        same = (keys == sq_ref[...]) & (keys >= 0)
        bias_ref[pad:] = jnp.where(same, 0.0, MASKED)

    keys = jnp.concatenate(
        [pk_ref[0], own_ref[0, 0]] + [other_ref[i, 0, 0] for i in range(others)], axis=0
    )
    values = jnp.concatenate(
        [pv_ref[0], own_ref[1, 0]] + [other_ref[i, 1, 0] for i in range(others)], axis=0
    )
    queries = q_ref[0]
    lane = lax.broadcasted_iota(jnp.int32, queries.shape, 1)
    parts = []
    inverses = []
    for head in range(2):
        chosen = (lane // HEAD) == head
        scores = dot_nt(keys, jnp.where(chosen, queries, bf16(0))) + bias_ref[...]
        raised = jnp.exp(scores - jnp.max(scores, axis=0, keepdims=True))
        inverse = 1.0 / jnp.sum(raised, axis=0, keepdims=True)
        low = raised.astype(bf16)
        raised_ref[0, head] = low
        out = dot_tn(values, low)[head * HEAD : (head + 1) * HEAD]
        parts.append(out * inverse)
        inverses.append(jnp.broadcast_to(inverse, out.shape))
    mixed_ref[0] = jnp.concatenate(parts, axis=0).T.astype(bf16)
    inverse_ref[0] = jnp.concatenate(inverses, axis=0).T


def attend(q, own, other, pk, pv, prefix_count, seg_q, seg_k):
    pairs, count, _ = q.shape
    others = other.shape[0]
    pad = pk.shape[1]
    total = pad + count * (others + 1)
    by_pair = pl.BlockSpec((1, count, PAIR), lambda i: (i, 0, 0))
    by_prefix = pl.BlockSpec((1, pad, PAIR), lambda i: (i, 0, 0))
    return call(
        functools.partial(attend_kernel, prefix_count),
        (pairs,),
        [
            by_pair,
            pl.BlockSpec((2, 1, count, PAIR), lambda i: (0, i, 0, 0)),
            pl.BlockSpec((others, 2, 1, count, PAIR), lambda i: (0, 0, i, 0, 0)),
            by_prefix,
            by_prefix,
            whole((1, count)),
            whole((total - pad, 1)),
        ],
        [
            by_pair,
            pl.BlockSpec((1, 2, total, count), lambda i: (i, 0, 0, 0)),
            by_pair,
        ],
        [
            struct((pairs, count, PAIR), bf16),
            struct((pairs, 2, total, count), bf16),
            struct((pairs, count, PAIR), f32),
        ],
        scratch=[pltpu.VMEM((total, count), f32)],
        flops=8 * total * count * PAIR * pairs,
        moved=4 * pairs * total * count,
        exps=2 * pairs * total * count,
    )(q, own, other, pk, pv, seg_q, seg_k)


def feed_kernel(
    x_ref, mixed_ref, out_w_ref, vec_ref, up_ref, down_ref, ub_ref,
    out_ref, z1_ref, r1_ref, z2_ref, r2_ref, slope_ref, normed_ref, low_ref, acc_ref,
):
    step = pl.program_id(0)
    pairs = mixed_ref.shape[0]

    @pl.when(step == 0)
    def _():
        mixed = jnp.concatenate([mixed_ref[i] for i in range(pairs)], axis=1)
        rows = []
        for i in range(pairs):
            rows += [out_w_ref[0, i], out_w_ref[1, i]]
        attended = dot_nn(mixed, jnp.concatenate(rows, axis=0))
        z, r = unit(x_ref[...].astype(f32) + attended + vec_ref[0:1])
        z1_ref[...] = z
        r1_ref[...] = r
        normed = z * vec_ref[2:3] + vec_ref[4:5]
        normed_ref[...] = normed
        low_ref[...] = normed.astype(bf16)
        acc_ref[...] = jnp.zeros(acc_ref.shape, f32)

    pre = dot_nt(low_ref[...], up_ref[0, 0]) + ub_ref[0]
    spread = 0.5 + 0.5 * lax.erf(pre * math.sqrt(0.5))
    slope = spread + pre * (jnp.exp(-0.5 * pre * pre) * (1.0 / math.sqrt(2.0 * math.pi)))
    slope_ref[0] = slope.astype(bf16)
    acc_ref[...] += dot_nn((pre * spread).astype(bf16), down_ref[0, 0])

    @pl.when(step == pl.num_programs(0) - 1)
    def _():
        z, r = unit(normed_ref[...] + acc_ref[...] + vec_ref[1:2])
        z2_ref[...] = z
        r2_ref[...] = r
        out_ref[...] = (z * vec_ref[3:4] + vec_ref[5:6]).astype(bf16)


def feed(x, mixed, out_table, vectors, up_table, down_table, up_bias):
    count, width = x.shape
    pairs = mixed.shape[0]
    pieces = up_bias.shape[0]
    hidden = up_bias.shape[2]
    square = whole((count, width))
    column = whole((count, 1))
    return call(
        feed_kernel,
        (pieces,),
        [
            square,
            whole(mixed.shape),
            table_all(out_table, width),
            whole(vectors.shape),
            table_piece(up_table, width),
            table_piece(down_table, width),
            pl.BlockSpec((1, 1, hidden), lambda i: (i, 0, 0)),
        ],
        [square, square, column, square, column,
         pl.BlockSpec((1, count, hidden), lambda i: (i, 0, 0))],
        [
            struct((count, width), bf16),
            struct((count, width), f32),
            struct((count, 1), f32),
            struct((count, width), f32),
            struct((count, 1), f32),
            struct((pieces, count, hidden), bf16),
        ],
        scratch=[
            pltpu.VMEM((count, width), f32),
            pltpu.VMEM((count, width), bf16),
            pltpu.VMEM((count, width), f32),
        ],
        flops=2 * count * width * (width + 2 * hidden * pieces),
        moved=2 * (4 * hidden * pieces * width + 10 * count * width),
        exps=2 * count * hidden * pieces,
    )(x, mixed, out_table[0], vectors, up_table[0], down_table[0], up_bias)


def feed_back_kernel(
    grad_ref, z1_ref, r1_ref, z2_ref, r2_ref, slope_ref, out_w_ref, vec_ref, up_ref, down_ref,
    first_ref, mixed_ref, second_ref, low_ref, acc_ref,
):
    step = pl.program_id(0)
    pairs = mixed_ref.shape[0]

    @pl.when(step == 0)
    def _():
        second = unit_back(grad_ref[...].astype(f32), z2_ref[...], r2_ref[...], vec_ref[3:4])
        acc_ref[...] = second
        low_ref[...] = second.astype(bf16)

    d_act = dot_nt(low_ref[...], down_ref[0, 0])
    d_pre = (d_act * slope_ref[0].astype(f32)).astype(bf16)
    acc_ref[...] += dot_nn(d_pre, up_ref[0, 0])

    @pl.when(step == pl.num_programs(0) - 1)
    def _():
        first = unit_back(acc_ref[...], z1_ref[...], r1_ref[...], vec_ref[2:3])
        first_ref[...] = first
        low = first.astype(bf16)
        for i in range(pairs):
            rows = jnp.concatenate([out_w_ref[0, i], out_w_ref[1, i]], axis=0)
            mixed_ref[i] = dot_nt(low, rows).astype(bf16)


def feed_back(grad, kept, slope, out_table, vectors, up_table, down_table):
    count, width = grad.shape
    pieces, _, hidden = slope.shape
    pairs = out_table[0].shape[1]
    square = whole((count, width))
    column = whole((count, 1))
    return call(
        feed_back_kernel,
        (pieces,),
        [
            square, square, column, square, column,
            pl.BlockSpec((1, count, hidden), lambda i: (i, 0, 0)),
            table_all(out_table, width),
            whole(vectors.shape),
            table_piece(up_table, width),
            table_piece(down_table, width),
        ],
        [square, whole((pairs, count, PAIR))],
        [struct((count, width), f32), struct((pairs, count, PAIR), bf16)],
        scratch=[
            pltpu.VMEM((count, width), f32),
            pltpu.VMEM((count, width), bf16),
            pltpu.VMEM((count, width), f32),
        ],
        flops=2 * count * width * (width + 2 * hidden * pieces),
        moved=2 * (4 * hidden * pieces * width + 10 * count * width),
    )(grad, *kept, slope, out_table[0], vectors, up_table[0], down_table[0])


def attend_back_kernel(
    grad_ref, mixed_ref, inverse_ref, raised_ref, q_ref, own_ref, other_ref, pk_ref, pv_ref,
    dq_ref, down_ref, dother_ref, dpk_ref, dpv_ref,
):
    pad = pk_ref.shape[1]
    others = other_ref.shape[0]
    count = q_ref.shape[1]
    keys = jnp.concatenate(
        [pk_ref[0], own_ref[0, 0]] + [other_ref[i, 0, 0] for i in range(others)], axis=0
    )
    values = jnp.concatenate(
        [pv_ref[0], own_ref[1, 0]] + [other_ref[i, 1, 0] for i in range(others)], axis=0
    )
    queries = q_ref[0]
    lane = lax.broadcasted_iota(jnp.int32, queries.shape, 1)
    scaled = grad_ref[0].astype(f32) * inverse_ref[0]
    products = (scaled * mixed_ref[0].astype(f32)).T
    scaled = scaled.astype(bf16)
    d_keys = jnp.zeros(keys.shape, f32)
    d_values = jnp.zeros(keys.shape, f32)
    parts = []
    for head in range(2):
        chosen = (lane // HEAD) == head
        span = slice(head * HEAD, (head + 1) * HEAD)
        delta = jnp.sum(products[span], axis=0, keepdims=True)
        here = jnp.where(chosen, scaled, bf16(0))
        raised = raised_ref[0, head]
        d_score = (raised.astype(f32) * (dot_nt(values, here) - delta)).astype(bf16)
        d_values += dot_nn(raised, here)
        d_keys += dot_nn(d_score, jnp.where(chosen, queries, bf16(0)))
        parts.append(dot_tn(keys, d_score)[span])
    d_query = jnp.concatenate(parts, axis=0).T * (1.0 / math.sqrt(HEAD))
    dq_ref[0] = d_query.astype(bf16)
    dpk_ref[0] = d_keys[:pad]
    dpv_ref[0] = d_values[:pad]
    down_ref[0, 0] = d_keys[pad : pad + count].astype(bf16)
    down_ref[1, 0] = d_values[pad : pad + count].astype(bf16)
    for i in range(others):
        span = slice(pad + (i + 1) * count, pad + (i + 2) * count)
        dother_ref[i, 0, 0] = d_keys[span].astype(bf16)
        dother_ref[i, 1, 0] = d_values[span].astype(bf16)


def attend_back(grad, mixed, inverse, raised, q, own, other, pk, pv):
    pairs, count, _ = q.shape
    others = other.shape[0]
    pad = pk.shape[1]
    total = pad + count * (others + 1)
    by_pair = pl.BlockSpec((1, count, PAIR), lambda i: (i, 0, 0))
    by_prefix = pl.BlockSpec((1, pad, PAIR), lambda i: (i, 0, 0))
    by_own = pl.BlockSpec((2, 1, count, PAIR), lambda i: (0, i, 0, 0))
    by_other = pl.BlockSpec((others, 2, 1, count, PAIR), lambda i: (0, 0, i, 0, 0))
    return call(
        attend_back_kernel,
        (pairs,),
        [
            by_pair, by_pair, by_pair,
            pl.BlockSpec((1, 2, total, count), lambda i: (i, 0, 0, 0)),
            by_pair, by_own, by_other, by_prefix, by_prefix,
        ],
        [by_pair, by_own, by_other, by_prefix, by_prefix],
        [
            struct(q.shape, bf16),
            struct(own.shape, bf16),
            struct(other.shape, bf16),
            struct(pk.shape, f32),
            struct(pk.shape, f32),
        ],
        flops=16 * total * count * PAIR * pairs,
        moved=4 * pairs * total * count,
    )(grad, mixed, inverse, raised, q, own, other, pk, pv)


def project_back_kernel(first_ref, dq_ref, own_ref, got_ref, w_ref, out_ref, acc_ref):
    step = pl.program_id(0)
    others = got_ref.shape[0]

    @pl.when(step == 0)
    def _():
        acc_ref[...] = first_ref[...]

    parts = [dq_ref[0]]
    for part in range(2):
        total = own_ref[part, 0].astype(f32)
        for i in range(others):
            total += got_ref[i, part, 0].astype(f32)
        parts.append(total.astype(bf16))
    acc_ref[...] += dot_nn(jnp.concatenate(parts, axis=1), pair_rows(w_ref))

    @pl.when(step == pl.num_programs(0) - 1)
    def _():
        out_ref[...] = acc_ref[...].astype(bf16)


def project_back(first, dq, own, got, table):
    count, width = first.shape
    pairs = dq.shape[0]
    others = got.shape[0]
    return call(
        project_back_kernel,
        (pairs,),
        [
            whole((count, width)),
            pl.BlockSpec((1, count, PAIR), lambda i: (i, 0, 0)),
            pl.BlockSpec((2, 1, count, PAIR), lambda i: (0, i, 0, 0)),
            pl.BlockSpec((others, 2, 1, count, PAIR), lambda i: (0, 0, i, 0, 0)),
            table_pair(table, width),
        ],
        whole((count, width)),
        struct((count, width), bf16),
        scratch=[pltpu.VMEM((count, width), f32)],
        flops=2 * count * width * 3 * PAIR * pairs,
        moved=2 * (count * width * 7 + 3 * width * PAIR * pairs),
    )(first, dq, own, got, table[0])


def per_device(
    boundary, segment_ids, project_weight, project_bias, output_weight, output_biases,
    norm_gains, norm_shifts, up_weight, up_bias, down_weight, prefix_keys, prefix_values,
):
    section = lax.axis_index("section")
    rank = lax.axis_index("tensor")
    ranks = lax.axis_size("tensor")
    is_first = section == 0
    micro, slots, rows, width = boundary.shape[1:]
    length = slots * ranks
    row_count = micro * rows
    chips = ranks // row_count
    blocks = SECTIONS * chips
    count = length // blocks
    place = rank % chips
    swap = [(0, 1), (1, 0)]
    heads_all = project_weight.shape[3] * ranks
    pairs = heads_all // PAIR
    shards = ranks // pairs
    prefix_count = prefix_keys.shape[1]
    pad = -(-prefix_count // 32) * 32
    low_width = project_weight.shape[3] // 2
    hidden = up_weight.shape[2] // 2

    project_rows = jnp.transpose(project_weight[0], (1, 2, 0)).reshape(3, 2, low_width, width)
    project_rows = jnp.transpose(project_rows, (1, 0, 2, 3)).reshape(2, 3 * low_width, width)
    out_rows = output_weight[0].reshape(2, low_width, width)
    up_rows = jnp.transpose(up_weight[0], (1, 0)).reshape(2, hidden, width)
    down_rows = down_weight[0].reshape(2, hidden, width)
    small = jnp.concatenate(
        [
            jnp.transpose(project_bias[0].reshape(3, 2, low_width), (1, 0, 2)).reshape(2, -1),
            up_bias[0].reshape(2, hidden),
            jnp.transpose(prefix_keys[0].reshape(-1, 2, low_width), (1, 0, 2)).reshape(2, -1),
            jnp.transpose(prefix_values[0].reshape(-1, 2, low_width), (1, 0, 2)).reshape(2, -1),
        ],
        axis=1,
    )
    small_size = small.shape[1]
    small_rows = -(-small_size // (16 * width)) * 16
    small = jnp.pad(small, ((0, 0), (0, small_rows * width - small_size)))
    packed = jnp.concatenate(
        [project_rows, out_rows, up_rows, down_rows, small.reshape(2, small_rows, width)], axis=1
    )
    keep = lax.dynamic_index_in_dim(packed, section, 0, keepdims=False)
    give = lax.dynamic_index_in_dim(packed, 1 - section, 0, keepdims=False)
    got = lax.ppermute(give, "section", swap)
    layer_rows = [jnp.where(is_first, keep, got), jnp.where(is_first, got, keep)]
    sizes = [3 * low_width, low_width, hidden, hidden, small_rows]
    ends = [sum(sizes[: i + 1]) for i in range(len(sizes))]
    p_end, o_end, u_end, d_end, s_end = ends
    early = jnp.concatenate(
        [
            layer_rows[0][:d_end],
            layer_rows[1][:o_end],
            layer_rows[0][d_end:],
            layer_rows[1][d_end:],
        ],
        axis=0,
    )
    late = layer_rows[1][o_end:d_end]
    gather = lambda array: lax.all_gather(array, ("section", "tensor"), axis=0).reshape(
        2, ranks, array.shape[0], width
    )
    early = gather(early)
    late = gather(late)

    def table(array, first, size, groups=1):
        if shards == 1:
            return (array, first, size)
        part = array[:, :, first : first + size].reshape(
            2, pairs, shards, groups, size // groups, width
        )
        part = jnp.transpose(part, (2, 1, 3, 0, 4, 5))
        return (part.reshape(2, pairs, 2 * size, width), 0, 2 * size)

    tables = []
    smalls = []
    for layer in range(2):
        base = layer * d_end
        source, shift = (early, 0) if layer == 0 else (late, -o_end)
        tables.append(
            (
                table(early, base, 3 * low_width, 3),
                table(early, base + p_end, low_width),
                table(source, shift + o_end, hidden),
                table(source, shift + u_end, hidden),
            )
        )
        start = d_end + o_end + layer * small_rows
        flat = early[:, :, start : start + small_rows].reshape(2, ranks, -1)
        cut = 0
        pieces = []
        for groups, size in ((3, low_width), (1, hidden), (prefix_count, low_width), (prefix_count, low_width)):
            part = flat[:, :, cut : cut + groups * size].reshape(2, pairs, shards, groups, size)
            cut += groups * size
            if shards == 1:
                part = part[:, :, 0]
            else:
                part = jnp.transpose(part, (2, 1, 3, 0, 4)).reshape(2, pairs, groups, 2 * size)
            pieces.append(part)
        p_bias = jnp.transpose(pieces[0], (1, 2, 0, 3)).reshape(pairs, 1, 3 * PAIR).astype(f32)
        u_bias = pieces[1].reshape(2 * pairs, 1, -1).astype(f32)
        prefix = [
            jnp.pad(
                jnp.transpose(part, (1, 2, 0, 3)).reshape(pairs, prefix_count, PAIR),
                ((0, 0), (0, pad - prefix_count), (0, 0)),
            )
            for part in pieces[2:]
        ]
        smalls.append((p_bias, u_bias, prefix[0], prefix[1]))

    own_vectors = jnp.concatenate(
        [output_biases[0], norm_gains[0], norm_shifts[0], norm_shifts[0]], axis=0
    )
    got_vectors = lax.ppermute(own_vectors, "section", swap)
    vectors = [
        jnp.where(is_first, own_vectors, got_vectors).astype(f32),
        jnp.where(is_first, got_vectors, own_vectors).astype(f32),
    ]

    by_row = jnp.transpose(boundary[0], (0, 2, 1, 3)).reshape(row_count, slots, width)
    if chips > 1:
        by_row = jnp.repeat(by_row, chips, axis=0)
    row = lax.all_to_all(by_row, "tensor", 0, 0, tiled=True).reshape(length, width)
    block = section * chips + place
    other_block = (1 - section) * chips + place
    mine = lax.dynamic_slice_in_dim(row, block * count, count, 0)
    theirs = lax.dynamic_slice_in_dim(row, other_block * count, count, 0)
    got = lax.ppermute(theirs, "section", swap)
    tokens = jnp.where(is_first, mine, got)
    cotangent = jnp.where(is_first, got, mine)

    def flips():
        routes = []
        for distance in range(1, blocks):
            route = []
            for s in range(SECTIONS):
                for t in range(ranks):
                    index = (s * chips + t % chips) ^ distance
                    route.append(
                        (s * ranks + t, (index // chips) * ranks + t // chips * chips + index % chips)
                    )
            routes.append(route)
        return routes

    routes = flips()

    def exchange(parts):
        return jnp.stack(
            [
                lax.ppermute(part, ("section", "tensor"), route) if chips > 1
                else lax.ppermute(part, "section", swap)
                for part, route in zip(parts, routes)
            ]
        )

    segments = lax.dynamic_index_in_dim(
        segment_ids.reshape(row_count, length), rank // chips, 0, keepdims=False
    )
    seg_q = lax.dynamic_slice_in_dim(segments, block * count, count, 0)
    seg_k = jnp.concatenate(
        [
            lax.dynamic_slice_in_dim(segments, (block ^ distance) * count, count, 0)
            for distance in range(blocks)
        ]
    )[:, None]
    seg_q = seg_q[None, :]

    saved = []
    x = tokens
    for layer in range(2):
        p_table, o_table, u_table, d_table = tables[layer]
        p_bias, u_bias, pk, pv = smalls[layer]
        q, own = project(x, p_table, p_bias)
        other = exchange([own] * (blocks - 1))
        mixed, raised, inverse = attend(q, own, other, pk, pv, prefix_count, seg_q, seg_k)
        out, z1, r1, z2, r2, slope = feed(x, mixed, o_table, vectors[layer], u_table, d_table, u_bias)
        saved.append((q, own, other, mixed, raised, inverse, (z1, r1, z2, r2), slope))
        x = out

    grad = cotangent
    prefix_grads = []
    for layer in (1, 0):
        p_table, o_table, u_table, d_table = tables[layer]
        p_bias, u_bias, pk, pv = smalls[layer]
        q, own, other, mixed, raised, inverse, kept, slope = saved[layer]
        first, d_mixed = feed_back(grad, kept, slope, o_table, vectors[layer], u_table, d_table)
        dq, down, dother, dpk, dpv = attend_back(
            d_mixed, mixed, inverse, raised, q, own, other, pk, pv
        )
        got = exchange([dother[i] for i in range(blocks - 1)])
        grad = project_back(first, dq, down, got, p_table)
        flat = jnp.stack([dpk[:, :prefix_count], dpv[:, :prefix_count]])
        prefix_grads.append(lax.psum(flat, ("section", "dp", "tensor")))

    give = jnp.where(is_first, out, grad)
    keep = jnp.where(is_first, grad, out)
    got = lax.ppermute(give, "section", swap)
    lower = jnp.where(is_first, keep, got)
    upper = jnp.where(is_first, got, keep)
    if chips == 1:
        row = jnp.concatenate([lower, upper], axis=0)
    else:
        row = jnp.zeros((length, width), bf16)
        row = lax.dynamic_update_slice_in_dim(row, lower, place * count, 0)
        row = lax.dynamic_update_slice_in_dim(row, upper, (chips + place) * count, 0)
    back = lax.all_to_all(row.reshape(ranks, slots, width), "tensor", 0, 0, tiled=True)
    if chips > 1:
        back = jnp.sum(back.reshape(row_count, chips, slots, width), axis=1)
    result = jnp.transpose(back.reshape(micro, rows, slots, width), (0, 2, 1, 3))[None]

    both = jnp.where(is_first, prefix_grads[1], prefix_grads[0])
    both = jnp.transpose(both, (0, 2, 1, 3)).reshape(2, prefix_count, heads_all)
    share = heads_all // ranks
    both = lax.dynamic_slice_in_dim(both, rank * share, share, 2)
    return (result, both[0][None], both[1][None])


def solution(mesh):
    in_specs = (
        P("section", None, "tensor", "dp", None),
        P(None, "dp", None),
        P("section", None, None, "tensor"),
        P("section", None, "tensor"),
        P("section", "tensor", None),
        P("section", None, None),
        P("section", None, None),
        P("section", None, None),
        P("section", None, "tensor"),
        P("section", "tensor"),
        P("section", "tensor", None),
        P("section", None, "tensor"),
        P("section", None, "tensor"),
    )
    out_specs = (
        P("section", None, "tensor", "dp", None),
        P("section", None, "tensor"),
        P("section", None, "tensor"),
    )
    return jax.shard_map(
        per_device, mesh=mesh, in_specs=in_specs, out_specs=out_specs, check_vma=False
    )
```

time: 5640 us -> 719 us (0.13)
  waiting for transfers between devices: 4070 us -> 389 us
  matrix products: 819 us -> 0 us
  local copies, waits for them, and re-layouts: 407 us -> 31.7 us
  other arithmetic: 280 us -> 10.6 us
  Pallas kernels: 0 us -> 254 us
    reduce_scatter x24 -> x0, waiting for transfers between devices: 2610 us -> none  [the longest x6 885 us: layer_forward(): lax.psum_scatter(jnp.dot(activated, down_weight, preferred_element_type=j...]
    all_gather x24 -> x2, waiting for transfers between devices: 1440 us -> 148 us  [per_device(): lax.all_gather(array, ('section', 'tensor'), axis=0)]
    dot_general x102 -> x0, matrix products: 673 us -> none  [the longest x18 168 us: against(): lax.dot_general(left, right, (((1,), (1,)), ((), ())), preferred_element_...]
    pallas_call x0 -> x12, Pallas kernels: none -> 254 us  [the longest x2 62.9 us: feed(): call(feed_kernel, (pieces,), [square, whole(mixed.shape), table_all(out_t...]
    convert_element_type x36 -> x5, other arithmetic: 161 us -> 0.8 us  [the longest x1 0.65 us: per_device(): jnp.where(is_first, got_vectors, own_vectors).astype(f32)]
    psum x0 -> x1, waiting for transfers between devices: none -> 149 us  [per_device(): prefix_grads.append(lax.psum(flat, ('section', 'dp', 'tensor')))]
    sub x24 -> x0, matrix products: 146 us -> none  [row_softmax(): raised = jnp.exp(scores - largest)]
    reshape x29 -> x16, local copies, waits for them, and re-layouts: 111 us -> 3.94 us  [the longest x1 2.3 us: per_device(): up_rows = jnp.transpose(up_weight[0], (1, 0)).reshape(2, hidden, width)]
  transfers between devices with their start and end apart: 58 -> 13, of which waited for: 54 -> 11; matrix products, arithmetic and copies ran while one was open for 11% -> 3% of each run, Pallas kernels for 0% -> 13%
where the time goes in v1:
time: 719 us; the launch traced here: 715 us
  waiting for transfers between devices  389 us (54%)
  Pallas kernels  254 us (35%)
  local copies, waits for them, and re-layouts  31.7 us (4%)
  starting transfers between devices  14.8 us (2%)
  between operations  14.6 us (2%)
  other arithmetic  10.6 us (1%)
    psum x1, waiting for transfers between devices, per_device(): prefix_grads.append(lax.psum(flat, ('section', 'dp', 'tensor')))  149 us
    all_gather x2, waiting for transfers between devices, per_device(): lax.all_gather(array, ('section', 'tensor'), axis=0)  148 us
    all_to_all x1, waiting for transfers between devices, per_device(): lax.all_to_all(by_row, 'tensor', 0, 0, tiled=True).reshape(length, width)  71.1 us
    pallas_call x2, Pallas kernels, feed(): call(feed_kernel, (pieces,), [square, whole(mixed.shape), table_all(out_t...  62.9 us
    pallas_call x2, Pallas kernels, feed_back(): call(feed_back_kernel, (pieces,), [square, square, column, square, column...  61.2 us
    pallas_call x2, Pallas kernels, attend_back(): call(attend_back_kernel, (pairs,), [by_pair, by_pair, by_pair, pl.BlockSp...  44 us
    pallas_call x2, Pallas kernels, attend(): call(functools.partial(attend_kernel, prefix_count), (pairs,), [by_pair,...  43.5 us
    pallas_call x2, Pallas kernels, project_back(): call(project_back_kernel, (pairs,), [whole((count, width)), pl.BlockSpec(...  22.6 us
  transfers between devices with their start and end apart: 13, of which 11 were waited for; matrix products, arithmetic and copies ran while one was open for 3% of the time, Pallas kernels for 13%

profile of v1, /device:TPU:0, one launch (start us, length us, event | category | flops | bytes accessed | tf_op | source)
XLA Modules:
  0.0 715.0 jit_solution(17494541582921320040)
XLA Ops:
  7.2 1.4 copy.45
  8.8 2.3 copy.65
  11.8 1.4 constant_dynamic-update-slice_fusion.1
  13.5 1.4 dynamic-slice_bitcast_fusion
  15.7 3.1 collective-permute-done.1
  18.8 2.1 bitcast_select_fusion.1
  21.1 1.6 pad_maximum_fusion
  22.8 1.0 slice.97
  23.8 3.5 copy.44
  27.4 7.4 %all-to-all-start = ((bf16[8,128,1024]{2,1,0:T(8,128)(2,1)}), bf16[8,128,1024]{2,1,0:T(8,128)(2,1)S(1)}, u32[]{:S(2)}, u32[]{:S(2)}) async-start(bf16[8,128,1024]{2,1,0:T(8,128)(2,1)} %bitcast.102), calls=%async_computation | async-start | bytes 4194304 | tf_op jit(solution)/shard_map/all_to_all | solution.py:575
  34.8 71.1 %all-to-all-done = bf16[8,128,1024]{2,1,0:T(8,128)(2,1)S(1)} async-done(((bf16[8,128,1024]{2,1,0:T(8,128)(2,1)}), bf16[8,128,1024]{2,1,0:T(8,128)(2,1)S(1)}, u32[]{:S(2)}, u32[]{:S(2)}) %all-to-all-start) | async-done | bytes 2097184 | tf_op jit(solution)/shard_map/all_to_all | solution.py:575
  105.8 1.0 constant_dynamic-slice_fusion.2
  106.9 2.9 collective-permute-done
  109.7 1.9 broadcast_select_fusion.5
  111.7 120.5 %all-gather.5.cloned.1.call-done = bf16[16896,1024]{1,0:T(8,128)(2,1)} async-done(((bf16[1056,1024]{1,0:T(8,128)(2,1)}), bf16[16896,1024]{1,0:T(8,128)(2,1)}) %all-gather.5.cloned.1.call-update) | async-done | bytes 34603024 | tf_op jit(solution)/shard_map/all_gather | solution.py:512
  232.2 1.3 fusion
  233.9 0.7 reshape.155.b_ref
  234.6 10.0 %shard_map.148 = (bf16[8,512,128]{2,1,0:T(8,128)(2,1)}, bf16[2,8,512,128]{3,2,1,0:T(8,128)(2,1)}) custom-call(bf16[512,1024]{1,0:T(8,128)(2,1)} %get-tuple-element.90.x_ref, bf16[2,8,1056,1024]{3,2,1,0:T(8,128)(2,1)} %bitcast.82, f32[8,1,384]{2,1,0:T(1,128)} %reshape.155.b_ref), custom_call_target="tpu_custom_call" | custom-call | flops 3221225472 | bytes 10485760 | tf_op jit(solution)/shard_map/pallas_call | solution.py:110
  245.3 1.1 copy.56.sk_ref
  246.4 2.4 collective-permute-done.3
  252.5 0.7 reshape.157.b_ref
  253.2 21.6 %shard_map.149 = (bf16[8,512,128]{2,1,0:T(8,128)(2,1)}, bf16[8,2,1056,512]{3,2,1,0:T(8,128)(2,1)}, f32[8,512,128]{2,1,0:T(8,128)}) custom-call(bf16[8,512,128]{2,1,0:T(8,128)(2,1)} %get-tuple-element.39.q_ref, bf16[2,8,512,128]{3,2,1,0:T(8,128)(2,1)} %get-tuple-element.40.own_ref, bf16[1,2,8,512,128]{4,3,2,1,0:T(8,128)(2,1)} %bitcast.21.other_ref, ...), custom_call_target="tpu_custom_call" | custom-call | flops 4429185024 | bytes 17301504 | tf_op jit(solution)/shard_map/pallas_call | solution.py:174
  274.8 31.5 %shard_map.150 = (bf16[512,1024]{1,0:T(8,128)(2,1)}, f32[512,1024]{1,0:T(8,128)}, f32[512,1]{1,0:T(8,128)}, f32[512,1024]{1,0:T(8,128)}, f32[512,1]{1,0:T(8,128)}, /*index=5*/bf16[16,512,256]{2,1,0:T(8,128)(2,1)}) custom-call(bf16[512,1024]{1,0:T(8,128)(2,1)} %get-tuple-element.90.x_ref, bf16[8,512,128]{2,1,0:T(8,128)(2,1)} %get-tuple-element.41.mixed_ref, ...), custom_call_target="tpu_custom_call" | custom-call | flops 9663676416 | bytes 44040192 | tf_op jit(solution)/shard_map/pallas_call | solution.py:246
  306.3 10.1 %shard_map.151 = (bf16[8,512,128]{2,1,0:T(8,128)(2,1)}, bf16[2,8,512,128]{3,2,1,0:T(8,128)(2,1)}) custom-call(bf16[512,1024]{1,0:T(8,128)(2,1)} %get-tuple-element.42.x_ref, bf16[2,8,1056,1024]{3,2,1,0:T(8,128)(2,1)} %bitcast.86, f32[8,1,384]{2,1,0:T(1,128)} %reshape.157.b_ref), custom_call_target="tpu_custom_call" | custom-call | flops 3221225472 | bytes 10485760 | tf_op jit(solution)/shard_map/pallas_call | solution.py:110
  319.4 1.4 collective-permute-done.4
  320.8 1.3 copy-done.20
  322.1 21.9 %shard_map.152 = (bf16[8,512,128]{2,1,0:T(8,128)(2,1)}, bf16[8,2,1056,512]{3,2,1,0:T(8,128)(2,1)}, f32[8,512,128]{2,1,0:T(8,128)}) custom-call(bf16[8,512,128]{2,1,0:T(8,128)(2,1)} %get-tuple-element.43.q_ref, bf16[2,8,512,128]{3,2,1,0:T(8,128)(2,1)} %get-tuple-element.44.own_ref, bf16[1,2,8,512,128]{4,3,2,1,0:T(8,128)(2,1)} %bitcast.130, ...), custom_call_target="tpu_custom_call" | custom-call | flops 4429185024 | bytes 17301504 | tf_op jit(solution)/shard_map/pallas_call | solution.py:174
  344.0 27.6 %all-gather.7.cloned.1.call-done = bf16[8192,1024]{1,0:T(8,128)(2,1)} async-done(((bf16[512,1024]{1,0:T(8,128)(2,1)}), bf16[8192,1024]{1,0:T(8,128)(2,1)}) %all-gather.7.cloned.1.call-update) | async-done | bytes 16777232 | tf_op jit(solution)/shard_map/all_gather | solution.py:512
  371.6 31.3 %shard_map.153 = (bf16[512,1024]{1,0:T(8,128)(2,1)}, f32[512,1024]{1,0:T(8,128)}, f32[512,1]{1,0:T(8,128)}, f32[512,1024]{1,0:T(8,128)}, f32[512,1]{1,0:T(8,128)}, /*index=5*/bf16[16,512,256]{2,1,0:T(8,128)(2,1)}) custom-call(bf16[512,1024]{1,0:T(8,128)(2,1)} %get-tuple-element.42.x_ref, bf16[8,512,128]{2,1,0:T(8,128)(2,1)} %get-tuple-element.45.mixed_ref, ...), custom_call_target="tpu_custom_call" | custom-call | flops 9663676416 | bytes 44040192 | tf_op jit(solution)/shard_map/pallas_call | solution.py:246
  403.0 30.6 %shard_map.154 = (f32[512,1024]{1,0:T(8,128)}, bf16[8,512,128]{2,1,0:T(8,128)(2,1)}) custom-call(bf16[512,1024]{1,0:T(8,128)(2,1)} %get-tuple-element.89.grad_ref, f32[512,1024]{1,0:T(8,128)} %get-tuple-element.46.z1_ref, f32[512,1]{1,0:T(8,128)} %get-tuple-element.47.r1_ref, f32[512,1024]{1,0:T(8,128)} %get-tuple-element.48.z2_ref, ...), custom_call_target="tpu_custom_call" | custom-call | flops 9663676416 | bytes 44040192 | tf_op jit(solution)/shard_map/pallas_call | solution.py:312
  433.5 22.1 %shard_map.155 = (bf16[8,512,128]{2,1,0:T(8,128)(2,1)}, bf16[2,8,512,128]{3,2,1,0:T(8,128)(2,1)}, bf16[1,2,8,512,128]{4,3,2,1,0:T(8,128)(2,1)}, f32[8,32,128]{2,1,0:T(8,128)}, f32[8,32,128]{2,1,0:T(8,128)}) custom-call(bf16[8,512,128]{2,1,0:T(8,128)(2,1)} %get-tuple-element.52.grad_ref, bf16[8,512,128]{2,1,0:T(8,128)(2,1)} %get-tuple-element.45.mixed_ref, ...), custom_call_target="tpu_custom_call" | custom-call | flops 8858370048 | bytes 17301504 | tf_op jit(solution)/shard_map/pallas_call | solution.py:387
  456.0 4.1 collective-permute-done.5
  460.1 1.3 copy-done.4
  461.4 11.3 %shard_map.156.grad_ref = bf16[512,1024]{1,0:T(8,128)(2,1)} custom-call(f32[512,1024]{1,0:T(8,128)} %get-tuple-element.51.first_ref, bf16[8,512,128]{2,1,0:T(8,128)(2,1)} %get-tuple-element.55.dq_ref, bf16[2,8,512,128]{3,2,1,0:T(8,128)(2,1)} %get-tuple-element.56.own_ref, bf16[1,2,8,512,128]{4,3,2,1,0:T(8,128)(2,1)} %bitcast.107, ...), custom_call_target="tpu_custom_call" | custom-call | flops 3221225472 | bytes 13631488 | tf_op jit(solution)/shard_map/pallas_call | solution.py:433
  472.6 30.6 %shard_map.157 = (f32[512,1024]{1,0:T(8,128)}, bf16[8,512,128]{2,1,0:T(8,128)(2,1)}) custom-call(bf16[512,1024]{1,0:T(8,128)(2,1)} %shard_map.156.grad_ref, f32[512,1024]{1,0:T(8,128)} %get-tuple-element.58.z1_ref, f32[512,1]{1,0:T(8,128)} %get-tuple-element.59.r1_ref, f32[512,1024]{1,0:T(8,128)} %get-tuple-element.60.z2_ref, ...), custom_call_target="tpu_custom_call" | custom-call | flops 9663676416 | bytes 44040192 | tf_op jit(solution)/shard_map/pallas_call | solution.py:312
  503.3 21.9 %shard_map.158 = (bf16[8,512,128]{2,1,0:T(8,128)(2,1)}, bf16[2,8,512,128]{3,2,1,0:T(8,128)(2,1)}, bf16[1,2,8,512,128]{4,3,2,1,0:T(8,128)(2,1)}, f32[8,32,128]{2,1,0:T(8,128)}, f32[8,32,128]{2,1,0:T(8,128)}) custom-call(bf16[8,512,128]{2,1,0:T(8,128)(2,1)} %get-tuple-element.64.grad_ref, bf16[8,512,128]{2,1,0:T(8,128)(2,1)} %get-tuple-element.41.mixed_ref, ...), custom_call_target="tpu_custom_call" | custom-call | flops 8858370048 | bytes 17301504 | tf_op jit(solution)/shard_map/pallas_call | solution.py:387
  525.4 4.1 collective-permute-done.6
  529.6 1.3 copy-done.3
  530.9 11.4 %shard_map.159 = bf16[512,1024]{1,0:T(8,128)(2,1)} custom-call(f32[512,1024]{1,0:T(8,128)} %get-tuple-element.63.first_ref, bf16[8,512,128]{2,1,0:T(8,128)(2,1)} %get-tuple-element.67.dq_ref, bf16[2,8,512,128]{3,2,1,0:T(8,128)(2,1)} %get-tuple-element.68.own_ref, bf16[1,2,8,512,128]{4,3,2,1,0:T(8,128)(2,1)} %bitcast.106, bf16[2,8,1056,1024]{3,2,1,0:T(8,128)(2,1)} %bitcast.93), custom_call_target="tpu_custom_call" | custom-call | flops 3221225472 | bytes 13631488 | tf_op jit(solution)/shard_map/pallas_call | solution.py:433
  542.4 1.6 collective-permute-start.7
  544.0 2.3 collective-permute-done.7
  546.5 1.5 pad_maximum_fusion.1
  548.0 3.7 all-to-all-start.1
  551.9 0.7 pad_maximum_fusion.3
  553.3 149.5 %all-reduce.8.cloned.1.call-done = (f32[2,8,20,128]{3,2,1,0:T(8,128)}, f32[2,8,20,128]{3,2,1,0:T(8,128)}) async-done(((f32[2,8,20,128]{3,2,1,0:T(8,128)}, f32[2,8,20,128]{3,2,1,0:T(8,128)}), (f32[2,8,20,128]{3,2,1,0:T(8,128)}, f32[2,8,20,128]{3,2,1,0:T(8,128)})) %all-reduce.8.cloned.1.call-update) | async-done | bytes 327696 | tf_op jit(solution)/shard_map/psum | solution.py:645
  702.8 1.0 select_bitcast_fusion
  703.8 0.7 constant_dynamic-slice_fusion.1
  704.6 3.5 copy.64
  (118 shorter events, 11.7 us)
Async XLA Ops:
  7.2 225.0 %all-gather.5.cloned.1.call-start = ((), (), s32[]{:S(2)}) async-start(), calls=%async_computation.2 | async-start | bytes 36765696 | tf_op jit(solution)/shard_map/all_gather | solution.py:512
  8.7 2.4 copy-start.19
  8.7 2.6 copy-start.18
  8.7 2.6 copy-start.16
  8.7 2.8 copy-start.17
  8.7 3.0 copy-start.6
  11.7 1.5 copy-start.5
  13.5 2.2 copy-start.1
  14.9 3.9 collective-permute-start.1
  22.7 348.9 %all-gather.7.cloned.1.call-start = ((), (), s32[]{:S(2)}) async-start(), calls=%async_computation.3 | async-start | bytes 17825792 | tf_op jit(solution)/shard_map/all_gather | solution.py:512
  27.4 78.5 %all-to-all-start = ((bf16[8,128,1024]{2,1,0:T(8,128)(2,1)}), bf16[8,128,1024]{2,1,0:T(8,128)(2,1)S(1)}, u32[]{:S(2)}, u32[]{:S(2)}) async-start(bf16[8,128,1024]{2,1,0:T(8,128)(2,1)} %bitcast.102), calls=%async_computation | async-start | bytes 4194304 | tf_op jit(solution)/shard_map/all_to_all | solution.py:575
  106.9 2.9 collective-permute-start
  234.5 10.3 %copy-start.12 = (bf16[1,2,1024]{2,1,0:T(2,128)(2,1)S(1)}, bf16[1,2,1024]{2,1,0:T(2,128)(2,1)}, u32[]{:S(2)}) copy-start(bf16[1,2,1024]{2,1,0:T(2,128)(2,1)} %param.20) | copy-start | bytes 12292
  234.6 10.3 %copy-start.13 = (bf16[1,2,1024]{2,1,0:T(2,128)(2,1)S(1)}, bf16[1,2,1024]{2,1,0:T(2,128)(2,1)}, u32[]{:S(2)}) copy-start(bf16[1,2,1024]{2,1,0:T(2,128)(2,1)} %param.19) | copy-start | bytes 12292
  234.6 10.3 %copy-start.14 = (bf16[1,2,1024]{2,1,0:T(2,128)(2,1)S(1)}, bf16[1,2,1024]{2,1,0:T(2,128)(2,1)}, u32[]{:S(2)}) copy-start(bf16[1,2,1024]{2,1,0:T(2,128)(2,1)} %param.18) | copy-start | bytes 12292
  234.6 10.7 %copy-start.11 = (s32[4,2,1024]{2,1,0:T(2,128)S(1)}, s32[4,2,1024]{2,1,0:T(2,128)}, u32[]{:S(2)}) copy-start(s32[4,2,1024]{2,1,0:T(2,128)} %param.14) | copy-start | bytes 98308
  244.6 8.6 %collective-permute-start.2 = (bf16[2,8,512,128]{3,2,1,0:T(8,128)(2,1)}, bf16[2,8,512,128]{3,2,1,0:T(8,128)(2,1)}, u32[]{:S(2)}, u32[]{:S(2)}) collective-permute-start(bf16[2,8,512,128]{3,2,1,0:T(8,128)(2,1)} %get-tuple-element.40.own_ref), channel_id=1, source_target_pairs={{0,16},{16,0},{1,17},{17,1},{2,18},{18,2},{3,19},{19,3},{4,20},{20... | collective-permute-start | bytes 6291464 | tf_op jit(solution)/shard_map/ppermute | solution.py:603
  244.9 3.9 collective-permute-start.3
  245.3 7.9 %copy-start.15 = (s32[1,512]{1,0:T(1,128)}, s32[1,512]{1,0:T(1,128)S(1)}, u32[]{:S(2)}) copy-start(s32[1,512]{1,0:T(1,128)S(1)} %get-tuple-element.98.sq_ref) | copy-start | bytes 6148
  316.4 4.4 collective-permute-start.4
  320.8 1.3 copy-start.20
  455.6 4.4 collective-permute-start.5
  460.1 1.3 copy-start.4
  525.1 4.4 collective-permute-start.6
  529.6 1.3 copy-start.3
  530.9 11.4 %copy-start.2 = (bf16[512,1024]{1,0:T(8,128)(2,1)S(1)}, bf16[512,1024]{1,0:T(8,128)(2,1)}, u32[]{:S(2)}) copy-start(bf16[512,1024]{1,0:T(8,128)(2,1)} %get-tuple-element.70) | copy-start | bytes 3145732
  542.3 4.0 copy-start
  542.4 3.9 collective-permute-start.7
  548.0 3.8 copy-start.7
  548.0 3.8 copy-start.8
  548.0 4.5 copy-start.9
  548.0 4.5 copy-start.10
  548.0 156.5 %all-to-all-start.1 = ((bf16[8,128,1024]{2,1,0:T(8,128)(2,1)}), bf16[8,128,1024]{2,1,0:T(8,128)(2,1)S(1)}, u32[]{:S(2)}, u32[]{:S(2)}) async-start(bf16[8,128,1024]{2,1,0:T(8,128)(2,1)} %bitcast.101), calls=%async_computation.1 | async-start | bytes 4194304 | tf_op jit(solution)/shard_map/all_to_all | solution.py:658
  551.8 151.0 %all-reduce.8.cloned.1.call-start = ((), (), s32[]{:S(2)}) async-start(), calls=%async_computation.4 | async-start | bytes 786432 | tf_op jit(solution)/shard_map/psum | solution.py:645
Sparse Core Ops, SparseCore 0:
  22.8 209.3 all-gather.4
  234.4 137.1 all-gather.6
  558.1 144.6 all-reduce.7

commit v2 on v1

v2 whole, which is shorter than its diff:
```python
import functools
import math

import jax
import jax.numpy as jnp
from jax import lax
from jax.experimental import pallas as pl
from jax.experimental.pallas import tpu as pltpu
from jax.sharding import PartitionSpec as P

HEAD = 64
PAIR = 2 * HEAD
EPSILON = 1e-05
MASKED = -1000000000.0
VMEM = 56 * 1024 * 1024
SECTIONS = 2

bf16 = jnp.bfloat16
f32 = jnp.float32


def dot_nn(left, right):
    return lax.dot_general(left, right, (((1,), (0,)), ((), ())), preferred_element_type=f32)


def dot_nt(left, right):
    return lax.dot_general(left, right, (((1,), (1,)), ((), ())), preferred_element_type=f32)


def dot_tn(left, right):
    return lax.dot_general(left, right, (((0,), (0,)), ((), ())), preferred_element_type=f32)


def unit(hidden):
    average = jnp.mean(hidden, axis=-1, keepdims=True)
    centered = hidden - average
    variance = jnp.mean(centered * centered, axis=-1, keepdims=True)
    inverse = lax.rsqrt(variance + EPSILON)
    return centered * inverse, inverse


def unit_back(grad, normed, inverse, gain):
    scaled = grad * gain
    return inverse * (
        scaled
        - jnp.mean(scaled, axis=-1, keepdims=True)
        - normed * jnp.mean(scaled * normed, axis=-1, keepdims=True)
    )


GROUP = 1024


class Copies:
    def __init__(self, semaphores):
        self.semaphores = semaphores
        self.used = 0

    def start(self, source, target):
        copy = pltpu.make_async_copy(source, target, self.semaphores.at[self.used])
        self.used += 1
        copy.start()
        return copy


def wait(copies):
    for copy in copies:
        copy.wait()


def call(kernel, in_specs, out_specs, out_shape, scratch=(), grid=None, flops=0, moved=0, exps=0):
    more = {} if grid is None else {"grid": grid}
    return pl.pallas_call(
        kernel,
        in_specs=in_specs,
        out_specs=out_specs,
        out_shape=out_shape,
        scratch_shapes=list(scratch),
        compiler_params=pltpu.CompilerParams(vmem_limit_bytes=VMEM),
        cost_estimate=pl.CostEstimate(flops=flops, bytes_accessed=moved, transcendentals=exps),
        **more,
    )


IN_VMEM = pl.BlockSpec(memory_space=pltpu.VMEM)
IN_HBM = pl.BlockSpec(memory_space=pl.ANY)
IN_SMEM = pl.BlockSpec(memory_space=pltpu.SMEM)


def whole(shape):
    return pl.BlockSpec(shape, lambda i: (0,) * len(shape))


def struct(shape, dtype):
    return jax.ShapeDtypeStruct(shape, dtype)


def load_heads(copies, ref, first, parts, pairs, target):
    started = []
    for part in range(parts):
        started.append([])
        for pair in range(pairs):
            for half in range(2):
                place = (part * pairs + pair) * PAIR + half * HEAD
                started[-1].append(
                    copies.start(
                        ref.at[half, pair, pl.ds(first + part * HEAD, HEAD)],
                        target.at[pl.ds(place, HEAD)],
                    )
                )
    return started


class Hidden:
    def __init__(self, copies, refs, pieces, up, down):
        self.copies, self.refs, self.pieces = copies, refs, pieces
        self.targets = (up, down)
        self.groups = up.shape[0] // GROUP
        self.started = 0
        self.loads = ([], [])

    def fetch(self, group):
        end = (group + 1) * GROUP
        place = sum(piece[4] for piece in self.pieces[: self.started])
        while self.started < len(self.pieces) and place < end:
            index, lead, *firsts, rows = self.pieces[self.started]
            for kind in range(2):
                copy = self.copies.start(
                    self.refs[index].at[(*lead, pl.ds(firsts[kind], rows))],
                    self.targets[kind].at[pl.ds(place, rows)],
                )
                self.loads[kind].append((place, copy))
            place += rows
            self.started += 1

    def wait(self, group, kind):
        end = (group + 1) * GROUP
        while self.loads[kind] and self.loads[kind][0][0] < end:
            self.loads[kind].pop(0)[1].wait()


def project_kernel(first, x_ref, w_ref, b_ref, q_ref, kv_ref, weight, stage, semaphores):
    copies = Copies(semaphores)
    pairs = stage.shape[1]
    wide = pairs * PAIR
    loads = load_heads(copies, w_ref, first, 3, pairs, weight)
    stores = []
    for part in (0, 1, 2):
        wait(loads[part])
        out = dot_nt(x_ref[...], weight[part * wide : (part + 1) * wide]) + b_ref[part]
        out = out.astype(bf16)
        if part == 0:
            out = out * bf16(1.0 / math.sqrt(HEAD))
        for pair in range(pairs):
            stage[part, pair] = out[:, pair * PAIR : (pair + 1) * PAIR]
        target = q_ref if part == 0 else kv_ref.at[part - 1]
        stores.append(copies.start(stage.at[part], target))
    wait(stores)


def project(x, table, bias):
    count, width = x.shape
    pairs = table[0].shape[1]
    return call(
        functools.partial(project_kernel, table[1]),
        [IN_VMEM, IN_HBM, IN_VMEM],
        [IN_HBM, IN_HBM],
        [struct((pairs, count, PAIR), bf16), struct((2, pairs, count, PAIR), bf16)],
        scratch=[
            pltpu.VMEM((3 * pairs * PAIR, width), bf16),
            pltpu.VMEM((3, pairs, count, PAIR), bf16),
            pltpu.SemaphoreType.DMA((6 * pairs + 3,)),
        ],
        flops=2 * count * width * 3 * PAIR * pairs,
        moved=2 * (count * width * 4 + 3 * width * PAIR * pairs),
    )(x, table[0], bias)


def feed_forward(copies, places, x_ref, mixed_ref, ow_ref, h_refs, vec_ref, ub_ref,
                 z1_ref, r1_ref, weight_o, weight_u, weight_d, slope, normed, low, acc):
    o_first, pieces = places
    pairs = mixed_ref.shape[0]
    loads_o = load_heads(copies, ow_ref, o_first, 1, pairs, weight_o)[0]
    weights = Hidden(copies, h_refs, pieces, weight_u, weight_d)
    groups = weights.groups
    weights.fetch(0)
    mixed = jnp.concatenate([mixed_ref[i] for i in range(pairs)], axis=1)
    wait(loads_o)
    attended = dot_nn(mixed, weight_o[...])
    z, r = unit(x_ref[...].astype(f32) + attended + vec_ref[0:1])
    z1_ref[...] = z
    r1_ref[...] = r
    out = z * vec_ref[2:3] + vec_ref[4:5]
    normed[...] = out
    low[...] = out.astype(bf16)

    def before(group):
        weights.fetch(min(group + 1, groups - 1))
        weights.wait(group, 0)
        span = slice(group * GROUP, (group + 1) * GROUP)
        return dot_nt(low[...], weight_u[span]) + ub_ref[:, span]

    later = before(0)
    for group in range(groups):
        pre = later
        if group + 1 < groups:
            later = before(group + 1)
        span = slice(group * GROUP, (group + 1) * GROUP)
        spread = 0.5 + 0.5 * lax.erf(pre * math.sqrt(0.5))
        bell = jnp.exp(-0.5 * pre * pre) * (1.0 / math.sqrt(2.0 * math.pi))
        slope[:, span] = (spread + pre * bell).astype(bf16)
        weights.wait(group, 1)
        out = dot_nn((pre * spread).astype(bf16), weight_d[span])
        if group == 0:
            acc[...] = out
        else:
            acc[...] += out
    return unit(normed[...] + acc[...] + vec_ref[1:2])


def feed_kernel(places, sources, blocks, x_ref, mixed_ref, ow_ref, vec_ref, ub_ref, rank_ref, *rest):
    h_refs = rest[:sources]
    out_refs = rest[sources : sources + max(blocks, 1)]
    (z1_ref, r1_ref, z2_ref, r2_ref, slope_ref, weight_o, weight_u, weight_d,
     z1, slope, normed, low, acc, semaphores) = rest[sources + max(blocks, 1) :]
    copies = Copies(semaphores)
    z, r = feed_forward(
        copies, places, x_ref, mixed_ref, ow_ref, h_refs, vec_ref, ub_ref,
        z1, r1_ref, weight_o, weight_u, weight_d, slope, normed, low, acc,
    )
    stores = [copies.start(z1, z1_ref), copies.start(slope, slope_ref)]
    acc[...] = z
    r2_ref[...] = r
    stores.append(copies.start(acc, z2_ref))
    low[...] = (z * vec_ref[3:4] + vec_ref[5:6]).astype(bf16)
    rows = low.shape[0] // max(blocks, 1)
    for j in range(max(blocks, 1)):
        start = pl.multiple_of((rank_ref[0] ^ j) * rows, rows) if blocks else 0
        stores.append(copies.start(low.at[pl.ds(start, rows)], out_refs[j]))
    wait(stores)


def feed_scratch(count, width, wide, hidden, pairs):
    return [
        pltpu.VMEM((wide, width), bf16),
        pltpu.VMEM((hidden, width), bf16),
        pltpu.VMEM((hidden, width), bf16),
        pltpu.VMEM((count, width), f32),
        pltpu.VMEM((count, hidden), bf16),
        pltpu.VMEM((count, width), f32),
        pltpu.VMEM((count, width), bf16),
        pltpu.VMEM((count, width), f32),
        pltpu.SemaphoreType.DMA((16 * pairs + 8,)),
    ]


def feed_sizes(x, mixed, up_bias):
    count, width = x.shape
    pairs = mixed.shape[0]
    return count, width, pairs, pairs * PAIR, up_bias.shape[1]


def feed(x, mixed, tables, vectors, up_bias, rank, blocks):
    o_table, (arrays, pieces) = tables
    count, width, pairs, wide, hidden = feed_sizes(x, mixed, up_bias)
    square = struct((count, width), f32)
    column = struct((count, 1), f32)
    parts = max(blocks, 1)
    out, kept = [], []
    found = call(
        functools.partial(feed_kernel, (o_table[1], pieces), len(arrays), blocks),
        [IN_VMEM, IN_VMEM, IN_HBM, IN_VMEM, IN_VMEM, IN_SMEM] + [IN_HBM] * len(arrays),
        [IN_HBM] * parts + [IN_HBM, IN_VMEM, IN_HBM, IN_VMEM, IN_HBM],
        [struct((count // parts, width), bf16)] * parts
        + [square, column, square, column, struct((count, hidden), bf16)],
        scratch=feed_scratch(count, width, wide, hidden, pairs),
        flops=2 * count * width * (wide + 2 * hidden),
        moved=2 * (2 * hidden * width + 12 * count * width),
        exps=2 * count * hidden,
    )(x, mixed, o_table[0], vectors, up_bias, rank, *arrays)
    return (found[:blocks] if blocks else found[0], *found[parts:])


def feed_back(weight_o, weight_u, weight_d, vec_ref, z1, r1, slope, low, acc,
              first_ref, mixed_ref, before=lambda group: None, ready=lambda: None):
    pairs = mixed_ref.shape[0]
    low[...] = acc[...].astype(bf16)
    for group in range(weight_u.shape[0] // GROUP):
        before(group)
        span = slice(group * GROUP, (group + 1) * GROUP)
        d_act = dot_nt(low[...], weight_d[span])
        d_pre = (d_act * slope[:, span].astype(f32)).astype(bf16)
        acc[...] += dot_nn(d_pre, weight_u[span])
    ready()
    first = unit_back(acc[...], z1[...], r1[...], vec_ref[2:3])
    first_ref[...] = first
    d_mixed = dot_nt(first.astype(bf16), weight_o[...]).astype(bf16)
    for pair in range(pairs):
        mixed_ref[pair] = d_mixed[:, pair * PAIR : (pair + 1) * PAIR]


def scatter_rows(stage, rank_ref, targets):
    rows = targets[0].shape[0]
    for j, target in enumerate(targets):
        start = pl.multiple_of((rank_ref[0] ^ j) * rows, rows)
        target[...] = stage[pl.ds(start, rows)]


def project_back(first_ref, dq_ref, own_ref, got_ref, weight, loads):
    pairs = dq_ref.shape[0]
    wide = pairs * PAIR
    total = first_ref[...]
    for part in range(3):
        columns = []
        for pair in range(pairs):
            if part == 0:
                columns.append(dq_ref[pair])
            else:
                column = own_ref[part - 1, pair].astype(f32)
                for i in range(got_ref.shape[0]):
                    column += got_ref[i, part - 1, pair].astype(f32)
                columns.append(column.astype(bf16))
        wait(loads[part])
        total += dot_nn(jnp.concatenate(columns, axis=1), weight[part * wide : (part + 1) * wide])
    return total


def link_kernel(p_first, places, sources, *rest):
    if p_first is None:
        grad_ref, *rest = rest
    else:
        first1_ref, dq_ref, own_ref, got_ref, pw_ref, *rest = rest
    ow_ref, vec_ref, z1_ref, r1_ref, z2_ref, r2_ref, slope_ref, *rest = rest
    h_refs = rest[:sources]
    (first_ref, d_mixed_ref,
     weight_o, weight_u, weight_d, z1, slope, low, acc, semaphores, *weight_p) = rest[sources:]
    o_first, pieces = places
    copies = Copies(semaphores)
    pairs = d_mixed_ref.shape[0]
    if p_first is not None:
        loads_p = load_heads(copies, pw_ref, p_first, 3, pairs, weight_p[0])
    weights = Hidden(copies, h_refs, pieces, weight_u, weight_d)
    groups = weights.groups
    slopes = []

    def fetch(group):
        weights.fetch(group)
        span = (slice(None), pl.ds(group * GROUP, GROUP))
        slopes.append(copies.start(slope_ref.at[span], slope.at[span]))

    if p_first is None:
        fetch(0)
        grad = grad_ref[...].astype(f32)
    else:
        total = project_back(first1_ref, dq_ref, own_ref, got_ref, weight_p[0], loads_p)
        fetch(0)
        grad = total.astype(bf16).astype(f32)
    acc[...] = unit_back(grad, z2_ref[...], r2_ref[...], vec_ref[3:4])
    last = []

    def before(group):
        if group + 1 < groups:
            fetch(group + 1)
        else:
            last.append(copies.start(z1_ref, z1))
            last.extend(load_heads(copies, ow_ref, o_first, 1, pairs, weight_o)[0])
        slopes[group].wait()
        weights.wait(group, 0)
        weights.wait(group, 1)

    feed_back(
        weight_o, weight_u, weight_d, vec_ref, z1, r1_ref, slope, low, acc, first_ref, d_mixed_ref,
        before, lambda: wait(last),
    )


def link(grads, p_table, tables, vectors, kept):
    o_table, (arrays, pieces) = tables
    count, width = grads[0].shape
    pairs = o_table[0].shape[1]
    wide = pairs * PAIR
    slope = kept[-1]
    hidden = slope.shape[1]
    more = [] if p_table is None else [p_table[0]]
    return call(
        functools.partial(
            link_kernel, p_table and p_table[1], (o_table[1], pieces), len(arrays)
        ),
        [IN_VMEM] * len(grads) + [IN_HBM] * len(more)
        + [IN_HBM, IN_VMEM, IN_HBM, IN_VMEM, IN_VMEM, IN_VMEM, IN_HBM]
        + [IN_HBM] * len(arrays),
        [IN_VMEM] * 2,
        [struct((count, width), f32), struct((pairs, count, PAIR), bf16)],
        scratch=[
            pltpu.VMEM((wide, width), bf16),
            pltpu.VMEM((hidden, width), bf16),
            pltpu.VMEM((hidden, width), bf16),
            pltpu.VMEM((count, width), f32),
            pltpu.VMEM((count, hidden), bf16),
            pltpu.VMEM((count, width), bf16),
            pltpu.VMEM((count, width), f32),
            pltpu.SemaphoreType.DMA((16 * pairs + 16,)),
        ]
        + [pltpu.VMEM((3 * wide, width), bf16)] * len(more),
        flops=2 * count * width * (4 * wide + 2 * hidden),
        moved=2 * (2 * hidden * width + 4 * wide * width + 16 * count * width),
    )(*grads, *more, o_table[0], vectors, *kept, *arrays)


def leave_kernel(p_first, first_ref, dq_ref, own_ref, got_ref, pw_ref, rank_ref, *rest):
    (*out_refs, weight_p, low, semaphores) = rest
    copies = Copies(semaphores)
    loads = load_heads(copies, pw_ref, p_first, 3, dq_ref.shape[0], weight_p)
    low[...] = project_back(first_ref, dq_ref, own_ref, got_ref, weight_p, loads).astype(bf16)
    scatter_rows(low, rank_ref, out_refs)


def leave(first, dq, own, got, p_table, rank, blocks):
    count, width = first.shape
    pairs = dq.shape[0]
    return call(
        functools.partial(leave_kernel, p_table[1]),
        [IN_VMEM] * 4 + [IN_HBM, IN_SMEM],
        [IN_VMEM] * blocks,
        [struct((count // blocks, width), bf16)] * blocks,
        scratch=[
            pltpu.VMEM((3 * pairs * PAIR, width), bf16),
            pltpu.VMEM((count, width), bf16),
            pltpu.SemaphoreType.DMA((6 * pairs,)),
        ],
        flops=2 * count * width * 3 * PAIR * pairs,
        moved=2 * (count * width * 7 + 3 * width * PAIR * pairs),
    )(first, dq, own, got, p_table[0], rank)


def attend_kernel(
    prefix_count, q_ref, own_ref, other_ref, pk_ref, pv_ref, sq_ref, sk_ref,
    mixed_ref, raised_ref, inverse_ref, bias_ref,
):
    pad = pk_ref.shape[1]
    others = other_ref.shape[0]

    @pl.when(pl.program_id(0) == 0)
    def _():
        row = lax.broadcasted_iota(jnp.int32, (pad, bias_ref.shape[1]), 0)
        bias_ref[:pad] = jnp.where(row < prefix_count, 0.0, MASKED)
        keys = sk_ref[...]
        same = (keys == sq_ref[...]) & (keys >= 0)
        bias_ref[pad:] = jnp.where(same, 0.0, MASKED)

    keys = jnp.concatenate(
        [pk_ref[0], own_ref[0, 0]] + [other_ref[i, 0, 0] for i in range(others)], axis=0
    )
    values = jnp.concatenate(
        [pv_ref[0], own_ref[1, 0]] + [other_ref[i, 1, 0] for i in range(others)], axis=0
    )
    queries = q_ref[0]
    lane = lax.broadcasted_iota(jnp.int32, queries.shape, 1)
    parts = []
    inverses = []
    for head in range(2):
        chosen = (lane // HEAD) == head
        scores = dot_nt(keys, jnp.where(chosen, queries, bf16(0))) + bias_ref[...]
        raised = jnp.exp(scores - jnp.max(scores, axis=0, keepdims=True))
        inverse = 1.0 / jnp.sum(raised, axis=0, keepdims=True)
        low = raised.astype(bf16)
        raised_ref[0, head] = low
        out = dot_tn(values, low)[head * HEAD : (head + 1) * HEAD]
        parts.append(out * inverse)
        inverses.append(jnp.broadcast_to(inverse, out.shape))
    mixed_ref[0] = jnp.concatenate(parts, axis=0).T.astype(bf16)
    inverse_ref[0] = jnp.concatenate(inverses, axis=0).T


def attend(q, own, other, pk, pv, prefix_count, seg_q, seg_k):
    pairs, count, _ = q.shape
    others = other.shape[0]
    pad = pk.shape[1]
    total = pad + count * (others + 1)
    by_pair = pl.BlockSpec((1, count, PAIR), lambda i: (i, 0, 0))
    by_prefix = pl.BlockSpec((1, pad, PAIR), lambda i: (i, 0, 0))
    return call(
        functools.partial(attend_kernel, prefix_count),
        [
            by_pair,
            pl.BlockSpec((2, 1, count, PAIR), lambda i: (0, i, 0, 0)),
            pl.BlockSpec((others, 2, 1, count, PAIR), lambda i: (0, 0, i, 0, 0)),
            by_prefix,
            by_prefix,
            whole((1, count)),
            whole((total - pad, 1)),
        ],
        [
            by_pair,
            pl.BlockSpec((1, 2, total, count), lambda i: (i, 0, 0, 0)),
            by_pair,
        ],
        [
            struct((pairs, count, PAIR), bf16),
            struct((pairs, 2, total, count), bf16),
            struct((pairs, count, PAIR), f32),
        ],
        scratch=[pltpu.VMEM((total, count), f32)],
        grid=(pairs,),
        flops=8 * total * count * PAIR * pairs,
        moved=4 * pairs * total * count,
        exps=2 * pairs * total * count,
    )(q, own, other, pk, pv, seg_q, seg_k)


def attend_back_kernel(
    grad_ref, mixed_ref, inverse_ref, raised_ref, q_ref, own_ref, other_ref, pk_ref, pv_ref,
    dq_ref, down_ref, dother_ref, prefix_ref,
):
    pad = pk_ref.shape[1]
    others = other_ref.shape[0]
    count = q_ref.shape[1]
    keys = jnp.concatenate(
        [pk_ref[0], own_ref[0, 0]] + [other_ref[i, 0, 0] for i in range(others)], axis=0
    )
    values = jnp.concatenate(
        [pv_ref[0], own_ref[1, 0]] + [other_ref[i, 1, 0] for i in range(others)], axis=0
    )
    queries = q_ref[0]
    lane = lax.broadcasted_iota(jnp.int32, queries.shape, 1)
    scaled = grad_ref[0].astype(f32) * inverse_ref[0]
    products = (scaled * mixed_ref[0].astype(f32)).T
    scaled = scaled.astype(bf16)
    d_keys = jnp.zeros(keys.shape, f32)
    d_values = jnp.zeros(keys.shape, f32)
    parts = []
    for head in range(2):
        chosen = (lane // HEAD) == head
        span = slice(head * HEAD, (head + 1) * HEAD)
        delta = jnp.sum(products[span], axis=0, keepdims=True)
        here = jnp.where(chosen, scaled, bf16(0))
        raised = raised_ref[0, head]
        d_score = (raised.astype(f32) * (dot_nt(values, here) - delta)).astype(bf16)
        d_values += dot_nn(raised, here)
        d_keys += dot_nn(d_score, jnp.where(chosen, queries, bf16(0)))
        parts.append(dot_tn(keys, d_score)[span])
    d_query = jnp.concatenate(parts, axis=0).T * (1.0 / math.sqrt(HEAD))
    dq_ref[0] = d_query.astype(bf16)
    prefix_ref[0, :pad] = d_keys[:pad]
    prefix_ref[0, pad:] = d_values[:pad]
    down_ref[0, 0] = d_keys[pad : pad + count].astype(bf16)
    down_ref[1, 0] = d_values[pad : pad + count].astype(bf16)
    for i in range(others):
        span = slice(pad + (i + 1) * count, pad + (i + 2) * count)
        dother_ref[i, 0, 0] = d_keys[span].astype(bf16)
        dother_ref[i, 1, 0] = d_values[span].astype(bf16)


def attend_back(grad, mixed, inverse, raised, q, own, other, pk, pv):
    pairs, count, _ = q.shape
    others = other.shape[0]
    pad = pk.shape[1]
    total = pad + count * (others + 1)
    by_pair = pl.BlockSpec((1, count, PAIR), lambda i: (i, 0, 0))
    by_prefix = pl.BlockSpec((1, pad, PAIR), lambda i: (i, 0, 0))
    by_own = pl.BlockSpec((2, 1, count, PAIR), lambda i: (0, i, 0, 0))
    by_other = pl.BlockSpec((others, 2, 1, count, PAIR), lambda i: (0, 0, i, 0, 0))
    return call(
        attend_back_kernel,
        [
            by_pair, by_pair, by_pair,
            pl.BlockSpec((1, 2, total, count), lambda i: (i, 0, 0, 0)),
            by_pair, by_own, by_other, by_prefix, by_prefix,
        ],
        [by_pair, by_own, by_other, pl.BlockSpec((1, 2 * pad, PAIR), lambda i: (i, 0, 0))],
        [
            struct(q.shape, bf16),
            struct(own.shape, bf16),
            struct(other.shape, bf16),
            struct((pairs, 2 * pad, PAIR), f32),
        ],
        grid=(pairs,),
        flops=16 * total * count * PAIR * pairs,
        moved=4 * pairs * total * count,
    )(grad, mixed, inverse, raised, q, own, other, pk, pv)


def per_device(
    boundary, segment_ids, project_weight, project_bias, output_weight, output_biases,
    norm_gains, norm_shifts, up_weight, up_bias, down_weight, prefix_keys, prefix_values,
):
    section = lax.axis_index("section")
    rank = lax.axis_index("tensor")
    ranks = lax.axis_size("tensor")
    is_first = section == 0
    micro, slots, rows, width = boundary.shape[1:]
    length = slots * ranks
    row_count = micro * rows
    chips = ranks // row_count
    blocks = SECTIONS * chips
    count = length // blocks
    place = rank % chips
    swap = [(0, 1), (1, 0)]
    after = lambda value, *first: lax.optimization_barrier((value, *first))[0]
    heads_all = project_weight.shape[3] * ranks
    pairs = heads_all // PAIR
    shards = ranks // pairs
    prefix_count = prefix_keys.shape[1]
    pad = -(-prefix_count // 32) * 32
    low_width = project_weight.shape[3] // 2
    hidden = up_weight.shape[2] // 2

    quick = chips == 1 and ranks == 8 and lax.axis_size("dp") == 2

    half_ranks = ranks // 2
    low_rank = rank % half_ranks
    block = section * chips + place
    by_row = jnp.transpose(boundary[0], (0, 2, 1, 3)).reshape(row_count, slots, width)

    def ordered(parts):
        for bit in (1, 2):
            flip = (low_rank & bit) != 0
            parts = [jnp.where(flip, parts[i ^ bit], part) for i, part in enumerate(parts)]
        return parts

    if quick:
        lower, upper = by_row[:half_ranks], by_row[half_ranks:]
        keep = jnp.where(is_first, lower, upper)
        got = lax.ppermute(jnp.where(is_first, upper, lower), "section", swap)

        def arrive(rows_here):
            parts = []
            for j in range(half_ranks):
                route = [
                    (s * ranks + t, (t // half_ranks) * ranks + half_ranks * s + ((t % half_ranks) ^ j))
                    for s in range(SECTIONS)
                    for t in range(ranks)
                ]
                part = lax.dynamic_index_in_dim(rows_here, low_rank ^ j, 0, keepdims=False)
                parts.append(lax.ppermute(part, ("section", "tensor"), route))
            return jnp.concatenate(ordered(parts), axis=0)

        tokens = arrive(jnp.where(is_first, keep, got))
        cotangent_rows = jnp.where(is_first, got, keep)
    else:
        if chips > 1:
            by_row = jnp.repeat(by_row, chips, axis=0)
        row = lax.all_to_all(by_row, "tensor", 0, 0, tiled=True).reshape(length, width)
        other_block = (1 - section) * chips + place
        mine = lax.dynamic_slice_in_dim(row, block * count, count, 0)
        theirs = lax.dynamic_slice_in_dim(row, other_block * count, count, 0)
        got = lax.ppermute(theirs, "section", swap)
        tokens = jnp.where(is_first, mine, got)
        cotangent = jnp.where(is_first, got, mine)

    project_rows = jnp.transpose(project_weight[0], (1, 2, 0)).reshape(3, 2, low_width, width)
    project_rows = jnp.transpose(project_rows, (1, 0, 2, 3)).reshape(2, 3 * low_width, width)
    out_rows = output_weight[0].reshape(2, low_width, width)
    up_rows = jnp.transpose(up_weight[0], (1, 0)).reshape(2, hidden, width)
    down_rows = down_weight[0].reshape(2, hidden, width)
    small = jnp.concatenate(
        [
            jnp.transpose(project_bias[0].reshape(3, 2, low_width), (1, 0, 2)).reshape(2, -1),
            up_bias[0].reshape(2, hidden),
            jnp.transpose(prefix_keys[0].reshape(-1, 2, low_width), (1, 0, 2)).reshape(2, -1),
            jnp.transpose(prefix_values[0].reshape(-1, 2, low_width), (1, 0, 2)).reshape(2, -1),
        ],
        axis=1,
    )
    small_size = small.shape[1]
    small_rows = -(-small_size // (16 * width)) * 16
    small = jnp.pad(small, ((0, 0), (0, small_rows * width - small_size)))
    packed = jnp.concatenate(
        [project_rows, out_rows, up_rows, down_rows, small.reshape(2, small_rows, width)], axis=1
    )
    keep = lax.dynamic_index_in_dim(packed, section, 0, keepdims=False)
    give = lax.dynamic_index_in_dim(packed, 1 - section, 0, keepdims=False)
    got = lax.ppermute(give, "section", swap)
    layer_rows = [jnp.where(is_first, keep, got), jnp.where(is_first, got, keep)]
    sizes = [3 * low_width, low_width, hidden, hidden, small_rows]
    p_end, o_end, u_end, d_end, s_end = [sum(sizes[: i + 1]) for i in range(len(sizes))]
    plane = lax.axis_index("dp")
    gather = lambda parts: lax.all_gather(
        jnp.concatenate(parts, axis=0), ("section", "tensor"), axis=0
    ).reshape(2, ranks, -1, width)

    def unpack(flat):
        cut = 0
        found = []
        for groups, size in ((3, low_width), (1, hidden), (prefix_count, low_width), (prefix_count, low_width)):
            part = flat[:, :, cut : cut + groups * size].reshape(2, pairs, shards, groups, size)
            cut += groups * size
            if shards == 1:
                part = part[:, :, 0]
            else:
                part = jnp.transpose(part, (2, 1, 3, 0, 4)).reshape(2, pairs, groups, 2 * size)
            found.append(part)
        p_bias = jnp.transpose(found[0], (2, 1, 0, 3)).reshape(3, 1, heads_all).astype(f32)
        prefix = [
            jnp.pad(
                jnp.transpose(part, (1, 2, 0, 3)).reshape(pairs, prefix_count, PAIR),
                ((0, 0), (0, pad - prefix_count), (0, 0)),
            )
            for part in found[2:]
        ]
        return p_bias, found[1][:, :, 0], prefix[0], prefix[1]

    tables = []
    smalls = []
    early_rows = [
        layer_rows[0][:d_end], layer_rows[1][:p_end], layer_rows[0][d_end:], layer_rows[1][d_end:],
    ]
    late_rows = layer_rows[1][p_end:d_end]
    early = gather(early_rows)
    late = gather([after(late_rows, early, tokens)])
    def table(array, first, size, groups=1):
        if shards == 1:
            return (array, first, size)
        part = array[:, :, first : first + size].reshape(
            2, pairs, shards, groups, size // groups, width
        )
        part = jnp.transpose(part, (2, 1, 3, 0, 4, 5))
        return (part.reshape(2, pairs, 2 * size, width), 0, 2 * size)

    for layer in range(2):
        source, shift = (late, -p_end) if layer else (early, 0)
        up, u_first, rows_here = table(source, shift + o_end, 2 * hidden, 2)
        rows_here //= 2
        pieces = tuple(
            (0, (s, t), u_first, u_first + rows_here, rows_here)
            for s in range(2)
            for t in range(pairs)
        )
        tables.append(
            (
                table(early, layer * d_end, 3 * low_width, 3),
                table(source, shift + p_end, low_width),
                ((up,), pieces),
            )
        )
        start = d_end + p_end + layer * small_rows
        p_bias, u_bias, pk, pv = unpack(
            early[:, :, start : start + small_rows].reshape(2, ranks, -1)
        )
        smalls.append((p_bias, u_bias.reshape(1, -1).astype(f32), pk, pv))

    own_vectors = jnp.concatenate(
        [output_biases[0], norm_gains[0], norm_shifts[0], norm_shifts[0]], axis=0
    )
    got_vectors = lax.ppermute(own_vectors, "section", swap)
    vectors = [
        jnp.where(is_first, own_vectors, got_vectors).astype(f32),
        jnp.where(is_first, got_vectors, own_vectors).astype(f32),
    ]

    def flips():
        routes = []
        for distance in range(1, blocks):
            route = []
            for s in range(SECTIONS):
                for t in range(ranks):
                    index = (s * chips + t % chips) ^ distance
                    route.append(
                        (s * ranks + t, (index // chips) * ranks + t // chips * chips + index % chips)
                    )
            routes.append(route)
        return routes

    routes = flips()

    def exchange(parts):
        return jnp.stack(
            [
                lax.ppermute(part, ("section", "tensor"), route) if chips > 1
                else lax.ppermute(part, "section", swap)
                for part, route in zip(parts, routes)
            ]
        )

    segments = lax.dynamic_index_in_dim(
        segment_ids.reshape(row_count, length), rank // chips, 0, keepdims=False
    )
    seg_q = lax.dynamic_slice_in_dim(segments, block * count, count, 0)
    seg_k = jnp.concatenate(
        [
            lax.dynamic_slice_in_dim(segments, (block ^ distance) * count, count, 0)
            for distance in range(blocks)
        ]
    )[:, None]
    seg_q = seg_q[None, :]

    out_blocks = half_ranks if quick else 1
    order = (low_rank if quick else 0 * rank).astype(jnp.int32).reshape(1)
    saved = []
    x = tokens
    for layer in range(2):
        p_table, *others = tables[layer]
        p_bias, u_bias, pk, pv = smalls[layer]
        q, own = project(x, p_table, p_bias)
        other = exchange([own] * (blocks - 1))
        mixed, raised, inverse = attend(q, own, other, pk, pv, prefix_count, seg_q, seg_k)
        saved.append((mixed, inverse, raised, q, own, other, pk, pv))
        if layer == 1 and quick:
            cotangent = arrive(after(cotangent_rows, late))
        x, *kept = feed(
            x, mixed, others, vectors[layer], u_bias, order, out_blocks if layer else 0
        )
        saved[-1] += (kept,)
    outs = x
    kept_0, kept_1 = (entry[-1] for entry in saved)
    saved = [entry[:-1] for entry in saved]
    first, d_mixed = link((cotangent,), None, tables[1][1:], vectors[1], kept_1)

    def send_blocks(parts):
        got = []
        for j, part in enumerate(parts):
            route = [
                (s * ranks + t, (t // half_ranks) * ranks + half_ranks * s + ((t % half_ranks) ^ j))
                for s in range(SECTIONS)
                for t in range(ranks)
            ]
            got.append(lax.ppermute(part, ("section", "tensor"), route))
        return got

    dq, down, dother, prefix_1 = attend_back(d_mixed, *saved[1])
    if quick:
        outs = send_blocks(outs)
        dother, *outs = lax.optimization_barrier((dother, *outs))
    got = exchange([dother[i] for i in range(blocks - 1)])
    first, d_mixed = link(
        (first, dq, down, got), tables[1][0], tables[0][1:], vectors[0], kept_0
    )
    dq, down, dother, prefix_0 = attend_back(d_mixed, *saved[0])
    got = exchange([dother[i] for i in range(blocks - 1)])
    if quick:
        prefix = jnp.stack([prefix_0, prefix_1], axis=1)
        lower, upper = prefix[: pairs // 2], prefix[pairs // 2 :]
        other = lax.ppermute(jnp.where(is_first, upper, lower), "section", swap)
        prefix = jnp.where(is_first, lower, upper) + other
        got, prefix = lax.optimization_barrier((got, prefix))
    grads = leave(first, dq, down, got, tables[0][0], order, out_blocks)

    if quick:
        grads = send_blocks(grads)
        prefix = sum(
            send_blocks(
                [
                    lax.dynamic_index_in_dim(prefix, low_rank ^ j, 0, keepdims=False)
                    for j in range(half_ranks)
                ]
            )
        )
        outs = jnp.stack(ordered(outs))
        prefix += lax.ppermute(prefix, "dp", swap)
        prefix = jnp.where(is_first, prefix[0], prefix[1]) + lax.ppermute(
            jnp.where(is_first, prefix[1], prefix[0]), "section", swap
        )
        grads = jnp.stack(ordered(grads))
        keep = jnp.where(is_first, grads, outs)
        got = lax.ppermute(jnp.where(is_first, outs, grads), "section", swap)
        back = jnp.concatenate(
            [jnp.where(is_first, keep, got), jnp.where(is_first, got, keep)], axis=0
        )
    else:
        keep = jnp.where(is_first, grads[0], outs[0])
        got = lax.ppermute(jnp.where(is_first, outs[0], grads[0]), "section", swap)
        row = jnp.zeros((length, width), bf16)
        row = lax.dynamic_update_slice_in_dim(
            row, jnp.where(is_first, keep, got), place * count, 0
        )
        row = lax.dynamic_update_slice_in_dim(
            row, jnp.where(is_first, got, keep), (chips + place) * count, 0
        )
        back = lax.all_to_all(row.reshape(ranks, slots, width), "tensor", 0, 0, tiled=True)
        back = jnp.sum(back.reshape(row_count, chips, slots, width), axis=1)
    result = jnp.transpose(back.reshape(micro, rows, slots, width), (0, 2, 1, 3))[None]

    if quick:
        both = prefix.reshape(2, pad, PAIR)[:, :prefix_count]
    else:
        both = jnp.where(
            is_first,
            lax.psum(prefix_0, ("section", "dp", "tensor")),
            lax.psum(prefix_1, ("section", "dp", "tensor")),
        )
        both = both.reshape(pairs, 2, pad, PAIR)[:, :, :prefix_count]
        both = jnp.transpose(both, (1, 2, 0, 3)).reshape(2, prefix_count, heads_all)
        share = heads_all // ranks
        both = lax.dynamic_slice_in_dim(both, rank * share, share, 2)
    return (result, both[0][None], both[1][None])


def solution(mesh):
    in_specs = (
        P("section", None, "tensor", "dp", None),
        P(None, "dp", None),
        P("section", None, None, "tensor"),
        P("section", None, "tensor"),
        P("section", "tensor", None),
        P("section", None, None),
        P("section", None, None),
        P("section", None, None),
        P("section", None, "tensor"),
        P("section", "tensor"),
        P("section", "tensor", None),
        P("section", None, "tensor"),
        P("section", None, "tensor"),
    )
    out_specs = (
        P("section", None, "tensor", "dp", None),
        P("section", None, "tensor"),
        P("section", None, "tensor"),
    )
    return jax.shard_map(
        per_device, mesh=mesh, in_specs=in_specs, out_specs=out_specs, check_vma=False
    )
```

time: 719 us -> 522 us (0.73)
  waiting for transfers between devices: 389 us -> 196 us
  Pallas kernels: 254 us -> 206 us
  starting transfers between devices: 14.8 us -> 50.7 us
    psum x1 -> x0, waiting for transfers between devices: 149 us -> none  [per_device(): prefix_grads.append(lax.psum(flat, ('section', 'dp', 'tensor')))]
    all_to_all x2 -> x0, waiting for transfers between devices: 71.1 us -> none  [the longest x1 71.1 us: per_device(): lax.all_to_all(by_row, 'tensor', 0, 0, tiled=True).reshape(length, width)]
    pallas_call x12 -> x11, Pallas kernels: 254 us -> 206 us  [the longest x2 49 us: feed(): call(functools.partial(feed_kernel, (o_table[1], pieces), len(arrays), bl...]
    ppermute x1 -> x25, starting transfers between devices: 0.01 us -> 40 us  [the longest x12 13.8 us: send_blocks(): got.append(lax.ppermute(part, ('section', 'tensor'), route))]
    ppermute x1 -> x25, waiting for transfers between devices: 2.87 us -> 41.9 us  [the longest x8 23.7 us: arrive(): parts.append(lax.ppermute(part, ('section', 'tensor'), route))]
    all_to_all x2 -> x0, starting transfers between devices: 11.1 us -> none  [the longest x1 7.37 us: per_device(): lax.all_to_all(by_row, 'tensor', 0, 0, tiled=True).reshape(length, width)]
    ppermute x4, starting transfers between devices: 1.18 us -> 9.85 us  [exchange(): lax.ppermute(part, 'section', swap)]
  transfers between devices with their start and end apart: 13 -> 33, of which waited for: 11 -> 15; matrix products, arithmetic and copies ran while one was open for 3% -> 5% of each run, Pallas kernels for 13% -> 29%
where the time goes in v2:
time: 522 us; the launch traced here: 518 us
  Pallas kernels  206 us (39%)
  waiting for transfers between devices  196 us (38%)
  starting transfers between devices  50.7 us (10%)
  local copies, waits for them, and re-layouts  32.9 us (6%)
  other arithmetic  16.4 us (3%)
  between operations  14.8 us (3%)
    all_gather x2, waiting for transfers between devices, per_device(): lax.all_gather(jnp.concatenate(parts, axis=0), ('section', 'tensor'), axi...  143 us
    pallas_call x2, Pallas kernels, feed(): call(functools.partial(feed_kernel, (o_table[1], pieces), len(arrays), bl...  49 us
    pallas_call x2, Pallas kernels, attend_back(): call(attend_back_kernel, [by_pair, by_pair, by_pair, pl.BlockSpec((1, 2,...  43.9 us
    pallas_call x2, Pallas kernels, attend(): call(functools.partial(attend_kernel, prefix_count), [by_pair, pl.BlockSp...  43.5 us
    pallas_call x2, Pallas kernels, link(): call(functools.partial(link_kernel, p_table and p_table[1], (o_table[1],...  43 us
    ppermute x8, waiting for transfers between devices, arrive(): parts.append(lax.ppermute(part, ('section', 'tensor'), route))  23.7 us
    pallas_call x2, Pallas kernels, project(): call(functools.partial(project_kernel, table[1]), [IN_VMEM, IN_HBM, IN_VM...  16.5 us
    ppermute x12, starting transfers between devices, send_blocks(): got.append(lax.ppermute(part, ('section', 'tensor'), route))  13.8 us
  transfers between devices with their start and end apart: 33, of which 15 were waited for; matrix products, arithmetic and copies ran while one was open for 5% of the time, Pallas kernels for 29%

profile of v2, /device:TPU:0, one launch (start us, length us, event | category | flops | bytes accessed | tf_op | source)
XLA Modules:
  0.0 517.6 jit_solution(12751065657972499340)
XLA Ops:
  10.6 1.4 copy.51
  13.0 1.3 copy.72
  15.8 1.4 constant_dynamic-update-slice_fusion.1
  17.3 1.4 dynamic-slice_bitcast_fusion
  19.5 3.0 collective-permute-done.1
  22.6 2.1 bitcast_select_fusion
  24.9 1.5 pad_maximum_fusion.1
  26.4 3.0 broadcast_select_fusion
  32.3 1.4 collective-permute-done
  33.7 1.7 bitcast_select_fusion.2
  36.2 3.4 collective-permute-start.4
  39.6 1.9 collective-permute-start.5
  41.5 1.7 collective-permute-start.3
  43.2 8.8 %collective-permute-done.4 = bf16[128,1024]{1,0:T(8,128)(2,1)} collective-permute-done((bf16[128,1024]{1,0:T(8,128)(2,1)}, bf16[128,1024]{1,0:T(8,128)(2,1)}, u32[]{:S(2)}, u32[]{:S(2)}) %collective-permute-start.4) | collective-permute-done | bytes 262176 | tf_op jit(solution)/shard_map/ppermute | solution.py:635
  52.0 4.3 collective-permute-done.3
  56.4 10.6 %collective-permute-done.2 = bf16[128,1024]{1,0:T(8,128)(2,1)} collective-permute-done((bf16[128,1024]{1,0:T(8,128)(2,1)S(1)}, bf16[128,1024]{1,0:T(8,128)(2,1)}, u32[]{:S(2)}, u32[]{:S(2)}) %collective-permute-start.2) | collective-permute-done | bytes 262176 | tf_op jit(solution)/shard_map/ppermute | solution.py:635
  70.5 138.6 %all-gather.5.cloned.1.call-done = bf16[15872,1024]{1,0:T(8,128)(2,1)} async-done(((bf16[992,1024]{1,0:T(8,128)(2,1)}), bf16[15872,1024]{1,0:T(8,128)(2,1)}) %all-gather.5.cloned.1.call-update) | async-done | bytes 32505872 | tf_op jit(solution)/shard_map/all_gather | solution.py:678
  211.5 8.2 %shard_map.148 = (bf16[8,512,128]{2,1,0:T(8,128)(2,1)}, bf16[2,8,512,128]{3,2,1,0:T(8,128)(2,1)}) custom-call(bf16[512,1024]{1,0:T(8,128)(2,1)} %pad_maximum_fusion.2.x_ref, bf16[2,8,992,1024]{3,2,1,0:T(8,128)(2,1)} %bitcast.117, f32[3,1,1024]{2,1,0:T(1,128)} %reshape.158.b_ref), custom_call_target="tpu_custom_call" | custom-call | flops 3221225472 | bytes 10485760 | tf_op jit(solution)/shard_map/pallas_call | solution.py:164
  221.6 2.4 collective-permute-done.10
  228.4 21.8 %shard_map.149 = (bf16[8,512,128]{2,1,0:T(8,128)(2,1)}, bf16[8,2,1056,512]{3,2,1,0:T(8,128)(2,1)}, f32[8,512,128]{2,1,0:T(8,128)}) custom-call(bf16[8,512,128]{2,1,0:T(8,128)(2,1)} %get-tuple-element.55.q_ref, bf16[2,8,512,128]{3,2,1,0:T(8,128)(2,1)} %get-tuple-element.56.own_ref, bf16[1,2,8,512,128]{4,3,2,1,0:T(8,128)(2,1)} %bitcast.34.other_ref, ...), custom_call_target="tpu_custom_call" | custom-call | flops 4429185024 | bytes 17301504 | tf_op jit(solution)/shard_map/pallas_call | solution.py:482
  250.2 24.8 %shard_map.150 = (bf16[512,1024]{1,0:T(8,128)(2,1)}, f32[512,1024]{1,0:T(8,128)}, f32[512,1]{1,0:T(8,128)}, f32[512,1024]{1,0:T(8,128)}, f32[512,1]{1,0:T(8,128)}, /*index=5*/bf16[512,4096]{1,0:T(8,128)(2,1)}) custom-call(bf16[512,1024]{1,0:T(8,128)(2,1)} %pad_maximum_fusion.2.x_ref, bf16[8,512,128]{2,1,0:T(8,128)(2,1)} %get-tuple-element.57.mixed_ref, ...), custom_call_target="tpu_custom_call" | custom-call | flops 9663676416 | bytes 29360128 | tf_op jit(solution)/shard_map/pallas_call | solution.py:270
  275.0 8.3 %shard_map.151 = (bf16[8,512,128]{2,1,0:T(8,128)(2,1)}, bf16[2,8,512,128]{3,2,1,0:T(8,128)(2,1)}) custom-call(bf16[512,1024]{1,0:T(8,128)(2,1)} %get-tuple-element.58.x_ref, bf16[2,8,992,1024]{3,2,1,0:T(8,128)(2,1)} %bitcast.120, f32[3,1,1024]{2,1,0:T(1,128)} %reshape.160.b_ref), custom_call_target="tpu_custom_call" | custom-call | flops 3221225472 | bytes 10485760 | tf_op jit(solution)/shard_map/pallas_call | solution.py:164
  286.3 1.6 collective-permute-done.12
  287.8 21.7 %shard_map.152 = (bf16[8,512,128]{2,1,0:T(8,128)(2,1)}, bf16[8,2,1056,512]{3,2,1,0:T(8,128)(2,1)}, f32[8,512,128]{2,1,0:T(8,128)}) custom-call(bf16[8,512,128]{2,1,0:T(8,128)(2,1)} %get-tuple-element.59.q_ref, bf16[2,8,512,128]{3,2,1,0:T(8,128)(2,1)} %get-tuple-element.60.own_ref, bf16[1,2,8,512,128]{4,3,2,1,0:T(8,128)(2,1)} %bitcast.42.other_ref, ...), custom_call_target="tpu_custom_call" | custom-call | flops 4429185024 | bytes 17301504 | tf_op jit(solution)/shard_map/pallas_call | solution.py:482
  309.6 4.9 all-gather.7.cloned.1.call-done
  316.7 2.1 collective-permute-start.7
  319.2 24.2 %shard_map.153 = (bf16[128,1024]{1,0:T(8,128)(2,1)}, bf16[128,1024]{1,0:T(8,128)(2,1)}, bf16[128,1024]{1,0:T(8,128)(2,1)}, bf16[128,1024]{1,0:T(8,128)(2,1)}, f3...) custom-call(bf16[512,1024]{1,0:T(8,128)(2,1)} %get-tuple-element.58., ...), custom_call_target="tpu_custom_call" | custom-call | flops 9663676416 | bytes 29360128 | tf_op jit(solution)/shard_map/pallas_call | solution.py:270
  343.4 2.0 collective-permute-start.13
  346.6 1.9 collective-permute-start.15
  350.1 18.2 %shard_map.154 = (f32[512,1024]{1,0:T(8,128)}, bf16[8,512,128]{2,1,0:T(8,128)(2,1)}) custom-call(bf16[512,1024]{1,0:T(8,128)(2,1)} %pad_maximum_fusion.3.rest_0_, bf16[2,8,576,1024]{3,2,1,0:T(8,128)(2,1)} %bitcast.127, f32[8,1024]{1,0:T(8,128)} %get-tuple-element.156.vec_ref.rest_2_, f32[512,1024]{1,0:T(8,128)} %get-tuple-element.62.rest_3_, ...), custom_call_target="tpu_custom_call" | custom-call | flops 12884901888 | bytes 41943040 | tf_op jit(solution)/shard_map/pallas_call | solution.py:385
  368.3 22.0 %shard_map.155 = (bf16[8,512,128]{2,1,0:T(8,128)(2,1)}, bf16[2,8,512,128]{3,2,1,0:T(8,128)(2,1)}, bf16[1,2,8,512,128]{4,3,2,1,0:T(8,128)(2,1)}, f32[8,64,128]{2,1,0:T(8,128)}) custom-call(bf16[8,512,128]{2,1,0:T(8,128)(2,1)} %get-tuple-element.68.grad_ref, bf16[8,512,128]{2,1,0:T(8,128)(2,1)} %get-tuple-element.61.mixed_ref, ...), custom_call_target="tpu_custom_call" | custom-call | flops 8858370048 | bytes 17301504 | tf_op jit(solution)/shard_map/pallas_call | solution.py:563
  390.4 8.8 %collective-permute-start.17 = (bf16[2,8,512,128]{3,2,1,0:T(8,128)(2,1)}, bf16[2,8,512,128]{3,2,1,0:T(8,128)(2,1)S(1)}, u32[]{:S(2)}, u32[]{:S(2)}) collective-permute-start(bf16[2,8,512,128]{3,2,1,0:T(8,128)(2,1)} %bitcast.164), channel_id=1, source_target_pairs={{0,16},{16,0},{1,17},{17,1},{2,18},{18,2},{3,19},{19,3},{4,20},{20... | collective-permute-start | bytes 6291464 | tf_op jit(solution)/shard_map/ppermute | solution.py:770
  399.2 4.0 collective-permute-done.17
  403.2 1.3 copy-done.2
  404.6 24.9 %shard_map.156 = (f32[512,1024]{1,0:T(8,128)}, bf16[8,512,128]{2,1,0:T(8,128)(2,1)}) custom-call(f32[512,1024]{1,0:T(8,128)} %get-tuple-element.67.rest_0_, bf16[8,512,128]{2,1,0:T(8,128)(2,1)} %get-tuple-element.71.rest_1_, bf16[2,8,512,128]{3,2,1,0:T(8,128)(2,1)} %get-tuple-element.72.rest_2_, bf16[1,2,8,512,128]{4,3,2,1,0:T(8,128)(2,1)} %bitcast.136, ...), custom_call_target="tpu_custom_call" | custom-call | flops 12884901888 | bytes 41943040 | tf_op jit(solution)/shard_map/pallas_call | solution.py:385
  429.4 21.9 %shard_map.157 = (bf16[8,512,128]{2,1,0:T(8,128)(2,1)}, bf16[2,8,512,128]{3,2,1,0:T(8,128)(2,1)}, bf16[1,2,8,512,128]{4,3,2,1,0:T(8,128)(2,1)}, f32[8,64,128]{2,1,0:T(8,128)}) custom-call(bf16[8,512,128]{2,1,0:T(8,128)(2,1)} %get-tuple-element.85.grad_ref, bf16[8,512,128]{2,1,0:T(8,128)(2,1)} %get-tuple-element.57.mixed_ref, ...), custom_call_target="tpu_custom_call" | custom-call | flops 8858370048 | bytes 17301504 | tf_op jit(solution)/shard_map/pallas_call | solution.py:563
  453.0 3.0 collective-permute-done.19
  457.0 1.3 copy-done.1
  458.3 10.5 %shard_map.158 = (bf16[128,1024]{1,0:T(8,128)(2,1)}, bf16[128,1024]{1,0:T(8,128)(2,1)}, bf16[128,1024]{1,0:T(8,128)(2,1)}, bf16[128,1024]{1,0:T(8,128)(2,1)}) custom-call(f32[512,1024]{1,0:T(8,128)} %get-tuple-element.84.first_ref, bf16[8,512,128]{2,1,0:T(8,128)(2,1)} %get-tuple-element.88.dq_ref, bf16[2,8,512,128]{3,2,1,0:T(8,128)(2,1)} %get-tuple-element.89.own_ref, ...), custom_call_target="tpu_custom_call" | custom-call | flops 3221225472 | bytes 13631488 | tf_op jit(solution)/shard_map/pallas_call | solution.py:421
  468.9 2.7 collective-permute-start.21
  472.4 1.6 collective-permute-start.23
  475.4 2.0 collective-permute-done.20
  478.6 8.1 %collective-permute-done.21 = bf16[128,1024]{1,0:T(8,128)(2,1)S(1)} collective-permute-done((bf16[128,1024]{1,0:T(8,128)(2,1)}, bf16[128,1024]{1,0:T(8,128)(2,1)S(1)}, u32[]{:S(2)}, u32[]{:S(2)}) %collective-permute-start.21) | collective-permute-done | bytes 262176 | tf_op jit(solution)/shard_map/ppermute | solution.py:817
  487.7 10.3 %collective-permute-start.24 = (bf16[4,128,1024]{2,1,0:T(8,128)(2,1)S(1)}, bf16[4,128,1024]{2,1,0:T(8,128)(2,1)S(1)}, u32[]{:S(2)}, u32[]{:S(2)}) collective-permute-start(bf16[4,128,1024]{2,1,0:T(8,128)(2,1)S(1)} %broadcast_select_fusion.4), channel_id=1, source_target_pairs={{0,16},{16,0},{1,17},{17,1},{2,18},{18,2},{3,19},{19,3},{4,20},{20... | collective-permute-start | bytes 3145736 | tf_op jit(solution)/shard_map/ppermute | solution.py:855
  498.0 1.5 collective-permute-start.29
  499.6 2.8 collective-permute-done.29
  502.4 2.1 collective-permute-start.30
  507.1 3.5 copy.87
  (149 shorter events, 41.1 us)
Async XLA Ops:
  7.2 5.9 %copy-start.3 = (bf16[1,1024,512]{2,1,0:T(8,128)(2,1)S(1)}, bf16[1,1024,512]{2,1,0:T(8,128)(2,1)}, u32[]{:S(2)}) copy-start(bf16[1,1024,512]{2,1,0:T(8,128)(2,1)} %param.21) | copy-start | bytes 3145732
  7.2 201.9 %all-gather.5.cloned.1.call-start = ((), (), s32[]{:S(2)}) async-start(), calls=%async_computation | async-start | bytes 34537472 | tf_op jit(solution)/shard_map/all_gather | solution.py:678
  13.0 2.7 copy-start.6
  15.7 1.5 copy-start.4
  17.3 2.2 copy-start
  18.7 3.9 collective-permute-start.1
  26.4 288.1 %all-gather.7.cloned.1.call-start = ((), (), s32[]{:S(2)}) async-start(), calls=%async_computation.1 | async-start | bytes 20054016 | tf_op jit(solution)/shard_map/all_gather | solution.py:678
  30.7 3.0 collective-permute-start
  36.2 15.8 %collective-permute-start.4 = (bf16[128,1024]{1,0:T(8,128)(2,1)}, bf16[128,1024]{1,0:T(8,128)(2,1)}, u32[]{:S(2)}, u32[]{:S(2)}) collective-permute-start(bf16[128,1024]{1,0:T(8,128)(2,1)} %get-tuple-element.139), channel_id=1, source_target_pairs={{0,1},{1,0},{2,3},{3,2},{4,17},{5,16},{6,19},{7,18},{16,5},{17,4},... | collective-permute-start | bytes 786440 | tf_op jit(solution)/shard_map/ppermute | solution.py:635
  39.6 12.4 %collective-permute-start.5 = (bf16[128,1024]{1,0:T(8,128)(2,1)S(1)}, bf16[128,1024]{1,0:T(8,128)(2,1)}, u32[]{:S(2)}, u32[]{:S(2)}) collective-permute-start(bf16[128,1024]{1,0:T(8,128)(2,1)S(1)} %get-tuple-element.140), channel_id=1, source_target_pairs={{0,0},{1,1},{2,2},{3,3},{4,16},{5,17},{6,18},{7,19},{16,4},{17,5},... | collective-permute-start | bytes 786440 | tf_op jit(solution)/shard_map/ppermute | solution.py:635
  41.5 14.9 %collective-permute-start.3 = (bf16[128,1024]{1,0:T(8,128)(2,1)S(1)}, bf16[128,1024]{1,0:T(8,128)(2,1)}, u32[]{:S(2)}, u32[]{:S(2)}) collective-permute-start(bf16[128,1024]{1,0:T(8,128)(2,1)S(1)} %get-tuple-element.141), channel_id=1, source_target_pairs={{0,2},{1,3},{2,0},{3,1},{4,18},{5,19},{6,16},{7,17},{16,6},{17,7},... | collective-permute-start | bytes 786440 | tf_op jit(solution)/shard_map/ppermute | solution.py:635
  43.2 23.8 %collective-permute-start.2 = (bf16[128,1024]{1,0:T(8,128)(2,1)S(1)}, bf16[128,1024]{1,0:T(8,128)(2,1)}, u32[]{:S(2)}, u32[]{:S(2)}) collective-permute-start(bf16[128,1024]{1,0:T(8,128)(2,1)S(1)} %get-tuple-element.142), channel_id=1, source_target_pairs={{0,3},{1,2},{2,1},{3,0},{4,19},{5,18},{6,17},{7,16},{16,7},{17,6},... | collective-permute-start | bytes 786440 | tf_op jit(solution)/shard_map/ppermute | solution.py:635
  211.5 8.5 %copy-start.8 = (bf16[1,2,1024]{2,1,0:T(2,128)(2,1)S(1)}, bf16[1,2,1024]{2,1,0:T(2,128)(2,1)}, u32[]{:S(2)}) copy-start(bf16[1,2,1024]{2,1,0:T(2,128)(2,1)} %param.20) | copy-start | bytes 12292
  211.5 8.5 %copy-start.9 = (bf16[1,2,1024]{2,1,0:T(2,128)(2,1)S(1)}, bf16[1,2,1024]{2,1,0:T(2,128)(2,1)}, u32[]{:S(2)}) copy-start(bf16[1,2,1024]{2,1,0:T(2,128)(2,1)} %param.19) | copy-start | bytes 12292
  211.5 8.5 %copy-start.10 = (bf16[1,2,1024]{2,1,0:T(2,128)(2,1)S(1)}, bf16[1,2,1024]{2,1,0:T(2,128)(2,1)}, u32[]{:S(2)}) copy-start(bf16[1,2,1024]{2,1,0:T(2,128)(2,1)} %param.18) | copy-start | bytes 12292
  211.5 8.9 %copy-start.7 = (s32[4,2,1024]{2,1,0:T(2,128)S(1)}, s32[4,2,1024]{2,1,0:T(2,128)}, u32[]{:S(2)}) copy-start(s32[4,2,1024]{2,1,0:T(2,128)} %param.14) | copy-start | bytes 98308
  219.7 8.7 %collective-permute-start.11 = (bf16[2,8,512,128]{3,2,1,0:T(8,128)(2,1)}, bf16[2,8,512,128]{3,2,1,0:T(8,128)(2,1)}, u32[]{:S(2)}, u32[]{:S(2)}) collective-permute-start(bf16[2,8,512,128]{3,2,1,0:T(8,128)(2,1)} %get-tuple-element.56.own_ref), channel_id=1, source_target_pairs={{0,16},{16,0},{1,17},{17,1},{2,18},{18,2},{3,19},{19,3},{4,20},{20... | collective-permute-start | bytes 6291464 | tf_op jit(solution)/shard_map/ppermute | solution.py:770
  220.1 3.9 collective-permute-start.10
  220.5 7.9 %copy-start.11 = (s32[1,512]{1,0:T(1,128)}, s32[1,512]{1,0:T(1,128)S(1)}, u32[]{:S(2)}) copy-start(s32[1,512]{1,0:T(1,128)S(1)} %get-tuple-element.154.sq_ref) | copy-start | bytes 6148
  283.3 4.6 collective-permute-start.12
  314.5 30.9 %collective-permute-start.8 = (bf16[128,1024]{1,0:T(8,128)(2,1)S(1)}, bf16[128,1024]{1,0:T(8,128)(2,1)S(1)}, u32[]{:S(2)}, u32[]{:S(2)}) collective-permute-start(bf16[128,1024]{1,0:T(8,128)(2,1)S(1)} %get-tuple-element.131), channel_id=1, source_target_pairs={{0,1},{1,0},{2,3},{3,2},{4,17},{5,16},{6,19},{7,18},{16,5},{17,4},... | collective-permute-start | bytes 786440 | tf_op jit(solution)/shard_map/ppermute | solution.py:635
  315.8 30.8 %collective-permute-start.9 = (bf16[128,1024]{1,0:T(8,128)(2,1)S(1)}, bf16[128,1024]{1,0:T(8,128)(2,1)S(1)}, u32[]{:S(2)}, u32[]{:S(2)}) collective-permute-start(bf16[128,1024]{1,0:T(8,128)(2,1)S(1)} %get-tuple-element.132), channel_id=1, source_target_pairs={{0,0},{1,1},{2,2},{3,3},{4,16},{5,17},{6,18},{7,19},{16,4},{17,5},... | collective-permute-start | bytes 786440 | tf_op jit(solution)/shard_map/ppermute | solution.py:635
  316.7 31.9 %collective-permute-start.7 = (bf16[128,1024]{1,0:T(8,128)(2,1)S(1)}, bf16[128,1024]{1,0:T(8,128)(2,1)S(1)}, u32[]{:S(2)}, u32[]{:S(2)}) collective-permute-start(bf16[128,1024]{1,0:T(8,128)(2,1)S(1)} %get-tuple-element.133), channel_id=1, source_target_pairs={{0,2},{1,3},{2,0},{3,1},{4,18},{5,19},{6,16},{7,17},{16,6},{17,7},... | collective-permute-start | bytes 786440 | tf_op jit(solution)/shard_map/ppermute | solution.py:635
  318.8 30.2 %collective-permute-start.6 = (bf16[128,1024]{1,0:T(8,128)(2,1)S(1)}, bf16[128,1024]{1,0:T(8,128)(2,1)S(1)}, u32[]{:S(2)}, u32[]{:S(2)}) collective-permute-start(bf16[128,1024]{1,0:T(8,128)(2,1)S(1)} %get-tuple-element.134), channel_id=1, source_target_pairs={{0,3},{1,2},{2,1},{3,0},{4,19},{5,18},{6,17},{7,16},{16,7},{17,6},... | collective-permute-start | bytes 786440 | tf_op jit(solution)/shard_map/ppermute | solution.py:635
  343.4 46.9 %collective-permute-start.13 = (bf16[128,1024]{1,0:T(8,128)(2,1)}, bf16[128,1024]{1,0:T(8,128)(2,1)S(1)}, u32[]{:S(2)}, u32[]{:S(2)}) collective-permute-start(bf16[128,1024]{1,0:T(8,128)(2,1)} %get-tuple-element.74), channel_id=1, source_target_pairs={{0,0},{1,1},{2,2},{3,3},{4,16},{5,17},{6,18},{7,19},{16,4},{17,5},... | collective-permute-start | bytes 786440 | tf_op jit(solution)/shard_map/ppermute | solution.py:817
  345.4 44.9 %collective-permute-start.14 = (bf16[128,1024]{1,0:T(8,128)(2,1)}, bf16[128,1024]{1,0:T(8,128)(2,1)S(1)}, u32[]{:S(2)}, u32[]{:S(2)}) collective-permute-start(bf16[128,1024]{1,0:T(8,128)(2,1)} %get-tuple-element.75), channel_id=1, source_target_pairs={{0,1},{1,0},{2,3},{3,2},{4,17},{5,16},{6,19},{7,18},{16,5},{17,4},... | collective-permute-start | bytes 786440 | tf_op jit(solution)/shard_map/ppermute | solution.py:817
  346.6 43.8 %collective-permute-start.15 = (bf16[128,1024]{1,0:T(8,128)(2,1)}, bf16[128,1024]{1,0:T(8,128)(2,1)S(1)}, u32[]{:S(2)}, u32[]{:S(2)}) collective-permute-start(bf16[128,1024]{1,0:T(8,128)(2,1)} %get-tuple-element.76), channel_id=1, source_target_pairs={{0,2},{1,3},{2,0},{3,1},{4,18},{5,19},{6,16},{7,17},{16,6},{17,7},... | collective-permute-start | bytes 786440 | tf_op jit(solution)/shard_map/ppermute | solution.py:817
  348.6 41.8 %collective-permute-start.16 = (bf16[128,1024]{1,0:T(8,128)(2,1)}, bf16[128,1024]{1,0:T(8,128)(2,1)S(1)}, u32[]{:S(2)}, u32[]{:S(2)}) collective-permute-start(bf16[128,1024]{1,0:T(8,128)(2,1)} %get-tuple-element.77), channel_id=1, source_target_pairs={{0,3},{1,2},{2,1},{3,0},{4,19},{5,18},{6,17},{7,16},{16,7},{17,6},... | collective-permute-start | bytes 786440 | tf_op jit(solution)/shard_map/ppermute | solution.py:817
  390.4 12.8 %collective-permute-start.17 = (bf16[2,8,512,128]{3,2,1,0:T(8,128)(2,1)}, bf16[2,8,512,128]{3,2,1,0:T(8,128)(2,1)S(1)}, u32[]{:S(2)}, u32[]{:S(2)}) collective-permute-start(bf16[2,8,512,128]{3,2,1,0:T(8,128)(2,1)} %bitcast.164), channel_id=1, source_target_pairs={{0,16},{16,0},{1,17},{17,1},{2,18},{18,2},{3,19},{19,3},{4,20},{20... | collective-permute-start | bytes 6291464 | tf_op jit(solution)/shard_map/ppermute | solution.py:770
  403.2 1.3 copy-start.2
  429.4 22.3 %copy-start.5 = (f32[8,64,128]{2,1,0:T(8,128)S(1)}, f32[8,64,128]{2,1,0:T(8,128)}, u32[]{:S(2)}) copy-start(f32[8,64,128]{2,1,0:T(8,128)} %get-tuple-element.92) | copy-start | bytes 786436
  451.3 5.6 %collective-permute-start.18 = (bf16[2,8,512,128]{3,2,1,0:T(8,128)(2,1)}, bf16[2,8,512,128]{3,2,1,0:T(8,128)(2,1)S(1)}, u32[]{:S(2)}, u32[]{:S(2)}) collective-permute-start(bf16[2,8,512,128]{3,2,1,0:T(8,128)(2,1)} %bitcast.165), channel_id=1, source_target_pairs={{0,16},{16,0},{1,17},{17,1},{2,18},{18,2},{3,19},{19,3},{4,20},{20... | collective-permute-start | bytes 6291464 | tf_op jit(solution)/shard_map/ppermute | solution.py:770
  452.8 3.2 collective-permute-start.19
  457.0 1.3 copy-start.1
  468.8 8.6 %collective-permute-start.20 = (bf16[128,1024]{1,0:T(8,128)(2,1)}, bf16[128,1024]{1,0:T(8,128)(2,1)S(1)}, u32[]{:S(2)}, u32[]{:S(2)}) collective-permute-start(bf16[128,1024]{1,0:T(8,128)(2,1)} %get-tuple-element.94), channel_id=1, source_target_pairs={{0,3},{1,2},{2,1},{3,0},{4,19},{5,18},{6,17},{7,16},{16,7},{17,6},... | collective-permute-start | bytes 786440 | tf_op jit(solution)/shard_map/ppermute | solution.py:817
  468.9 17.8 %collective-permute-start.21 = (bf16[128,1024]{1,0:T(8,128)(2,1)}, bf16[128,1024]{1,0:T(8,128)(2,1)S(1)}, u32[]{:S(2)}, u32[]{:S(2)}) collective-permute-start(bf16[128,1024]{1,0:T(8,128)(2,1)} %get-tuple-element.95), channel_id=1, source_target_pairs={{0,2},{1,3},{2,0},{3,1},{4,18},{5,19},{6,16},{7,17},{16,6},{17,7},... | collective-permute-start | bytes 786440 | tf_op jit(solution)/shard_map/ppermute | solution.py:817
  471.6 15.1 %collective-permute-start.22 = (bf16[128,1024]{1,0:T(8,128)(2,1)}, bf16[128,1024]{1,0:T(8,128)(2,1)S(1)}, u32[]{:S(2)}, u32[]{:S(2)}) collective-permute-start(bf16[128,1024]{1,0:T(8,128)(2,1)} %get-tuple-element.96), channel_id=1, source_target_pairs={{0,1},{1,0},{2,3},{3,2},{4,17},{5,16},{6,19},{7,18},{16,5},{17,4},... | collective-permute-start | bytes 786440 | tf_op jit(solution)/shard_map/ppermute | solution.py:817
  472.4 15.0 %collective-permute-start.23 = (bf16[128,1024]{1,0:T(8,128)(2,1)}, bf16[128,1024]{1,0:T(8,128)(2,1)S(1)}, u32[]{:S(2)}, u32[]{:S(2)}) collective-permute-start(bf16[128,1024]{1,0:T(8,128)(2,1)} %get-tuple-element.97), channel_id=1, source_target_pairs={{0,0},{1,1},{2,2},{3,3},{4,16},{5,17},{6,18},{7,19},{16,4},{17,5},... | collective-permute-start | bytes 786440 | tf_op jit(solution)/shard_map/ppermute | solution.py:817
  474.1 23.9 %collective-permute-start.26 = (f32[2,64,128]{2,1,0:T(8,128)S(1)}, f32[2,64,128]{2,1,0:T(8,128)S(1)}, u32[]{:S(2)}, u32[]{:S(2)}) collective-permute-start(f32[2,64,128]{2,1,0:T(8,128)S(1)} %get-tuple-element.147), channel_id=1, source_target_pairs={{0,1},{1,0},{2,3},{3,2},{4,17},{5,16},{6,19},{7,18},{16,5},{17,4},... | collective-permute-start | bytes 196616 | tf_op jit(solution)/shard_map/ppermute | solution.py:817
  477.4 20.6 %collective-permute-start.28 = (f32[2,64,128]{2,1,0:T(8,128)S(1)}, f32[2,64,128]{2,1,0:T(8,128)S(1)}, u32[]{:S(2)}, u32[]{:S(2)}) collective-permute-start(f32[2,64,128]{2,1,0:T(8,128)S(1)} %get-tuple-element.148), channel_id=1, source_target_pairs={{0,3},{1,2},{2,1},{3,0},{4,19},{5,18},{6,17},{7,16},{16,7},{17,6},... | collective-permute-start | bytes 196616 | tf_op jit(solution)/shard_map/ppermute | solution.py:817
  486.7 11.3 %collective-permute-start.27 = (f32[2,64,128]{2,1,0:T(8,128)S(1)}, f32[2,64,128]{2,1,0:T(8,128)S(1)}, u32[]{:S(2)}, u32[]{:S(2)}) collective-permute-start(f32[2,64,128]{2,1,0:T(8,128)S(1)} %get-tuple-element.149), channel_id=1, source_target_pairs={{0,2},{1,3},{2,0},{3,1},{4,18},{5,19},{6,16},{7,17},{16,6},{17,7},... | collective-permute-start | bytes 196616 | tf_op jit(solution)/shard_map/ppermute | solution.py:817
  486.7 11.3 %collective-permute-start.25 = (f32[2,64,128]{2,1,0:T(8,128)S(1)}, f32[2,64,128]{2,1,0:T(8,128)S(1)}, u32[]{:S(2)}, u32[]{:S(2)}) collective-permute-start(f32[2,64,128]{2,1,0:T(8,128)S(1)} %get-tuple-element.150), channel_id=1, source_target_pairs={{0,0},{1,1},{2,2},{3,3},{4,16},{5,17},{6,18},{7,19},{16,4},{17,5},... | collective-permute-start | bytes 196616 | tf_op jit(solution)/shard_map/ppermute | solution.py:817
  487.7 18.8 %collective-permute-start.24 = (bf16[4,128,1024]{2,1,0:T(8,128)(2,1)S(1)}, bf16[4,128,1024]{2,1,0:T(8,128)(2,1)S(1)}, u32[]{:S(2)}, u32[]{:S(2)}) collective-permute-start(bf16[4,128,1024]{2,1,0:T(8,128)(2,1)S(1)} %broadcast_select_fusion.4), channel_id=1, source_target_pairs={{0,16},{16,0},{1,17},{17,1},{2,18},{18,2},{3,19},{19,3},{4,20},{20... | collective-permute-start | bytes 3145736 | tf_op jit(solution)/shard_map/ppermute | solution.py:855
  498.0 4.3 collective-permute-start.29
  502.4 2.9 collective-permute-start.30
Sparse Core Ops, SparseCore 0:
  26.5 182.5 all-gather.4
  210.7 103.6 all-gather.6

commit v3 on v2

--- a/solution.py
+++ b/solution.py
@@ -12,7 +12,7 @@
 PAIR = 2 * HEAD
 EPSILON = 1e-05
 MASKED = -1000000000.0
-VMEM = 56 * 1024 * 1024
+VMEM = 60 * 1024 * 1024
 SECTIONS = 2
 
 bf16 = jnp.bfloat16
@@ -93,6 +93,35 @@
 
 def struct(shape, dtype):
     return jax.ShapeDtypeStruct(shape, dtype)
+
+
+def pack_kernel(p_ref, o_ref, u_ref, d_ref, s_ref, section_ref, keep_ref, give_ref, stage, semaphores):
+    copies = Copies(semaphores)
+    place = 0
+    sources = [(p_ref[part].T, HEAD) for part in range(3)]
+    sources += [(o_ref[...], HEAD), (u_ref[...].T, u_ref.shape[1] // 2), (d_ref[...], d_ref.shape[0] // 2)]
+    for value, rows in sources:
+        for half in range(2):
+            stage[half, place : place + rows] = value[half * rows : (half + 1) * rows]
+        place += rows
+    for half in range(2):
+        stage[half, place:] = s_ref[half]
+    section = section_ref[0]
+    wait([copies.start(stage.at[1 - section], give_ref), copies.start(stage.at[section], keep_ref)])
+
+
+def pack(project_w, out_w, up_w, down_w, small, section):
+    width = down_w.shape[1]
+    rows = (project_w.shape[2] * 3 + out_w.shape[0] + up_w.shape[1] + down_w.shape[0]) // 2
+    rows += small.shape[1]
+    return call(
+        pack_kernel,
+        [IN_VMEM] * 5 + [IN_SMEM],
+        [IN_HBM] * 2,
+        [struct((rows, width), bf16)] * 2,
+        scratch=[pltpu.VMEM((2, rows, width), bf16), pltpu.SemaphoreType.DMA((2,))],
+        moved=8 * rows * width,
+    )(project_w, out_w, up_w, down_w, small, section)
 
 
 def load_heads(copies, ref, first, parts, pairs, target):
@@ -111,6 +140,30 @@
     return started
 
 
+def load_projection(copies, refs, first, pairs, target, place_ref):
+    if len(refs) == 1:
+        return load_heads(copies, refs[0], first, 3, pairs, target)
+    started = []
+    unit_rows = HEAD // 2
+    for index, ref in enumerate(refs):
+        plane = place_ref[0] if index == 0 else 1 - place_ref[0]
+        for half in range(2 if index == 0 else 1):
+            here = (half, place_ref[1], 1 - place_ref[1])[index]
+            for pair in range(pairs):
+                for unit_index in range(3):
+                    place = 3 * plane + unit_index
+                    row = (place // 2) * pairs * PAIR + (place % 2) * unit_rows
+                    row = pl.multiple_of(row + pair * PAIR + here * HEAD, unit_rows)
+                    cut = pl.ds((first if index == 0 else 0) + unit_index * unit_rows, unit_rows)
+                    started.append(
+                        copies.start(
+                            ref.at[half, pair, cut] if index == 0 else ref.at[pair, cut],
+                            target.at[pl.ds(row, unit_rows)],
+                        )
+                    )
+    return [started, [], []]
+
+
 class Hidden:
     def __init__(self, copies, refs, pieces, up, down):
         self.copies, self.refs, self.pieces = copies, refs, pieces
@@ -139,11 +192,12 @@
             self.loads[kind].pop(0)[1].wait()
 
 
-def project_kernel(first, x_ref, w_ref, b_ref, q_ref, kv_ref, weight, stage, semaphores):
+def project_kernel(first, x_ref, b_ref, place_ref, *rest):
+    (*w_refs, q_ref, kv_ref, weight, stage, semaphores) = rest
     copies = Copies(semaphores)
     pairs = stage.shape[1]
     wide = pairs * PAIR
-    loads = load_heads(copies, w_ref, first, 3, pairs, weight)
+    loads = load_projection(copies, w_refs, first, pairs, weight, place_ref)
     stores = []
     for part in (0, 1, 2):
         wait(loads[part])
@@ -158,22 +212,23 @@
     wait(stores)
 
 
-def project(x, table, bias):
+def project(x, table, bias, place):
     count, width = x.shape
-    pairs = table[0].shape[1]
+    arrays, first = table
+    pairs = arrays[0].shape[1]
     return call(
-        functools.partial(project_kernel, table[1]),
-        [IN_VMEM, IN_HBM, IN_VMEM],
+        functools.partial(project_kernel, first),
+        [IN_VMEM, IN_VMEM, IN_SMEM] + [IN_HBM] * len(arrays),
         [IN_HBM, IN_HBM],
         [struct((pairs, count, PAIR), bf16), struct((2, pairs, count, PAIR), bf16)],
         scratch=[
             pltpu.VMEM((3 * pairs * PAIR, width), bf16),
             pltpu.VMEM((3, pairs, count, PAIR), bf16),
-            pltpu.SemaphoreType.DMA((6 * pairs + 3,)),
+            pltpu.SemaphoreType.DMA((12 * pairs + 3,)),
         ],
         flops=2 * count * width * 3 * PAIR * pairs,
         moved=2 * (count * width * 4 + 3 * width * PAIR * pairs),
-    )(x, table[0], bias)
+    )(x, bias, place, *arrays)
 
 
 def feed_forward(copies, places, x_ref, mixed_ref, ow_ref, h_refs, vec_ref, ub_ref,
@@ -183,38 +238,46 @@
     loads_o = load_heads(copies, ow_ref, o_first, 1, pairs, weight_o)[0]
     weights = Hidden(copies, h_refs, pieces, weight_u, weight_d)
     groups = weights.groups
-    weights.fetch(0)
+    weights.fetch(groups - 1)
     mixed = jnp.concatenate([mixed_ref[i] for i in range(pairs)], axis=1)
     wait(loads_o)
     attended = dot_nn(mixed, weight_o[...])
     z, r = unit(x_ref[...].astype(f32) + attended + vec_ref[0:1])
-    z1_ref[...] = z
+    z1_ref[...] = z.astype(bf16)
     r1_ref[...] = r
     out = z * vec_ref[2:3] + vec_ref[4:5]
     normed[...] = out
     low[...] = out.astype(bf16)
 
-    def before(group):
-        weights.fetch(min(group + 1, groups - 1))
-        weights.wait(group, 0)
+    halves = 2
+    rows = low.shape[0] // halves
+
+    def before(chunk):
+        group, half = divmod(chunk, halves)
+        if half == 0:
+            weights.fetch(min(group + 1, groups - 1))
+            weights.wait(group, 0)
         span = slice(group * GROUP, (group + 1) * GROUP)
-        return dot_nt(low[...], weight_u[span]) + ub_ref[:, span]
+        return dot_nt(low[half * rows : (half + 1) * rows], weight_u[span]) + ub_ref[:, span]
 
     later = before(0)
-    for group in range(groups):
+    for chunk in range(groups * halves):
+        group, half = divmod(chunk, halves)
         pre = later
-        if group + 1 < groups:
-            later = before(group + 1)
+        if chunk + 1 < groups * halves:
+            later = before(chunk + 1)
         span = slice(group * GROUP, (group + 1) * GROUP)
+        here = slice(half * rows, (half + 1) * rows)
         spread = 0.5 + 0.5 * lax.erf(pre * math.sqrt(0.5))
         bell = jnp.exp(-0.5 * pre * pre) * (1.0 / math.sqrt(2.0 * math.pi))
-        slope[:, span] = (spread + pre * bell).astype(bf16)
-        weights.wait(group, 1)
+        slope[here, span] = (spread + pre * bell).astype(bf16)
+        if half == 0:
+            weights.wait(group, 1)
         out = dot_nn((pre * spread).astype(bf16), weight_d[span])
         if group == 0:
-            acc[...] = out
+            acc[here] = out
         else:
-            acc[...] += out
+            acc[here] += out
     return unit(normed[...] + acc[...] + vec_ref[1:2])
 
 
@@ -222,16 +285,16 @@
     h_refs = rest[:sources]
     out_refs = rest[sources : sources + max(blocks, 1)]
     (z1_ref, r1_ref, z2_ref, r2_ref, slope_ref, weight_o, weight_u, weight_d,
-     z1, slope, normed, low, acc, semaphores) = rest[sources + max(blocks, 1) :]
+     z1, z2, slope, normed, low, acc, semaphores) = rest[sources + max(blocks, 1) :]
     copies = Copies(semaphores)
     z, r = feed_forward(
         copies, places, x_ref, mixed_ref, ow_ref, h_refs, vec_ref, ub_ref,
         z1, r1_ref, weight_o, weight_u, weight_d, slope, normed, low, acc,
     )
     stores = [copies.start(z1, z1_ref), copies.start(slope, slope_ref)]
-    acc[...] = z
+    z2[...] = z.astype(bf16)
     r2_ref[...] = r
-    stores.append(copies.start(acc, z2_ref))
+    stores.append(copies.start(z2, z2_ref))
     low[...] = (z * vec_ref[3:4] + vec_ref[5:6]).astype(bf16)
     rows = low.shape[0] // max(blocks, 1)
     for j in range(max(blocks, 1)):
@@ -245,7 +308,8 @@
         pltpu.VMEM((wide, width), bf16),
         pltpu.VMEM((hidden, width), bf16),
         pltpu.VMEM((hidden, width), bf16),
-        pltpu.VMEM((count, width), f32),
+        pltpu.VMEM((count, width), bf16),
+        pltpu.VMEM((count, width), bf16),
         pltpu.VMEM((count, hidden), bf16),
         pltpu.VMEM((count, width), f32),
         pltpu.VMEM((count, width), bf16),
@@ -263,7 +327,7 @@
 def feed(x, mixed, tables, vectors, up_bias, rank, blocks):
     o_table, (arrays, pieces) = tables
     count, width, pairs, wide, hidden = feed_sizes(x, mixed, up_bias)
-    square = struct((count, width), f32)
+    square = struct((count, width), bf16)
     column = struct((count, 1), f32)
     parts = max(blocks, 1)
     out, kept = [], []
@@ -281,148 +345,57 @@
     return (found[:blocks] if blocks else found[0], *found[parts:])
 
 
-def feed_back(weight_o, weight_u, weight_d, vec_ref, z1, r1, slope, low, acc,
-              first_ref, mixed_ref, before=lambda group: None, ready=lambda: None):
-    pairs = mixed_ref.shape[0]
-    low[...] = acc[...].astype(bf16)
-    for group in range(weight_u.shape[0] // GROUP):
-        before(group)
-        span = slice(group * GROUP, (group + 1) * GROUP)
-        d_act = dot_nt(low[...], weight_d[span])
-        d_pre = (d_act * slope[:, span].astype(f32)).astype(bf16)
-        acc[...] += dot_nn(d_pre, weight_u[span])
-    ready()
-    first = unit_back(acc[...], z1[...], r1[...], vec_ref[2:3])
-    first_ref[...] = first
-    d_mixed = dot_nt(first.astype(bf16), weight_o[...]).astype(bf16)
-    for pair in range(pairs):
-        mixed_ref[pair] = d_mixed[:, pair * PAIR : (pair + 1) * PAIR]
-
-
-def scatter_rows(stage, rank_ref, targets):
-    rows = targets[0].shape[0]
-    for j, target in enumerate(targets):
-        start = pl.multiple_of((rank_ref[0] ^ j) * rows, rows)
-        target[...] = stage[pl.ds(start, rows)]
+def summed(own, got, part):
+    columns = []
+    for pair in range(own.shape[1]):
+        column = own[part, pair].astype(f32)
+        for i in range(got.shape[0]):
+            column += got[i, part, pair].astype(f32)
+        columns.append(column.astype(bf16))
+    return jnp.concatenate(columns, axis=1)
 
 
 def project_back(first_ref, dq_ref, own_ref, got_ref, weight, loads):
     pairs = dq_ref.shape[0]
     wide = pairs * PAIR
-    total = first_ref[...]
+    total = first_ref[...].astype(f32)
     for part in range(3):
-        columns = []
-        for pair in range(pairs):
-            if part == 0:
-                columns.append(dq_ref[pair])
-            else:
-                column = own_ref[part - 1, pair].astype(f32)
-                for i in range(got_ref.shape[0]):
-                    column += got_ref[i, part - 1, pair].astype(f32)
-                columns.append(column.astype(bf16))
+        if part == 0:
+            left = jnp.concatenate([dq_ref[pair] for pair in range(pairs)], axis=1)
+        else:
+            left = summed(own_ref, got_ref, part - 1)
         wait(loads[part])
-        total += dot_nn(jnp.concatenate(columns, axis=1), weight[part * wide : (part + 1) * wide])
+        total += dot_nn(left, weight[part * wide : (part + 1) * wide])
     return total
 
 
-def link_kernel(p_first, places, sources, *rest):
-    if p_first is None:
-        grad_ref, *rest = rest
-    else:
-        first1_ref, dq_ref, own_ref, got_ref, pw_ref, *rest = rest
-    ow_ref, vec_ref, z1_ref, r1_ref, z2_ref, r2_ref, slope_ref, *rest = rest
-    h_refs = rest[:sources]
-    (first_ref, d_mixed_ref,
-     weight_o, weight_u, weight_d, z1, slope, low, acc, semaphores, *weight_p) = rest[sources:]
-    o_first, pieces = places
-    copies = Copies(semaphores)
-    pairs = d_mixed_ref.shape[0]
-    if p_first is not None:
-        loads_p = load_heads(copies, pw_ref, p_first, 3, pairs, weight_p[0])
-    weights = Hidden(copies, h_refs, pieces, weight_u, weight_d)
-    groups = weights.groups
-    slopes = []
-
-    def fetch(group):
-        weights.fetch(group)
-        span = (slice(None), pl.ds(group * GROUP, GROUP))
-        slopes.append(copies.start(slope_ref.at[span], slope.at[span]))
-
-    if p_first is None:
-        fetch(0)
-        grad = grad_ref[...].astype(f32)
-    else:
-        total = project_back(first1_ref, dq_ref, own_ref, got_ref, weight_p[0], loads_p)
-        fetch(0)
-        grad = total.astype(bf16).astype(f32)
-    acc[...] = unit_back(grad, z2_ref[...], r2_ref[...], vec_ref[3:4])
-    last = []
-
-    def before(group):
-        if group + 1 < groups:
-            fetch(group + 1)
-        else:
-            last.append(copies.start(z1_ref, z1))
-            last.extend(load_heads(copies, ow_ref, o_first, 1, pairs, weight_o)[0])
-        slopes[group].wait()
-        weights.wait(group, 0)
-        weights.wait(group, 1)
-
-    feed_back(
-        weight_o, weight_u, weight_d, vec_ref, z1, r1_ref, slope, low, acc, first_ref, d_mixed_ref,
-        before, lambda: wait(last),
-    )
-
-
-def link(grads, p_table, tables, vectors, kept):
-    o_table, (arrays, pieces) = tables
-    count, width = grads[0].shape
-    pairs = o_table[0].shape[1]
-    wide = pairs * PAIR
-    slope = kept[-1]
-    hidden = slope.shape[1]
-    more = [] if p_table is None else [p_table[0]]
-    return call(
-        functools.partial(
-            link_kernel, p_table and p_table[1], (o_table[1], pieces), len(arrays)
-        ),
-        [IN_VMEM] * len(grads) + [IN_HBM] * len(more)
-        + [IN_HBM, IN_VMEM, IN_HBM, IN_VMEM, IN_VMEM, IN_VMEM, IN_HBM]
-        + [IN_HBM] * len(arrays),
-        [IN_VMEM] * 2,
-        [struct((count, width), f32), struct((pairs, count, PAIR), bf16)],
-        scratch=[
-            pltpu.VMEM((wide, width), bf16),
-            pltpu.VMEM((hidden, width), bf16),
-            pltpu.VMEM((hidden, width), bf16),
-            pltpu.VMEM((count, width), f32),
-            pltpu.VMEM((count, hidden), bf16),
-            pltpu.VMEM((count, width), bf16),
-            pltpu.VMEM((count, width), f32),
-            pltpu.SemaphoreType.DMA((16 * pairs + 16,)),
-        ]
-        + [pltpu.VMEM((3 * wide, width), bf16)] * len(more),
-        flops=2 * count * width * (4 * wide + 2 * hidden),
-        moved=2 * (2 * hidden * width + 4 * wide * width + 16 * count * width),
-    )(*grads, *more, o_table[0], vectors, *kept, *arrays)
-
-
-def leave_kernel(p_first, first_ref, dq_ref, own_ref, got_ref, pw_ref, rank_ref, *rest):
+def leave_kernel(p_first, extra, first_ref, dq_ref, own_ref, got_ref, pw_ref, rank_ref, *rest):
+    if extra:
+        prefix_ref, *rest = rest
     (*out_refs, weight_p, low, semaphores) = rest
     copies = Copies(semaphores)
     loads = load_heads(copies, pw_ref, p_first, 3, dq_ref.shape[0], weight_p)
     low[...] = project_back(first_ref, dq_ref, own_ref, got_ref, weight_p, loads).astype(bf16)
-    scatter_rows(low, rank_ref, out_refs)
-
-
-def leave(first, dq, own, got, p_table, rank, blocks):
+    rows = low.shape[0] // len(out_refs)
+    for j, target in enumerate(out_refs):
+        start = pl.multiple_of((rank_ref[0] ^ j) * rows, rows)
+        target[:rows] = low[pl.ds(start, rows)]
+        if extra:
+            value = prefix_ref[rank_ref[0] ^ j].astype(bf16)
+            for column in range(value.shape[0] // 16):
+                span = slice(column * PAIR, (column + 1) * PAIR)
+                target[rows:, span] = value[column * 16 : (column + 1) * 16]
+
+
+def leave(first, dq, own, got, p_table, rank, blocks, prefix=None):
     count, width = first.shape
     pairs = dq.shape[0]
+    more = [] if prefix is None else [prefix]
     return call(
-        functools.partial(leave_kernel, p_table[1]),
-        [IN_VMEM] * 4 + [IN_HBM, IN_SMEM],
+        functools.partial(leave_kernel, p_table[1], len(more)),
+        [IN_VMEM] * 4 + [IN_HBM, IN_SMEM] + [IN_VMEM] * len(more),
         [IN_VMEM] * blocks,
-        [struct((count // blocks, width), bf16)] * blocks,
+        [struct((count // blocks + 16 * len(more), width), bf16)] * blocks,
         scratch=[
             pltpu.VMEM((3 * pairs * PAIR, width), bf16),
             pltpu.VMEM((count, width), bf16),
@@ -430,7 +403,7 @@
         ],
         flops=2 * count * width * 3 * PAIR * pairs,
         moved=2 * (count * width * 7 + 3 * width * PAIR * pairs),
-    )(first, dq, own, got, p_table[0], rank)
+    )(first, dq, own, got, p_table[0][0], rank, *more)
 
 
 def attend_kernel(
@@ -444,7 +417,7 @@
     def _():
         row = lax.broadcasted_iota(jnp.int32, (pad, bias_ref.shape[1]), 0)
         bias_ref[:pad] = jnp.where(row < prefix_count, 0.0, MASKED)
-        keys = sk_ref[...]
+        keys = jnp.broadcast_to(sk_ref[...], (8, sk_ref.shape[1])).T[:, :1]
         same = (keys == sq_ref[...]) & (keys >= 0)
         bias_ref[pad:] = jnp.where(same, 0.0, MASKED)
 
@@ -456,20 +429,29 @@
     )
     queries = q_ref[0]
     lane = lax.broadcasted_iota(jnp.int32, queries.shape, 1)
+    value_lane = lax.broadcasted_iota(jnp.int32, values.shape, 1)
     parts = []
     inverses = []
+    count = queries.shape[0]
+    score = lambda head: dot_nt(
+        keys, jnp.where((lane // HEAD) == head, queries, bf16(0))
+    ) + bias_ref[...]
+    ahead = score(0)
     for head in range(2):
-        chosen = (lane // HEAD) == head
-        scores = dot_nt(keys, jnp.where(chosen, queries, bf16(0))) + bias_ref[...]
+        scores = ahead
+        if head == 0:
+            ahead = score(1)
         raised = jnp.exp(scores - jnp.max(scores, axis=0, keepdims=True))
-        inverse = 1.0 / jnp.sum(raised, axis=0, keepdims=True)
         low = raised.astype(bf16)
         raised_ref[0, head] = low
-        out = dot_tn(values, low)[head * HEAD : (head + 1) * HEAD]
+        ones = jnp.where((value_lane // HEAD) == head, values, bf16(1))
+        out = dot_tn(ones, low)
+        inverse = 1.0 / out[(1 - head) * HEAD : (1 - head) * HEAD + 1]
+        out = out[head * HEAD : (head + 1) * HEAD]
         parts.append(out * inverse)
         inverses.append(jnp.broadcast_to(inverse, out.shape))
     mixed_ref[0] = jnp.concatenate(parts, axis=0).T.astype(bf16)
-    inverse_ref[0] = jnp.concatenate(inverses, axis=0).T
+    inverse_ref[0] = jnp.concatenate(inverses, axis=0).T.astype(bf16)
 
 
 def attend(q, own, other, pk, pv, prefix_count, seg_q, seg_k):
@@ -488,7 +470,7 @@
             by_prefix,
             by_prefix,
             whole((1, count)),
-            whole((total - pad, 1)),
+            whole((1, total - pad)),
         ],
         [
             by_pair,
@@ -498,7 +480,7 @@
         [
             struct((pairs, count, PAIR), bf16),
             struct((pairs, 2, total, count), bf16),
-            struct((pairs, count, PAIR), f32),
+            struct((pairs, count, PAIR), bf16),
         ],
         scratch=[pltpu.VMEM((total, count), f32)],
         grid=(pairs,),
@@ -508,23 +490,10 @@
     )(q, own, other, pk, pv, seg_q, seg_k)
 
 
-def attend_back_kernel(
-    grad_ref, mixed_ref, inverse_ref, raised_ref, q_ref, own_ref, other_ref, pk_ref, pv_ref,
-    dq_ref, down_ref, dother_ref, prefix_ref,
-):
-    pad = pk_ref.shape[1]
-    others = other_ref.shape[0]
-    count = q_ref.shape[1]
-    keys = jnp.concatenate(
-        [pk_ref[0], own_ref[0, 0]] + [other_ref[i, 0, 0] for i in range(others)], axis=0
-    )
-    values = jnp.concatenate(
-        [pv_ref[0], own_ref[1, 0]] + [other_ref[i, 1, 0] for i in range(others)], axis=0
-    )
-    queries = q_ref[0]
+def attention_back(d_out, mixed, inverse, raised, queries, keys, values):
     lane = lax.broadcasted_iota(jnp.int32, queries.shape, 1)
-    scaled = grad_ref[0].astype(f32) * inverse_ref[0]
-    products = (scaled * mixed_ref[0].astype(f32)).T
+    scaled = d_out.astype(f32) * inverse.astype(f32)
+    products = (scaled * mixed.astype(f32)).T
     scaled = scaled.astype(bf16)
     d_keys = jnp.zeros(keys.shape, f32)
     d_values = jnp.zeros(keys.shape, f32)
@@ -534,50 +503,217 @@
         span = slice(head * HEAD, (head + 1) * HEAD)
         delta = jnp.sum(products[span], axis=0, keepdims=True)
         here = jnp.where(chosen, scaled, bf16(0))
-        raised = raised_ref[0, head]
-        d_score = (raised.astype(f32) * (dot_nt(values, here) - delta)).astype(bf16)
-        d_values += dot_nn(raised, here)
+        low = raised(head)
+        d_score = (low.astype(f32) * (dot_nt(values, here) - delta)).astype(bf16)
+        d_values += dot_nn(low, here)
         d_keys += dot_nn(d_score, jnp.where(chosen, queries, bf16(0)))
         parts.append(dot_tn(keys, d_score)[span])
-    d_query = jnp.concatenate(parts, axis=0).T * (1.0 / math.sqrt(HEAD))
-    dq_ref[0] = d_query.astype(bf16)
-    prefix_ref[0, :pad] = d_keys[:pad]
-    prefix_ref[0, pad:] = d_values[:pad]
-    down_ref[0, 0] = d_keys[pad : pad + count].astype(bf16)
-    down_ref[1, 0] = d_values[pad : pad + count].astype(bf16)
-    for i in range(others):
-        span = slice(pad + (i + 1) * count, pad + (i + 2) * count)
-        dother_ref[i, 0, 0] = d_keys[span].astype(bf16)
-        dother_ref[i, 1, 0] = d_values[span].astype(bf16)
-
-
-def attend_back(grad, mixed, inverse, raised, q, own, other, pk, pv):
+    return jnp.concatenate(parts, axis=0).T * (1.0 / math.sqrt(HEAD)), d_keys, d_values
+
+
+def back_kernel(p_first, p_sources, o_first, pieces, sources, place_ref, *rest):
+    if p_first is None:
+        grad_ref, *rest = rest
+    else:
+        first1_ref, dq_in, own_in, got_in, *rest = rest
+        pw_refs, rest = rest[:p_sources], rest[p_sources:]
+    (ow_ref, vec_ref, z1_ref, r1_ref, z2_ref, r2_ref, slope_ref,
+     mixed_ref, inverse_ref, raised_ref, q_ref, own_ref, other_ref, pk_ref, pv_ref, *rest) = rest
+    h_refs, rest = rest[:sources], rest[sources:]
+    outs, rest = rest[:5], rest[5:]
+    (weight_o, weight_u, weight_d, unit_in, slope, low, acc, first, dq, down, dother, prefix,
+     mixed, inverse, raised, queries, own, other, semaphores, turns, stores, *weight_p) = rest
+    copies = Copies(semaphores)
+    pairs, count, _ = dq.shape
+    others = dother.shape[0]
+    pad = pk_ref.shape[1]
+    weights = Hidden(copies, h_refs, pieces, weight_u, weight_d)
+    groups = weights.groups
+    slopes = []
+
+    def fetch(group):
+        weights.fetch(group)
+        span = (slice(None), pl.ds(group * GROUP, GROUP))
+        slopes.append(copies.start(slope_ref.at[span], slope.at[span]))
+
+    if p_first is None:
+        load = copies.start(grad_ref, low)
+        load_z2 = copies.start(z2_ref, unit_in)
+        fetch(0)
+        load.wait()
+        grad = low[...].astype(f32)
+    else:
+        load_q = copies.start(dq_in, dq)
+        loads_p = load_projection(copies, pw_refs, p_first, pairs, weight_p[0], place_ref)
+        loads = [copies.start(own_in, down), copies.start(got_in, dother)]
+        load_first = copies.start(first1_ref, first)
+        load_z2 = copies.start(z2_ref, unit_in)
+        fetch(0)
+        wide = pairs * PAIR
+        load_q.wait()
+        wait(loads_p[0])
+        left = jnp.concatenate([dq[pair] for pair in range(pairs)], axis=1)
+        total = dot_nn(left, weight_p[0][:wide])
+        wait(loads)
+        for part in (1, 2):
+            wait(loads_p[part])
+            total += dot_nn(
+                summed(down, dother, part - 1), weight_p[0][part * wide : (part + 1) * wide]
+            )
+        load_first.wait()
+        grad = (total + first[...].astype(f32)).astype(bf16).astype(f32)
+    load_z2.wait()
+    acc[...] = unit_back(grad, unit_in[...].astype(f32), r2_ref[...], vec_ref[3:4])
+    low[...] = acc[...].astype(bf16)
+    load_z1 = copies.start(z1_ref, unit_in)
+    loads_o = load_heads(copies, ow_ref, o_first, 1, pairs, weight_o)[0]
+
+    def turn(pair, slot):
+        moves = (
+            (raised_ref.at[pair], raised.at[slot]),
+            (q_ref.at[pair], queries.at[slot]),
+            (mixed_ref.at[pair], mixed.at[slot]),
+            (inverse_ref.at[pair], inverse.at[slot]),
+            (own_ref.at[:, pair], own.at[slot]),
+            (other_ref.at[:, :, pair], other.at[slot]),
+        )
+        return [
+            pltpu.make_async_copy(source, target, turns.at[slot, i])
+            for i, (source, target) in enumerate(moves)
+        ]
+
+    for group in range(groups):
+        if group + 1 < groups:
+            fetch(group + 1)
+        if group == groups - 1:
+            for pair in range(2):
+                for copy in turn(pair, pair):
+                    copy.start()
+        slopes[group].wait()
+        weights.wait(group, 0)
+        weights.wait(group, 1)
+        span = slice(group * GROUP, (group + 1) * GROUP)
+        d_act = dot_nt(low[...], weight_d[span])
+        d_pre = (d_act * slope[:, span].astype(f32)).astype(bf16)
+        acc[...] += dot_nn(d_pre, weight_u[span])
+    load_z1.wait()
+    d_first = unit_back(acc[...], unit_in[...].astype(f32), r1_ref[...], vec_ref[2:3])
+    first[...] = d_first.astype(bf16)
+    store_first = copies.start(first, outs[0])
+    wait(loads_o)
+    low[...] = dot_nt(d_first.astype(bf16), weight_o[...]).astype(bf16)
+
+    def save(pair):
+        moves = (
+            (dq.at[pair], outs[1].at[pair]),
+            (down.at[:, pair], outs[2].at[:, pair]),
+            (dother.at[:, :, pair], outs[3].at[:, :, pair]),
+            (prefix.at[pair], outs[4].at[pair]),
+        )
+        return [
+            pltpu.make_async_copy(source, target, stores.at[pair, i])
+            for i, (source, target) in enumerate(moves)
+        ]
+
+    def step(pair, carry):
+        slot = lax.rem(pair, 2)
+        for copy in turn(pair, slot):
+            copy.wait()
+        keys = jnp.concatenate(
+            [pk_ref[pair], own[slot, 0]] + [other[slot, i, 0] for i in range(others)], axis=0
+        )
+        values = jnp.concatenate(
+            [pv_ref[pair], own[slot, 1]] + [other[slot, i, 1] for i in range(others)], axis=0
+        )
+        d_query, d_keys, d_values = attention_back(
+            low[:, pl.ds(pl.multiple_of(pair * PAIR, PAIR), PAIR)],
+            mixed[slot],
+            inverse[slot],
+            lambda head: raised[slot, head],
+            queries[slot],
+            keys,
+            values,
+        )
+        dq[pair] = d_query.astype(bf16)
+        prefix[pair, :pad] = d_keys[:pad]
+        prefix[pair, pad:] = d_values[:pad]
+        for part, d_part in enumerate((d_keys, d_values)):
+            down[part, pair] = d_part[pad : pad + count].astype(bf16)
+            for i in range(others):
+                start = pad + (i + 1) * count
+                dother[i, part, pair] = d_part[start : start + count].astype(bf16)
+        for copy in save(pair):
+            copy.start()
+
+        @pl.when(pair + 2 < pairs)
+        def _():
+            for copy in turn(pair + 2, slot):
+                copy.start()
+
+        return carry
+
+    lax.fori_loop(0, pairs, step, 0)
+    store_first.wait()
+    for pair in range(pairs):
+        for copy in save(pair):
+            copy.wait()
+
+
+def backward(grads, p_table, tables, vectors, kept, attention, place):
+    o_table, (arrays, pieces) = tables
+    mixed, inverse, raised, q, own, other, pk, pv = attention
     pairs, count, _ = q.shape
-    others = other.shape[0]
+    width = o_table[0].shape[-1]
+    wide = pairs * PAIR
+    total = raised.shape[2]
     pad = pk.shape[1]
-    total = pad + count * (others + 1)
-    by_pair = pl.BlockSpec((1, count, PAIR), lambda i: (i, 0, 0))
-    by_prefix = pl.BlockSpec((1, pad, PAIR), lambda i: (i, 0, 0))
-    by_own = pl.BlockSpec((2, 1, count, PAIR), lambda i: (0, i, 0, 0))
-    by_other = pl.BlockSpec((others, 2, 1, count, PAIR), lambda i: (0, 0, i, 0, 0))
+    slope = kept[-1]
+    hidden = slope.shape[1]
+    more, p_first = ([], None) if p_table is None else p_table
+    vm = pltpu.VMEM
     return call(
-        attend_back_kernel,
+        functools.partial(
+            back_kernel, p_first, len(more), o_table[1], pieces, len(arrays)
+        ),
+        [IN_SMEM] + [IN_HBM] * (len(grads) + len(more))
+        + [IN_HBM, IN_VMEM, IN_HBM, IN_VMEM, IN_HBM, IN_VMEM, IN_HBM]
+        + [IN_HBM] * 6 + [IN_VMEM] * 2
+        + [IN_HBM] * len(arrays),
+        [IN_HBM] * 5,
         [
-            by_pair, by_pair, by_pair,
-            pl.BlockSpec((1, 2, total, count), lambda i: (i, 0, 0, 0)),
-            by_pair, by_own, by_other, by_prefix, by_prefix,
-        ],
-        [by_pair, by_own, by_other, pl.BlockSpec((1, 2 * pad, PAIR), lambda i: (i, 0, 0))],
-        [
+            struct((count, width), bf16),
             struct(q.shape, bf16),
             struct(own.shape, bf16),
             struct(other.shape, bf16),
             struct((pairs, 2 * pad, PAIR), f32),
         ],
-        grid=(pairs,),
-        flops=16 * total * count * PAIR * pairs,
-        moved=4 * pairs * total * count,
-    )(grad, mixed, inverse, raised, q, own, other, pk, pv)
+        scratch=[
+            vm((wide, width), bf16),
+            vm((hidden, width), bf16),
+            vm((hidden, width), bf16),
+            vm((count, width), bf16),
+            vm((count, hidden), bf16),
+            vm((count, width), bf16),
+            vm((count, width), f32),
+            vm((count, width), bf16),
+            vm(q.shape, bf16),
+            vm(own.shape, bf16),
+            vm(other.shape, bf16),
+            vm((pairs, 2 * pad, PAIR), f32),
+            vm((2, count, PAIR), bf16),
+            vm((2, count, PAIR), bf16),
+            vm((2, 2, total, count), bf16),
+            vm((2, count, PAIR), bf16),
+            vm((2, 2, count, PAIR), bf16),
+            vm((2, other.shape[0], 2, count, PAIR), bf16),
+            pltpu.SemaphoreType.DMA((22 * pairs + 16,)),
+            pltpu.SemaphoreType.DMA((2, 6)),
+            pltpu.SemaphoreType.DMA((pairs, 4)),
+        ]
+        + [vm((3 * wide, width), bf16)] * (p_table is not None),
+        flops=2 * count * width * (4 * wide + 2 * hidden) + 16 * total * count * PAIR * pairs,
+        moved=2 * (2 * hidden * width + 4 * wide * width + 16 * count * width) + 4 * pairs * total * count,
+    )(place, *grads, *more, o_table[0], vectors, *kept, *attention, *arrays)
 
 
 def per_device(
@@ -613,9 +749,11 @@
     by_row = jnp.transpose(boundary[0], (0, 2, 1, 3)).reshape(row_count, slots, width)
 
     def ordered(parts):
-        for bit in (1, 2):
-            flip = (low_rank & bit) != 0
+        bit = 1
+        while bit < len(parts):
+            flip = (rank & bit) != 0
             parts = [jnp.where(flip, parts[i ^ bit], part) for i, part in enumerate(parts)]
+            bit *= 2
         return parts
 
     if quick:
@@ -647,6 +785,27 @@
         got = lax.ppermute(theirs, "section", swap)
         tokens = jnp.where(is_first, mine, got)
         cotangent = jnp.where(is_first, got, mine)
+
+    own_vectors = jnp.concatenate(
+        [output_biases[0], norm_gains[0], norm_shifts[0], norm_shifts[0]], axis=0
+    )
+    got_vectors = lax.ppermute(own_vectors, "section", swap)
+    vectors = [
+        jnp.where(is_first, own_vectors, got_vectors).astype(f32),
+        jnp.where(is_first, got_vectors, own_vectors).astype(f32),
+    ]
+
+    segments = lax.dynamic_index_in_dim(
+        segment_ids.reshape(row_count, length), rank // chips, 0, keepdims=False
+    )
+    seg_q = lax.dynamic_slice_in_dim(segments, block * count, count, 0)
+    seg_k = jnp.concatenate(
+        [
+            lax.dynamic_slice_in_dim(segments, (block ^ distance) * count, count, 0)
+            for distance in range(blocks)
+        ]
+    )[None, :]
+    seg_q = seg_q[None, :]
 
     project_rows = jnp.transpose(project_weight[0], (1, 2, 0)).reshape(3, 2, low_width, width)
     project_rows = jnp.transpose(project_rows, (1, 0, 2, 3)).reshape(2, 3 * low_width, width)
@@ -665,11 +824,16 @@
     small_size = small.shape[1]
     small_rows = -(-small_size // (16 * width)) * 16
     small = jnp.pad(small, ((0, 0), (0, small_rows * width - small_size)))
-    packed = jnp.concatenate(
-        [project_rows, out_rows, up_rows, down_rows, small.reshape(2, small_rows, width)], axis=1
-    )
-    keep = lax.dynamic_index_in_dim(packed, section, 0, keepdims=False)
-    give = lax.dynamic_index_in_dim(packed, 1 - section, 0, keepdims=False)
+    small = small.reshape(2, small_rows, width)
+    if quick:
+        keep, give = pack(
+            jnp.transpose(project_weight[0], (1, 0, 2)), output_weight[0], up_weight[0],
+            down_weight[0], small, section.astype(jnp.int32).reshape(1),
+        )
+    else:
+        packed = jnp.concatenate([project_rows, out_rows, up_rows, down_rows, small], axis=1)
+        keep = lax.dynamic_index_in_dim(packed, section, 0, keepdims=False)
+        give = lax.dynamic_index_in_dim(packed, 1 - section, 0, keepdims=False)
     got = lax.ppermute(give, "section", swap)
     layer_rows = [jnp.where(is_first, keep, got), jnp.where(is_first, got, keep)]
     sizes = [3 * low_width, low_width, hidden, hidden, small_rows]
@@ -702,12 +866,20 @@
 
     tables = []
     smalls = []
-    early_rows = [
-        layer_rows[0][:d_end], layer_rows[1][:p_end], layer_rows[0][d_end:], layer_rows[1][d_end:],
-    ]
+    plane = lax.axis_index("dp")
+    share = 3 * low_width // 2
+    if quick:
+        projection = lax.dynamic_slice_in_dim(layer_rows[1][:p_end], plane * share, share, 0)
+    else:
+        projection = layer_rows[1][:p_end]
+    early_rows = [layer_rows[0][:d_end], projection, layer_rows[0][d_end:], layer_rows[1][d_end:]]
+    projection_rows = projection.shape[0]
     late_rows = layer_rows[1][p_end:d_end]
     early = gather(early_rows)
-    late = gather([after(late_rows, early, tokens)])
+    early, vectors[0], vectors[1], seg_q, seg_k, tokens = lax.optimization_barrier(
+        (early, vectors[0], vectors[1], seg_q, seg_k, tokens)
+    )
+    late = gather([after(late_rows, early)])
     def table(array, first, size, groups=1):
         if shards == 1:
             return (array, first, size)
@@ -716,6 +888,12 @@
         )
         part = jnp.transpose(part, (2, 1, 3, 0, 4, 5))
         return (part.reshape(2, pairs, 2 * size, width), 0, 2 * size)
+
+    def projection_table(layer):
+        if quick and layer:
+            return None
+        array, first, _ = table(early, layer * d_end, 3 * low_width, 3)
+        return (array,), first
 
     for layer in range(2):
         source, shift = (late, -p_end) if layer else (early, 0)
@@ -728,25 +906,16 @@
         )
         tables.append(
             (
-                table(early, layer * d_end, 3 * low_width, 3),
+                projection_table(layer),
                 table(source, shift + p_end, low_width),
                 ((up,), pieces),
             )
         )
-        start = d_end + p_end + layer * small_rows
+        start = d_end + projection_rows + layer * small_rows
         p_bias, u_bias, pk, pv = unpack(
             early[:, :, start : start + small_rows].reshape(2, ranks, -1)
         )
         smalls.append((p_bias, u_bias.reshape(1, -1).astype(f32), pk, pv))
-
-    own_vectors = jnp.concatenate(
-        [output_biases[0], norm_gains[0], norm_shifts[0], norm_shifts[0]], axis=0
-    )
-    got_vectors = lax.ppermute(own_vectors, "section", swap)
-    vectors = [
-        jnp.where(is_first, own_vectors, got_vectors).astype(f32),
-        jnp.where(is_first, got_vectors, own_vectors).astype(f32),
-    ]
 
     def flips():
         routes = []
@@ -772,26 +941,24 @@
             ]
         )
 
-    segments = lax.dynamic_index_in_dim(
-        segment_ids.reshape(row_count, length), rank // chips, 0, keepdims=False
-    )
-    seg_q = lax.dynamic_slice_in_dim(segments, block * count, count, 0)
-    seg_k = jnp.concatenate(
-        [
-            lax.dynamic_slice_in_dim(segments, (block ^ distance) * count, count, 0)
-            for distance in range(blocks)
-        ]
-    )[:, None]
-    seg_q = seg_q[None, :]
-
     out_blocks = half_ranks if quick else 1
     order = (low_rank if quick else 0 * rank).astype(jnp.int32).reshape(1)
+    place_here = jnp.stack([plane, section]).astype(jnp.int32)
+    p_tables = []
     saved = []
     x = tokens
     for layer in range(2):
         p_table, *others = tables[layer]
         p_bias, u_bias, pk, pv = smalls[layer]
-        q, own = project(x, p_table, p_bias)
+        if quick and layer == 0:
+            cross = lax.dynamic_index_in_dim(
+                early[:, :, d_end : d_end + share], section, 0, keepdims=False
+            )
+            theirs = lax.ppermute(cross, "dp", swap)
+        if quick and layer == 1:
+            p_table = ((early, theirs, theirs_too), d_end)
+        p_tables.append(p_table)
+        q, own = project(x, p_table, p_bias, place_here)
         other = exchange([own] * (blocks - 1))
         mixed, raised, inverse = attend(q, own, other, pk, pv, prefix_count, seg_q, seg_k)
         saved.append((mixed, inverse, raised, q, own, other, pk, pv))
@@ -801,10 +968,15 @@
             x, mixed, others, vectors[layer], u_bias, order, out_blocks if layer else 0
         )
         saved[-1] += (kept,)
+        if layer == 0 and quick:
+            theirs, x = lax.optimization_barrier((theirs, x))
+            theirs_too = lax.ppermute(theirs, "section", swap)
     outs = x
     kept_0, kept_1 = (entry[-1] for entry in saved)
     saved = [entry[:-1] for entry in saved]
-    first, d_mixed = link((cotangent,), None, tables[1][1:], vectors[1], kept_1)
+    first, dq, down, dother, prefix_1 = backward(
+        (cotangent,), None, tables[1][1:], vectors[1], kept_1, saved[1], place_here
+    )
 
     def send_blocks(parts):
         got = []
@@ -817,42 +989,38 @@
             got.append(lax.ppermute(part, ("section", "tensor"), route))
         return got
 
-    dq, down, dother, prefix_1 = attend_back(d_mixed, *saved[1])
     if quick:
+        dother, *outs = lax.optimization_barrier((dother, *outs))
         outs = send_blocks(outs)
+    got = exchange([dother[i] for i in range(blocks - 1)])
+    first, dq, down, dother, prefix_0 = backward(
+        (first, dq, down, got), p_tables[1], tables[0][1:], vectors[0], kept_0, saved[0], place_here
+    )
+    if quick:
         dother, *outs = lax.optimization_barrier((dother, *outs))
-    got = exchange([dother[i] for i in range(blocks - 1)])
-    first, d_mixed = link(
-        (first, dq, down, got), tables[1][0], tables[0][1:], vectors[0], kept_0
-    )
-    dq, down, dother, prefix_0 = attend_back(d_mixed, *saved[0])
     got = exchange([dother[i] for i in range(blocks - 1)])
     if quick:
         prefix = jnp.stack([prefix_0, prefix_1], axis=1)
         lower, upper = prefix[: pairs // 2], prefix[pairs // 2 :]
         other = lax.ppermute(jnp.where(is_first, upper, lower), "section", swap)
         prefix = jnp.where(is_first, lower, upper) + other
-        got, prefix = lax.optimization_barrier((got, prefix))
-    grads = leave(first, dq, down, got, tables[0][0], order, out_blocks)
+        prefix = prefix.reshape(half_ranks, 4 * pad, PAIR)
+    else:
+        prefix = None
+    grads = leave(first, dq, down, got, tables[0][0], order, out_blocks, prefix)
 
     if quick:
         grads = send_blocks(grads)
-        prefix = sum(
-            send_blocks(
-                [
-                    lax.dynamic_index_in_dim(prefix, low_rank ^ j, 0, keepdims=False)
-                    for j in range(half_ranks)
-                ]
-            )
-        )
+        partial = sum(part[slots:].astype(f32) for part in grads)
+        grads = jnp.stack(ordered([part[:slots] for part in grads]))
         outs = jnp.stack(ordered(outs))
-        prefix += lax.ppermute(prefix, "dp", swap)
-        prefix = jnp.where(is_first, prefix[0], prefix[1]) + lax.ppermute(
-            jnp.where(is_first, prefix[1], prefix[0]), "section", swap
-        )
-        grads = jnp.stack(ordered(grads))
         keep = jnp.where(is_first, grads, outs)
         got = lax.ppermute(jnp.where(is_first, outs, grads), "section", swap)
+        partial += lax.ppermute(partial, "dp", swap)
+        partial = jnp.transpose(partial.reshape(16, -1, PAIR), (1, 0, 2)).reshape(2, 2 * pad, PAIR)
+        prefix = jnp.where(is_first, partial[0], partial[1]) + lax.ppermute(
+            jnp.where(is_first, partial[1], partial[0]), "section", swap
+        )
         back = jnp.concatenate(
             [jnp.where(is_first, keep, got), jnp.where(is_first, got, keep)], axis=0
         )

time: 522 us -> 495 us (0.948)
  waiting for transfers between devices: 196 us -> 173 us
  Pallas kernels: 206 us -> 198 us
    all_gather x2, waiting for transfers between devices: 143 us -> 125 us  [per_device(): lax.all_gather(jnp.concatenate(parts, axis=0), ('section', 'tensor'), axi...]
    pallas_call x2, Pallas kernels: 49 us -> 43.2 us  [feed(): call(functools.partial(feed_kernel, (o_table[1], pieces), len(arrays), bl...]
    ppermute x4, waiting for transfers between devices: 5.55 us -> 0.01 us  [exchange(): lax.ppermute(part, 'section', swap)]
    ppermute x12 -> x8, starting transfers between devices: 13.8 us -> 10.4 us  [send_blocks(): got.append(lax.ppermute(part, ('section', 'tensor'), route))]
    ppermute x12 -> x8, waiting for transfers between devices: 10.1 us -> 12.8 us  [send_blocks(): got.append(lax.ppermute(part, ('section', 'tensor'), route))]
    pallas_call x7 -> x6, Pallas kernels: 114 us -> 115 us  [the longest x2 82.4 us: backward(): call(functools.partial(back_kernel, p_first, len(more), o_table[1], piece...]
  transfers between devices with their start and end apart: 33 -> 31, of which waited for: 15 -> 12; matrix products, arithmetic and copies ran while one was open for 5% -> 8% of each run, Pallas kernels for 29% -> 30%
where the time goes in v3:
time: 495 us; the launch traced here: 490 us
  Pallas kernels  198 us (40%)
  waiting for transfers between devices  173 us (35%)
  starting transfers between devices  49.6 us (10%)
  local copies, waits for them, and re-layouts  35.5 us (7%)
  other arithmetic  19.7 us (4%)
  between operations  14.8 us (3%)
    all_gather x2, waiting for transfers between devices, per_device(): lax.all_gather(jnp.concatenate(parts, axis=0), ('section', 'tensor'), axi...  125 us
    pallas_call x2, Pallas kernels, backward(): call(functools.partial(back_kernel, p_first, len(more), o_table[1], piece...  82.4 us
    pallas_call x2, Pallas kernels, feed(): call(functools.partial(feed_kernel, (o_table[1], pieces), len(arrays), bl...  43.2 us
    pallas_call x2, Pallas kernels, attend(): call(functools.partial(attend_kernel, prefix_count), [by_pair, pl.BlockSp...  39.9 us
    ppermute x8, waiting for transfers between devices, arrive(): parts.append(lax.ppermute(part, ('section', 'tensor'), route))  22.6 us
    pallas_call x2, Pallas kernels, project(): call(functools.partial(project_kernel, first), [IN_VMEM, IN_VMEM, IN_SMEM...  18.1 us
    ppermute x8, starting transfers between devices, arrive(): parts.append(lax.ppermute(part, ('section', 'tensor'), route))  15.4 us
    ppermute x8, waiting for transfers between devices, send_blocks(): got.append(lax.ppermute(part, ('section', 'tensor'), route))  12.8 us
  transfers between devices with their start and end apart: 31, of which 12 were waited for; matrix products, arithmetic and copies ran while one was open for 8% of the time, Pallas kernels for 30%

profile of v3, /device:TPU:0, one launch (start us, length us, event | category | flops | bytes accessed | tf_op | source)
XLA Modules:
  0.0 490.3 jit_solution(13405990471566668048)
XLA Ops:
  11.4 4.2 shard_map.148
  16.0 3.3 collective-permute-done.1
  19.3 1.6 broadcast_select_fusion.2
  21.2 1.4 pad_maximum_fusion.1
  22.6 3.0 broadcast_select_fusion
  25.7 1.3 copy.29
  27.6 1.3 copy.30
  30.0 2.7 bitcast_select_fusion
  32.7 3.5 collective-permute-start.5
  37.2 1.7 collective-permute-start.4
  40.2 8.2 %collective-permute-done.5 = bf16[128,1024]{1,0:T(8,128)(2,1)S(1)} collective-permute-done((bf16[128,1024]{1,0:T(8,128)(2,1)S(1)}, bf16[128,1024]{1,0:T(8,128)(2,1)S(1)}, u32[]{:S(2)}, u32[]{:S(2)}) %collective-permute-start.5) | collective-permute-done | bytes 262176 | tf_op jit(solution)/shard_map/ppermute | solution.py:773
  48.4 3.6 collective-permute-done.4
  52.0 10.7 %collective-permute-done.3 = bf16[128,1024]{1,0:T(8,128)(2,1)} collective-permute-done((bf16[128,1024]{1,0:T(8,128)(2,1)S(1)}, bf16[128,1024]{1,0:T(8,128)(2,1)}, u32[]{:S(2)}, u32[]{:S(2)}) %collective-permute-start.3) | collective-permute-done | bytes 262176 | tf_op jit(solution)/shard_map/ppermute | solution.py:773
  65.9 124.6 %all-gather.5.cloned.1.call-done = bf16[14336,1024]{1,0:T(8,128)(2,1)} async-done(((bf16[896,1024]{1,0:T(8,128)(2,1)}), bf16[14336,1024]{1,0:T(8,128)(2,1)}) %all-gather.5.cloned.1.call-update) | async-done | bytes 29360144 | tf_op jit(solution)/shard_map/all_gather | solution.py:842
  191.2 2.1 fusion.1
  194.4 8.6 %shard_map.149 = (bf16[8,512,128]{2,1,0:T(8,128)(2,1)}, bf16[2,8,512,128]{3,2,1,0:T(8,128)(2,1)}) custom-call(bf16[512,1024]{1,0:T(8,128)(2,1)} %pad_maximum_fusion.2.x_ref, f32[3,1,1024]{2,1,0:T(1,128)} %reshape.160.b_ref, s32[2]{0:T(128)} %pad_add_fusion.1.place_ref, bf16[2,8,896,1024]{3,2,1,0:T(8,128)(2,1)} %bitcast.108), custom_call_target="tpu_custom_call" | custom-call | flops 3221225472 | bytes 10485760 | tf_op jit(solution)/shard_map/pallas_call | solution.py:219
  203.3 2.6 slice.112
  207.3 1.3 dynamic-slice_bitcast_fusion
  208.6 1.6 collective-permute-start.11
  213.2 20.1 %shard_map.150 = (bf16[8,512,128]{2,1,0:T(8,128)(2,1)}, bf16[8,2,1056,512]{3,2,1,0:T(8,128)(2,1)}, bf16[8,512,128]{2,1,0:T(8,128)(2,1)}) custom-call(bf16[8,512,128]{2,1,0:T(8,128)(2,1)} %get-tuple-element.71.q_ref.rest_17_, bf16[2,8,512,128]{3,2,1,0:T(8,128)(2,1)} %get-tuple-element.72.own_ref.rest_18_, ...), custom_call_target="tpu_custom_call" | custom-call | flops 4429185024 | bytes 17301504 | tf_op jit(solution)/shard_map/pallas_call | solution.py:464
  233.3 21.6 %shard_map.151 = (bf16[512,1024]{1,0:T(8,128)(2,1)}, bf16[512,1024]{1,0:T(8,128)(2,1)}, f32[512,1]{1,0:T(8,128)}, bf16[512,1024]{1,0:T(8,128)(2,1)}, f32[512,1]{1,0:T(8,128)}, /*index=5*/bf16[512,4096]{1,0:T(8,128)(2,1)}) custom-call(bf16[512,1024]{1,0:T(8,128)(2,1)} %pad_maximum_fusion.2.x_ref, bf16[8,512,128]{2,1,0:T(8,128)(2,1)} %get-tuple-element.75.mixed_ref.rest_14_, ...), custom_call_target="tpu_custom_call" | custom-call | flops 9663676416 | bytes 29360128 | tf_op jit(solution)/shard_map/pallas_call | solution.py:334
  255.1 2.5 reshape.153
  259.1 1.2 copy-done.1
  260.3 9.5 %shard_map.152 = (bf16[8,512,128]{2,1,0:T(8,128)(2,1)}, bf16[2,8,512,128]{3,2,1,0:T(8,128)(2,1)}) custom-call(bf16[512,1024]{1,0:T(8,128)(2,1)} %get-tuple-element.78.x_ref, f32[3,1,1024]{2,1,0:T(1,128)} %reshape.162.b_ref, s32[2]{0:T(128)} %pad_add_fusion.1.place_ref, bf16[2,8,896,1024]{3,2,1,0:T(8,128)(2,1)} %bitcast.112, bf16[8,96,1024]{2,1,0:T(8,128)(2,1)} %copy-done, ...), custom_call_target="tpu_custom_call" | custom-call | flops 3221225472 | bytes 10485760 | tf_op jit(solution)/shard_map/pallas_call | solution.py:219
  274.3 1.3 copy-done.12
  275.6 19.8 %shard_map.153 = (bf16[8,512,128]{2,1,0:T(8,128)(2,1)}, bf16[8,2,1056,512]{3,2,1,0:T(8,128)(2,1)}, bf16[8,512,128]{2,1,0:T(8,128)(2,1)}) custom-call(bf16[8,512,128]{2,1,0:T(8,128)(2,1)} %get-tuple-element.80.q_ref.rest_11_, bf16[2,8,512,128]{3,2,1,0:T(8,128)(2,1)} %get-tuple-element.81.own_ref.rest_12_, bf16[1,2,8,512,128]{4,3,2,1,0:T(8,128)(2,1)} %bitcast.158, ...), custom_call_target="tpu_custom_call" | custom-call | flops 4429185024 | bytes 17301504 | tf_op jit(solution)/shard_map/pallas_call | solution.py:464
  295.9 1.3 collective-permute-start.9
  298.2 6.2 %collective-permute-start.8 = (bf16[128,1024]{1,0:T(8,128)(2,1)S(1)}, bf16[128,1024]{1,0:T(8,128)(2,1)S(1)}, u32[]{:S(2)}, u32[]{:S(2)}) collective-permute-start(bf16[128,1024]{1,0:T(8,128)(2,1)S(1)} %get-tuple-element.152), channel_id=1, source_target_pairs={{0,2},{1,3},{2,0},{3,1},{4,18},{5,19},{6,16},{7,17},{16,6},{17,7},... | collective-permute-start | bytes 786440 | tf_op jit(solution)/shard_map/ppermute | solution.py:773
  305.1 21.6 %shard_map.154 = (bf16[128,1024]{1,0:T(8,128)(2,1)}, bf16[128,1024]{1,0:T(8,128)(2,1)}, bf16[128,1024]{1,0:T(8,128)(2,1)}, bf16[128,1024]{1,0:T(8,128)(2,1)}, bf...) custom-call(bf16[512,1024]{1,0:T(8,128)(2,1)} %get-tuple-element.78., ...), custom_call_target="tpu_custom_call" | custom-call | flops 9663676416 | bytes 29360128 | tf_op jit(solution)/shard_map/pallas_call | solution.py:334
  327.8 38.0 %shard_map.155 = (bf16[512,1024]{1,0:T(8,128)(2,1)}, bf16[8,512,128]{2,1,0:T(8,128)(2,1)}, bf16[2,8,512,128]{3,2,1,0:T(8,128)(2,1)}, bf16[1,2,8,512,128]{4,3,2,1,0:T(8,128)(2,1)}, f32[8,64,128]{2,1,0:T(8,128)}) custom-call(s32[2]{0:T(128)} %pad_add_fusion.1.place_ref, bf16[512,1024]{1,0:T(8,128)(2,1)} %pad_maximum_fusion.3.rest_0_, ...), custom_call_target="tpu_custom_call" | custom-call | flops 21743271936 | bytes 59244544 | tf_op jit(solution)/shard_map/pallas_call | solution.py:674
  365.8 4.2 collective-permute-start.15
  370.0 1.7 collective-permute-start.16
  371.7 1.5 collective-permute-start.17
  373.9 1.4 collective-permute-start.19
  375.3 1.4 copy-done.3
  376.6 44.4 %shard_map.156 = (bf16[512,1024]{1,0:T(8,128)(2,1)}, bf16[8,512,128]{2,1,0:T(8,128)(2,1)}, bf16[2,8,512,128]{3,2,1,0:T(8,128)(2,1)}, bf16[1,2,8,512,128]{4,3,2,1,0:T(8,128)(2,1)}, f32[8,64,128]{2,1,0:T(8,128)}) custom-call(s32[2]{0:T(128)} %pad_add_fusion.1.place_ref, bf16[512,1024]{1,0:T(8,128)(2,1)} %get-tuple-element.90.rest_0_, ...), custom_call_target="tpu_custom_call" | custom-call | flops 21743271936 | bytes 59244544 | tf_op jit(solution)/shard_map/pallas_call | solution.py:674
  421.1 4.0 collective-permute-start.20
  426.2 3.1 collective-permute-done.21
  431.1 1.3 copy-done.4
  432.4 10.2 %shard_map.157 = (bf16[144,1024]{1,0:T(8,128)(2,1)}, bf16[144,1024]{1,0:T(8,128)(2,1)}, bf16[144,1024]{1,0:T(8,128)(2,1)}, bf16[144,1024]{1,0:T(8,128)(2,1)}) custom-call(bf16[512,1024]{1,0:T(8,128)(2,1)} %get-tuple-element.106.first_ref, bf16[8,512,128]{2,1,0:T(8,128)(2,1)} %get-tuple-element.107.dq_ref, ...), custom_call_target="tpu_custom_call" | custom-call | flops 3221225472 | bytes 13631488 | tf_op jit(solution)/shard_map/pallas_call | solution.py:394
  442.7 2.9 collective-permute-start.23
  446.1 1.6 collective-permute-start.25
  447.8 3.9 collective-permute-done.22
  451.8 8.9 %collective-permute-done.23 = bf16[144,1024]{1,0:T(8,128)(2,1)S(1)} collective-permute-done((bf16[144,1024]{1,0:T(8,128)(2,1)}, bf16[144,1024]{1,0:T(8,128)(2,1)S(1)}, u32[]{:S(2)}, u32[]{:S(2)}) %collective-permute-start.23) | collective-permute-done | bytes 294944 | tf_op jit(solution)/shard_map/ppermute | solution.py:989
  461.0 11.4 %collective-permute-start.26 = (bf16[4,128,1024]{2,1,0:T(8,128)(2,1)S(1)}, bf16[4,128,1024]{2,1,0:T(8,128)(2,1)S(1)}, u32[]{:S(2)}, u32[]{:S(2)}) collective-permute-start(bf16[4,128,1024]{2,1,0:T(8,128)(2,1)S(1)} %broadcast_select_fusion.6), channel_id=1, source_target_pairs={{0,16},{16,0},{1,17},{17,1},{2,18},{18,2},{3,19},{19,3},{4,20},{20... | collective-permute-start | bytes 3145736 | tf_op jit(solution)/shard_map/ppermute | solution.py:1018
  473.0 3.7 collective-permute-done.27
  476.9 1.2 collective-permute-done.28
  479.8 3.5 copy.65
  (145 shorter events, 34.8 us)
Async XLA Ops:
  7.2 183.4 %all-gather.5.cloned.1.call-start = ((), (), s32[]{:S(2)}) async-start(), calls=%async_computation | async-start | bytes 31195136 | tf_op jit(solution)/shard_map/all_gather | solution.py:842
  15.5 3.8 collective-permute-start.1
  22.6 273.2 %all-gather.7.cloned.1.call-start = ((), (), s32[]{:S(2)}) async-start(), calls=%async_computation.1 | async-start | bytes 20054016 | tf_op jit(solution)/shard_map/all_gather | solution.py:842
  25.6 1.7 copy-start.8
  25.7 1.7 copy-start.9
  25.7 1.7 copy-start.10
  25.7 1.9 copy-start.7
  27.0 3.0 collective-permute-start
  27.4 12.1 %collective-permute-start.2 = (bf16[8,1024]{1,0:T(8,128)(2,1)S(1)}, bf16[8,1024]{1,0:T(8,128)(2,1)S(1)}, u32[]{:S(2)}, u32[]{:S(2)}) collective-permute-start(bf16[8,1024]{1,0:T(8,128)(2,1)S(1)} %pad_maximum_fusion.7), channel_id=1, source_target_pairs={{0,16},{16,0},{1,17},{17,1},{2,18},{18,2},{3,19},{19,3},{4,20},{20... | collective-permute-start | bytes 49160 | tf_op jit(solution)/shard_map/ppermute | solution.py:792
  28.9 10.0 %copy-start.11 = (s32[1,512]{1,0:T(1,128)}, s32[1,512]{1,0:T(1,128)S(1)}, u32[]{:S(2)}) copy-start(s32[1,512]{1,0:T(1,128)S(1)} %get-tuple-element.73.sq_ref) | copy-start | bytes 6148
  32.7 15.7 %collective-permute-start.5 = (bf16[128,1024]{1,0:T(8,128)(2,1)S(1)}, bf16[128,1024]{1,0:T(8,128)(2,1)S(1)}, u32[]{:S(2)}, u32[]{:S(2)}) collective-permute-start(bf16[128,1024]{1,0:T(8,128)(2,1)S(1)} %get-tuple-element.158), channel_id=1, source_target_pairs={{0,1},{1,0},{2,3},{3,2},{4,17},{5,16},{6,19},{7,18},{16,5},{17,4},... | collective-permute-start | bytes 786440 | tf_op jit(solution)/shard_map/ppermute | solution.py:773
  36.2 12.1 %collective-permute-start.6 = (bf16[128,1024]{1,0:T(8,128)(2,1)S(1)}, bf16[128,1024]{1,0:T(8,128)(2,1)S(1)}, u32[]{:S(2)}, u32[]{:S(2)}) collective-permute-start(bf16[128,1024]{1,0:T(8,128)(2,1)S(1)} %get-tuple-element.159), channel_id=1, source_target_pairs={{0,0},{1,1},{2,2},{3,3},{4,16},{5,17},{6,18},{7,19},{16,4},{17,5},... | collective-permute-start | bytes 786440 | tf_op jit(solution)/shard_map/ppermute | solution.py:773
  37.2 14.8 %collective-permute-start.4 = (bf16[128,1024]{1,0:T(8,128)(2,1)S(1)}, bf16[128,1024]{1,0:T(8,128)(2,1)S(1)}, u32[]{:S(2)}, u32[]{:S(2)}) collective-permute-start(bf16[128,1024]{1,0:T(8,128)(2,1)S(1)} %get-tuple-element.160), channel_id=1, source_target_pairs={{0,2},{1,3},{2,0},{3,1},{4,18},{5,19},{6,16},{7,17},{16,6},{17,7},... | collective-permute-start | bytes 786440 | tf_op jit(solution)/shard_map/ppermute | solution.py:773
  38.9 23.9 %collective-permute-start.3 = (bf16[128,1024]{1,0:T(8,128)(2,1)S(1)}, bf16[128,1024]{1,0:T(8,128)(2,1)}, u32[]{:S(2)}, u32[]{:S(2)}) collective-permute-start(bf16[128,1024]{1,0:T(8,128)(2,1)S(1)} %get-tuple-element.161), channel_id=1, source_target_pairs={{0,3},{1,2},{2,1},{3,0},{4,19},{5,18},{6,17},{7,16},{16,7},{17,6},... | collective-permute-start | bytes 786440 | tf_op jit(solution)/shard_map/ppermute | solution.py:773
  193.5 9.4 %copy-start.6 = (bf16[2,8,16384]{2,1,0:T(8,128)(2,1)}, bf16[2,8,16384]{2,1,0:T(8,128)(2,1)S(1)}, u32[]{:S(2)}) copy-start(bf16[2,8,16384]{2,1,0:T(8,128)(2,1)S(1)} %reshape.149) | copy-start | bytes 1572868
  203.0 10.2 %collective-permute-start.12 = (bf16[2,8,512,128]{3,2,1,0:T(8,128)(2,1)}, bf16[2,8,512,128]{3,2,1,0:T(8,128)(2,1)}, u32[]{:S(2)}, u32[]{:S(2)}) collective-permute-start(bf16[2,8,512,128]{3,2,1,0:T(8,128)(2,1)} %get-tuple-element.72.own_ref.rest_18_), channel_id=1, source_target_pairs={{0,16},{16,0},{1,17},{17,1},{2,18},{18,2},{3,19},{19,3},{4,20},{20... | collective-permute-start | bytes 6291464 | tf_op jit(solution)/shard_map/ppermute | solution.py:939
  208.6 46.3 %collective-permute-start.11 = (bf16[8,96,1024]{2,1,0:T(8,128)(2,1)}, bf16[8,96,1024]{2,1,0:T(8,128)(2,1)S(1)}, u32[]{:S(2)}, u32[]{:S(2)}) collective-permute-start(bf16[8,96,1024]{2,1,0:T(8,128)(2,1)} %dynamic-slice_bitcast_fusion), channel_id=1, source_target_pairs={{0,8},{8,0},{1,9},{9,1},{2,10},{10,2},{3,11},{11,3},{4,12},{12,4},... | collective-permute-start | bytes 4718600 | tf_op jit(solution)/shard_map/ppermute | solution.py:957
  255.0 4.1 copy-start
  255.0 4.1 collective-permute-start.13
  259.1 1.2 copy-start.1
  269.8 4.5 collective-permute-start.14
  274.3 1.3 copy-start.12
  275.6 20.2 %copy-start.2 = (bf16[4,128,1024]{2,1,0:T(8,128)(2,1)S(1)}, bf16[4,128,1024]{2,1,0:T(8,128)(2,1)}, u32[]{:S(2)}) copy-start(bf16[4,128,1024]{2,1,0:T(8,128)(2,1)} %get-tuple-element.68) | copy-start | bytes 3145732
  295.9 30.8 %collective-permute-start.9 = (bf16[128,1024]{1,0:T(8,128)(2,1)S(1)}, bf16[128,1024]{1,0:T(8,128)(2,1)S(1)}, u32[]{:S(2)}, u32[]{:S(2)}) collective-permute-start(bf16[128,1024]{1,0:T(8,128)(2,1)S(1)} %get-tuple-element.150), channel_id=1, source_target_pairs={{0,1},{1,0},{2,3},{3,2},{4,17},{5,16},{6,19},{7,18},{16,5},{17,4},... | collective-permute-start | bytes 786440 | tf_op jit(solution)/shard_map/ppermute | solution.py:773
  297.3 29.4 %collective-permute-start.10 = (bf16[128,1024]{1,0:T(8,128)(2,1)S(1)}, bf16[128,1024]{1,0:T(8,128)(2,1)S(1)}, u32[]{:S(2)}, u32[]{:S(2)}) collective-permute-start(bf16[128,1024]{1,0:T(8,128)(2,1)S(1)} %get-tuple-element.151), channel_id=1, source_target_pairs={{0,0},{1,1},{2,2},{3,3},{4,16},{5,17},{6,18},{7,19},{16,4},{17,5},... | collective-permute-start | bytes 786440 | tf_op jit(solution)/shard_map/ppermute | solution.py:773
  298.2 28.5 %collective-permute-start.8 = (bf16[128,1024]{1,0:T(8,128)(2,1)S(1)}, bf16[128,1024]{1,0:T(8,128)(2,1)S(1)}, u32[]{:S(2)}, u32[]{:S(2)}) collective-permute-start(bf16[128,1024]{1,0:T(8,128)(2,1)S(1)} %get-tuple-element.152), channel_id=1, source_target_pairs={{0,2},{1,3},{2,0},{3,1},{4,18},{5,19},{6,16},{7,17},{16,6},{17,7},... | collective-permute-start | bytes 786440 | tf_op jit(solution)/shard_map/ppermute | solution.py:773
  304.4 22.3 %collective-permute-start.7 = (bf16[128,1024]{1,0:T(8,128)(2,1)S(1)}, bf16[128,1024]{1,0:T(8,128)(2,1)S(1)}, u32[]{:S(2)}, u32[]{:S(2)}) collective-permute-start(bf16[128,1024]{1,0:T(8,128)(2,1)S(1)} %get-tuple-element.153), channel_id=1, source_target_pairs={{0,3},{1,2},{2,1},{3,0},{4,19},{5,18},{6,17},{7,16},{16,7},{17,6},... | collective-permute-start | bytes 786440 | tf_op jit(solution)/shard_map/ppermute | solution.py:773
  327.8 45.4 %copy-start.14 = (bf16[128,1024]{1,0:T(8,128)(2,1)S(1)}, bf16[128,1024]{1,0:T(8,128)(2,1)}, u32[]{:S(2)}) copy-start(bf16[128,1024]{1,0:T(8,128)(2,1)} %get-tuple-element.112) | copy-start | bytes 786436
  327.8 46.1 %copy-start.13 = (bf16[128,1024]{1,0:T(8,128)(2,1)S(1)}, bf16[128,1024]{1,0:T(8,128)(2,1)}, u32[]{:S(2)}) copy-start(bf16[128,1024]{1,0:T(8,128)(2,1)} %get-tuple-element.113) | copy-start | bytes 786436
  365.8 9.5 %collective-permute-start.15 = (bf16[2,8,512,128]{3,2,1,0:T(8,128)(2,1)}, bf16[2,8,512,128]{3,2,1,0:T(8,128)(2,1)S(1)}, u32[]{:S(2)}, u32[]{:S(2)}) collective-permute-start(bf16[2,8,512,128]{3,2,1,0:T(8,128)(2,1)} %bitcast.161), channel_id=1, source_target_pairs={{0,16},{16,0},{1,17},{17,1},{2,18},{18,2},{3,19},{19,3},{4,20},{20... | collective-permute-start | bytes 6291464 | tf_op jit(solution)/shard_map/ppermute | solution.py:939
  370.0 51.1 %collective-permute-start.16 = (bf16[128,1024]{1,0:T(8,128)(2,1)}, bf16[128,1024]{1,0:T(8,128)(2,1)S(1)}, u32[]{:S(2)}, u32[]{:S(2)}) collective-permute-start(bf16[128,1024]{1,0:T(8,128)(2,1)} %get-tuple-element.110), channel_id=1, source_target_pairs={{0,0},{1,1},{2,2},{3,3},{4,16},{5,17},{6,18},{7,19},{16,4},{17,5},... | collective-permute-start | bytes 786440 | tf_op jit(solution)/shard_map/ppermute | solution.py:989
  371.7 49.4 %collective-permute-start.17 = (bf16[128,1024]{1,0:T(8,128)(2,1)}, bf16[128,1024]{1,0:T(8,128)(2,1)S(1)}, u32[]{:S(2)}, u32[]{:S(2)}) collective-permute-start(bf16[128,1024]{1,0:T(8,128)(2,1)} %get-tuple-element.111), channel_id=1, source_target_pairs={{0,1},{1,0},{2,3},{3,2},{4,17},{5,16},{6,19},{7,18},{16,5},{17,4},... | collective-permute-start | bytes 786440 | tf_op jit(solution)/shard_map/ppermute | solution.py:989
  373.2 47.9 %collective-permute-start.18 = (bf16[128,1024]{1,0:T(8,128)(2,1)S(1)}, bf16[128,1024]{1,0:T(8,128)(2,1)S(1)}, u32[]{:S(2)}, u32[]{:S(2)}) collective-permute-start(bf16[128,1024]{1,0:T(8,128)(2,1)S(1)} %copy-done.14), channel_id=1, source_target_pairs={{0,2},{1,3},{2,0},{3,1},{4,18},{5,19},{6,16},{7,17},{16,6},{17,7},... | collective-permute-start | bytes 786440 | tf_op jit(solution)/shard_map/ppermute | solution.py:989
  373.9 47.2 %collective-permute-start.19 = (bf16[128,1024]{1,0:T(8,128)(2,1)S(1)}, bf16[128,1024]{1,0:T(8,128)(2,1)S(1)}, u32[]{:S(2)}, u32[]{:S(2)}) collective-permute-start(bf16[128,1024]{1,0:T(8,128)(2,1)S(1)} %copy-done.13), channel_id=1, source_target_pairs={{0,3},{1,2},{2,1},{3,0},{4,19},{5,18},{6,17},{7,16},{16,7},{17,6},... | collective-permute-start | bytes 786440 | tf_op jit(solution)/shard_map/ppermute | solution.py:989
  375.3 1.4 copy-start.3
  376.6 48.5 %copy-start.5 = (f32[8,64,128]{2,1,0:T(8,128)S(1)}, f32[8,64,128]{2,1,0:T(8,128)}, u32[]{:S(2)}) copy-start(f32[8,64,128]{2,1,0:T(8,128)} %get-tuple-element.116) | copy-start | bytes 786436
  421.1 9.9 %collective-permute-start.20 = (bf16[2,8,512,128]{3,2,1,0:T(8,128)(2,1)}, bf16[2,8,512,128]{3,2,1,0:T(8,128)(2,1)S(1)}, u32[]{:S(2)}, u32[]{:S(2)}) collective-permute-start(bf16[2,8,512,128]{3,2,1,0:T(8,128)(2,1)} %bitcast.160), channel_id=1, source_target_pairs={{0,16},{16,0},{1,17},{17,1},{2,18},{18,2},{3,19},{19,3},{4,20},{20... | collective-permute-start | bytes 6291464 | tf_op jit(solution)/shard_map/ppermute | solution.py:939
  426.2 3.2 collective-permute-start.21
  431.1 1.3 copy-start.4
  442.6 9.2 %collective-permute-start.22 = (bf16[144,1024]{1,0:T(8,128)(2,1)}, bf16[144,1024]{1,0:T(8,128)(2,1)S(1)}, u32[]{:S(2)}, u32[]{:S(2)}) collective-permute-start(bf16[144,1024]{1,0:T(8,128)(2,1)} %get-tuple-element.117), channel_id=1, source_target_pairs={{0,3},{1,2},{2,1},{3,0},{4,19},{5,18},{6,17},{7,16},{16,7},{17,6},... | collective-permute-start | bytes 884744 | tf_op jit(solution)/shard_map/ppermute | solution.py:989
  442.7 18.0 %collective-permute-start.23 = (bf16[144,1024]{1,0:T(8,128)(2,1)}, bf16[144,1024]{1,0:T(8,128)(2,1)S(1)}, u32[]{:S(2)}, u32[]{:S(2)}) collective-permute-start(bf16[144,1024]{1,0:T(8,128)(2,1)} %get-tuple-element.118), channel_id=1, source_target_pairs={{0,2},{1,3},{2,0},{3,1},{4,18},{5,19},{6,16},{7,17},{16,6},{17,7},... | collective-permute-start | bytes 884744 | tf_op jit(solution)/shard_map/ppermute | solution.py:989
  445.6 15.1 %collective-permute-start.24 = (bf16[144,1024]{1,0:T(8,128)(2,1)}, bf16[144,1024]{1,0:T(8,128)(2,1)S(1)}, u32[]{:S(2)}, u32[]{:S(2)}) collective-permute-start(bf16[144,1024]{1,0:T(8,128)(2,1)} %get-tuple-element.119), channel_id=1, source_target_pairs={{0,1},{1,0},{2,3},{3,2},{4,17},{5,16},{6,19},{7,18},{16,5},{17,4},... | collective-permute-start | bytes 884744 | tf_op jit(solution)/shard_map/ppermute | solution.py:989
  446.1 14.5 %collective-permute-start.25 = (bf16[144,1024]{1,0:T(8,128)(2,1)}, bf16[144,1024]{1,0:T(8,128)(2,1)S(1)}, u32[]{:S(2)}, u32[]{:S(2)}) collective-permute-start(bf16[144,1024]{1,0:T(8,128)(2,1)} %get-tuple-element.120), channel_id=1, source_target_pairs={{0,0},{1,1},{2,2},{3,3},{4,16},{5,17},{6,18},{7,19},{16,4},{17,5},... | collective-permute-start | bytes 884744 | tf_op jit(solution)/shard_map/ppermute | solution.py:989
  461.0 18.3 %collective-permute-start.26 = (bf16[4,128,1024]{2,1,0:T(8,128)(2,1)S(1)}, bf16[4,128,1024]{2,1,0:T(8,128)(2,1)S(1)}, u32[]{:S(2)}, u32[]{:S(2)}) collective-permute-start(bf16[4,128,1024]{2,1,0:T(8,128)(2,1)S(1)} %broadcast_select_fusion.6), channel_id=1, source_target_pairs={{0,16},{16,0},{1,17},{17,1},{2,18},{18,2},{3,19},{19,3},{4,20},{20... | collective-permute-start | bytes 3145736 | tf_op jit(solution)/shard_map/ppermute | solution.py:1018
  472.4 4.3 collective-permute-start.27
  476.8 1.3 collective-permute-start.28
Sparse Core Ops, SparseCore 0:
  22.7 167.8 all-gather.4
  192.2 103.6 all-gather.6

commit v4 on v3

--- a/solution.py
+++ b/solution.py
@@ -68,7 +68,7 @@
         copy.wait()
 
 
-def call(kernel, in_specs, out_specs, out_shape, scratch=(), grid=None, flops=0, moved=0, exps=0):
+def call(kernel, in_specs, out_specs, out_shape, scratch=(), grid=None, flops=0, moved=0, exps=0, vmem=VMEM):
     more = {} if grid is None else {"grid": grid}
     return pl.pallas_call(
         kernel,
@@ -76,14 +76,15 @@
         out_specs=out_specs,
         out_shape=out_shape,
         scratch_shapes=list(scratch),
-        compiler_params=pltpu.CompilerParams(vmem_limit_bytes=VMEM),
+        compiler_params=pltpu.CompilerParams(vmem_limit_bytes=vmem),
         cost_estimate=pl.CostEstimate(flops=flops, bytes_accessed=moved, transcendentals=exps),
         **more,
     )
 
 
 IN_VMEM = pl.BlockSpec(memory_space=pltpu.VMEM)
-IN_HBM = pl.BlockSpec(memory_space=pl.ANY)
+IN_HBM = pl.BlockSpec(memory_space=pltpu.HBM)
+IN_ANY = pl.BlockSpec(memory_space=pl.ANY)
 IN_SMEM = pl.BlockSpec(memory_space=pltpu.SMEM)
 
 
@@ -95,7 +96,7 @@
     return jax.ShapeDtypeStruct(shape, dtype)
 
 
-def pack_kernel(p_ref, o_ref, u_ref, d_ref, s_ref, section_ref, keep_ref, give_ref, stage, semaphores):
+def pack_kernel(p_ref, o_ref, u_ref, d_ref, section_ref, keep_ref, give_ref, stage, semaphores):
     copies = Copies(semaphores)
     place = 0
     sources = [(p_ref[part].T, HEAD) for part in range(3)]
@@ -104,24 +105,21 @@
         for half in range(2):
             stage[half, place : place + rows] = value[half * rows : (half + 1) * rows]
         place += rows
-    for half in range(2):
-        stage[half, place:] = s_ref[half]
     section = section_ref[0]
     wait([copies.start(stage.at[1 - section], give_ref), copies.start(stage.at[section], keep_ref)])
 
 
-def pack(project_w, out_w, up_w, down_w, small, section):
+def pack(project_w, out_w, up_w, down_w, section):
     width = down_w.shape[1]
     rows = (project_w.shape[2] * 3 + out_w.shape[0] + up_w.shape[1] + down_w.shape[0]) // 2
-    rows += small.shape[1]
     return call(
         pack_kernel,
-        [IN_VMEM] * 5 + [IN_SMEM],
+        [IN_VMEM] * 4 + [IN_SMEM],
         [IN_HBM] * 2,
         [struct((rows, width), bf16)] * 2,
         scratch=[pltpu.VMEM((2, rows, width), bf16), pltpu.SemaphoreType.DMA((2,))],
         moved=8 * rows * width,
-    )(project_w, out_w, up_w, down_w, small, section)
+    )(project_w, out_w, up_w, down_w, section)
 
 
 def load_heads(copies, ref, first, parts, pairs, target):
@@ -355,27 +353,26 @@
     return jnp.concatenate(columns, axis=1)
 
 
-def project_back(first_ref, dq_ref, own_ref, got_ref, weight, loads):
-    pairs = dq_ref.shape[0]
-    wide = pairs * PAIR
-    total = first_ref[...].astype(f32)
-    for part in range(3):
-        if part == 0:
-            left = jnp.concatenate([dq_ref[pair] for pair in range(pairs)], axis=1)
-        else:
-            left = summed(own_ref, got_ref, part - 1)
-        wait(loads[part])
-        total += dot_nn(left, weight[part * wide : (part + 1) * wide])
-    return total
-
-
 def leave_kernel(p_first, extra, first_ref, dq_ref, own_ref, got_ref, pw_ref, rank_ref, *rest):
     if extra:
         prefix_ref, *rest = rest
-    (*out_refs, weight_p, low, semaphores) = rest
+    (*out_refs, weight_p, low, first, dq, own, got, semaphores) = rest
     copies = Copies(semaphores)
-    loads = load_heads(copies, pw_ref, p_first, 3, dq_ref.shape[0], weight_p)
-    low[...] = project_back(first_ref, dq_ref, own_ref, got_ref, weight_p, loads).astype(bf16)
+    pairs = dq.shape[0]
+    wide = pairs * PAIR
+    load_q = copies.start(dq_ref, dq)
+    loads = load_heads(copies, pw_ref, p_first, 3, pairs, weight_p)
+    others = [copies.start(own_ref, own), copies.start(got_ref, got)]
+    load_first = copies.start(first_ref, first)
+    load_q.wait()
+    wait(loads[0])
+    total = dot_nn(jnp.concatenate([dq[pair] for pair in range(pairs)], axis=1), weight_p[:wide])
+    wait(others)
+    for part in (1, 2):
+        wait(loads[part])
+        total += dot_nn(summed(own, got, part - 1), weight_p[part * wide : (part + 1) * wide])
+    load_first.wait()
+    low[...] = (total + first[...].astype(f32)).astype(bf16)
     rows = low.shape[0] // len(out_refs)
     for j, target in enumerate(out_refs):
         start = pl.multiple_of((rank_ref[0] ^ j) * rows, rows)
@@ -393,16 +390,21 @@
     more = [] if prefix is None else [prefix]
     return call(
         functools.partial(leave_kernel, p_table[1], len(more)),
-        [IN_VMEM] * 4 + [IN_HBM, IN_SMEM] + [IN_VMEM] * len(more),
+        [IN_ANY] * 4 + [IN_HBM, IN_SMEM] + [IN_VMEM] * len(more),
         [IN_VMEM] * blocks,
         [struct((count // blocks + 16 * len(more), width), bf16)] * blocks,
         scratch=[
             pltpu.VMEM((3 * pairs * PAIR, width), bf16),
             pltpu.VMEM((count, width), bf16),
-            pltpu.SemaphoreType.DMA((6 * pairs,)),
+            pltpu.VMEM((count, width), bf16),
+            pltpu.VMEM(dq.shape, bf16),
+            pltpu.VMEM(own.shape, bf16),
+            pltpu.VMEM(got.shape, bf16),
+            pltpu.SemaphoreType.DMA((6 * pairs + 4,)),
         ],
         flops=2 * count * width * 3 * PAIR * pairs,
         moved=2 * (count * width * 7 + 3 * width * PAIR * pairs),
+        vmem=28 * 1024 * 1024,
     )(first, dq, own, got, p_table[0][0], rank, *more)
 
 
@@ -812,6 +814,19 @@
     out_rows = output_weight[0].reshape(2, low_width, width)
     up_rows = jnp.transpose(up_weight[0], (1, 0)).reshape(2, hidden, width)
     down_rows = down_weight[0].reshape(2, hidden, width)
+    if quick:
+        keep, give = pack(
+            jnp.transpose(project_weight[0], (1, 0, 2)), output_weight[0], up_weight[0],
+            down_weight[0], section.astype(jnp.int32).reshape(1),
+        )
+        give, project_bias, up_bias, prefix_keys, prefix_values = lax.optimization_barrier(
+            (give, project_bias, up_bias, prefix_keys, prefix_values)
+        )
+    else:
+        packed = jnp.concatenate([project_rows, out_rows, up_rows, down_rows], axis=1)
+        keep = lax.dynamic_index_in_dim(packed, section, 0, keepdims=False)
+        give = lax.dynamic_index_in_dim(packed, 1 - section, 0, keepdims=False)
+    got = lax.ppermute(give, "section", swap)
     small = jnp.concatenate(
         [
             jnp.transpose(project_bias[0].reshape(3, 2, low_width), (1, 0, 2)).reshape(2, -1),
@@ -825,17 +840,12 @@
     small_rows = -(-small_size // (16 * width)) * 16
     small = jnp.pad(small, ((0, 0), (0, small_rows * width - small_size)))
     small = small.reshape(2, small_rows, width)
-    if quick:
-        keep, give = pack(
-            jnp.transpose(project_weight[0], (1, 0, 2)), output_weight[0], up_weight[0],
-            down_weight[0], small, section.astype(jnp.int32).reshape(1),
-        )
-    else:
-        packed = jnp.concatenate([project_rows, out_rows, up_rows, down_rows, small], axis=1)
-        keep = lax.dynamic_index_in_dim(packed, section, 0, keepdims=False)
-        give = lax.dynamic_index_in_dim(packed, 1 - section, 0, keepdims=False)
-    got = lax.ppermute(give, "section", swap)
-    layer_rows = [jnp.where(is_first, keep, got), jnp.where(is_first, got, keep)]
+    keep_small = jnp.where(is_first, small[0], small[1])
+    got_small = lax.ppermute(jnp.where(is_first, small[1], small[0]), "section", swap)
+    small_first = jnp.where(is_first, keep_small, got_small)
+    small_second = jnp.where(is_first, got_small, keep_small)
+    rows_first = lambda cut: jnp.where(is_first, keep[cut], got[cut])
+    rows_second = lambda cut: jnp.where(is_first, got[cut], keep[cut])
     sizes = [3 * low_width, low_width, hidden, hidden, small_rows]
     p_end, o_end, u_end, d_end, s_end = [sum(sizes[: i + 1]) for i in range(len(sizes))]
     plane = lax.axis_index("dp")
@@ -868,13 +878,12 @@
     smalls = []
     plane = lax.axis_index("dp")
     share = 3 * low_width // 2
+    projection = rows_second(slice(0, p_end))
     if quick:
-        projection = lax.dynamic_slice_in_dim(layer_rows[1][:p_end], plane * share, share, 0)
-    else:
-        projection = layer_rows[1][:p_end]
-    early_rows = [layer_rows[0][:d_end], projection, layer_rows[0][d_end:], layer_rows[1][d_end:]]
+        projection = jnp.where(plane == 0, projection[:share], projection[share:])
+    early_rows = [rows_first(slice(0, d_end)), projection, small_first, small_second]
     projection_rows = projection.shape[0]
-    late_rows = layer_rows[1][p_end:d_end]
+    late_rows = rows_second(slice(p_end, d_end))
     early = gather(early_rows)
     early, vectors[0], vectors[1], seg_q, seg_k, tokens = lax.optimization_barrier(
         (early, vectors[0], vectors[1], seg_q, seg_k, tokens)
@@ -951,9 +960,9 @@
         p_table, *others = tables[layer]
         p_bias, u_bias, pk, pv = smalls[layer]
         if quick and layer == 0:
-            cross = lax.dynamic_index_in_dim(
-                early[:, :, d_end : d_end + share], section, 0, keepdims=False
-            )
+            cross = lax.dynamic_slice(
+                early, (section, 0, d_end, 0), (1, pairs, share, width)
+            ).reshape(pairs, share, width)
             theirs = lax.ppermute(cross, "dp", swap)
         if quick and layer == 1:
             p_table = ((early, theirs, theirs_too), d_end)

time: 495 us -> 489 us (0.988)
  transfers between devices with their start and end apart: 31 -> 32, of which waited for: 12 -> 12; matrix products, arithmetic and copies ran while one was open for 8% -> 8% of each run, Pallas kernels for 30% -> 30%
where the time goes in v4:
time: 489 us; the launch traced here: 479 us
  Pallas kernels  194 us (40%)
  waiting for transfers between devices  170 us (35%)
  starting transfers between devices  47.6 us (10%)
  local copies, waits for them, and re-layouts  31.6 us (6%)
  other arithmetic  20.8 us (4%)
  between operations  14.8 us (3%)
    all_gather x2, waiting for transfers between devices, per_device(): lax.all_gather(jnp.concatenate(parts, axis=0), ('section', 'tensor'), axi...  123 us
    pallas_call x2, Pallas kernels, backward(): call(functools.partial(back_kernel, p_first, len(more), o_table[1], piece...  82.4 us
    pallas_call x2, Pallas kernels, feed(): call(functools.partial(feed_kernel, (o_table[1], pieces), len(arrays), bl...  43.2 us
    pallas_call x2, Pallas kernels, attend(): call(functools.partial(attend_kernel, prefix_count), [by_pair, pl.BlockSp...  39.9 us
    ppermute x8, waiting for transfers between devices, arrive(): parts.append(lax.ppermute(part, ('section', 'tensor'), route))  23 us
    pallas_call x2, Pallas kernels, project(): call(functools.partial(project_kernel, first), [IN_VMEM, IN_VMEM, IN_SMEM...  18.1 us
    ppermute x8, starting transfers between devices, arrive(): parts.append(lax.ppermute(part, ('section', 'tensor'), route))  13.9 us
    ppermute x8, waiting for transfers between devices, send_blocks(): got.append(lax.ppermute(part, ('section', 'tensor'), route))  13.6 us
  transfers between devices with their start and end apart: 32, of which 12 were waited for; matrix products, arithmetic and copies ran while one was open for 8% of the time, Pallas kernels for 30%

profile of v4, /device:TPU:0, one launch (start us, length us, event | category | flops | bytes accessed | tf_op | source)
XLA Modules:
  0.0 479.4 jit_solution(17167642483183138163)
XLA Ops:
  7.3 4.1 shard_map.148
  13.0 2.0 collective-permute-done.2
  16.4 1.4 pad_maximum_fusion.1
  17.9 3.8 broadcast_select_fusion
  21.7 1.3 copy.29
  23.6 2.5 copy.30
  26.2 3.2 bitcast_select_fusion
  30.4 2.6 collective-permute-start.6
  33.0 3.6 collective-permute-start.7
  36.6 1.6 collective-permute-start.5
  39.4 5.9 %collective-permute-done.6 = bf16[128,1024]{1,0:T(8,128)(2,1)} collective-permute-done((bf16[128,1024]{1,0:T(8,128)(2,1)}, bf16[128,1024]{1,0:T(8,128)(2,1)}, u32[]{:S(2)}, u32[]{:S(2)}) %collective-permute-start.6) | collective-permute-done | bytes 262176 | tf_op jit(solution)/shard_map/ppermute | solution.py:775
  45.4 6.2 %collective-permute-done.5 = bf16[128,1024]{1,0:T(8,128)(2,1)} collective-permute-done((bf16[128,1024]{1,0:T(8,128)(2,1)}, bf16[128,1024]{1,0:T(8,128)(2,1)}, u32[]{:S(2)}, u32[]{:S(2)}) %collective-permute-start.5) | collective-permute-done | bytes 262176 | tf_op jit(solution)/shard_map/ppermute | solution.py:775
  51.6 10.8 %collective-permute-done.4 = bf16[128,1024]{1,0:T(8,128)(2,1)} collective-permute-done((bf16[128,1024]{1,0:T(8,128)(2,1)S(1)}, bf16[128,1024]{1,0:T(8,128)(2,1)}, u32[]{:S(2)}, u32[]{:S(2)}) %collective-permute-start.4) | collective-permute-done | bytes 262176 | tf_op jit(solution)/shard_map/ppermute | solution.py:775
  62.4 1.3 broadcast_select_fusion.30
  65.9 119.9 %all-gather.5.cloned.1.call-done = bf16[14336,1024]{1,0:T(8,128)(2,1)} async-done(((bf16[896,1024]{1,0:T(8,128)(2,1)}), bf16[14336,1024]{1,0:T(8,128)(2,1)}) %all-gather.5.cloned.1.call-update) | async-done | bytes 29360144 | tf_op jit(solution)/shard_map/all_gather | solution.py:852
  186.4 2.1 fusion.3
  189.5 8.6 %shard_map.149 = (bf16[8,512,128]{2,1,0:T(8,128)(2,1)}, bf16[2,8,512,128]{3,2,1,0:T(8,128)(2,1)}) custom-call(bf16[512,1024]{1,0:T(8,128)(2,1)} %pad_maximum_fusion.2.x_ref, f32[3,1,1024]{2,1,0:T(1,128)} %reshape.169.b_ref, s32[2]{0:T(128)} %pad_add_fusion.1.place_ref, bf16[2,8,896,1024]{3,2,1,0:T(8,128)(2,1)} %bitcast.106), custom_call_target="tpu_custom_call" | custom-call | flops 3221225472 | bytes 10485760 | tf_op jit(solution)/shard_map/pallas_call | solution.py:217
  199.2 1.6 dynamic-slice_bitcast_fusion
  200.8 1.6 collective-permute-start.12
  205.3 20.1 %shard_map.150 = (bf16[8,512,128]{2,1,0:T(8,128)(2,1)}, bf16[8,2,1056,512]{3,2,1,0:T(8,128)(2,1)}, bf16[8,512,128]{2,1,0:T(8,128)(2,1)}) custom-call(bf16[8,512,128]{2,1,0:T(8,128)(2,1)} %get-tuple-element.81.q_ref.rest_17_, bf16[2,8,512,128]{3,2,1,0:T(8,128)(2,1)} %get-tuple-element.82.own_ref.rest_18_, ...), custom_call_target="tpu_custom_call" | custom-call | flops 4429185024 | bytes 17301504 | tf_op jit(solution)/shard_map/pallas_call | solution.py:466
  225.4 21.7 %shard_map.151 = (bf16[512,1024]{1,0:T(8,128)(2,1)}, bf16[512,1024]{1,0:T(8,128)(2,1)}, f32[512,1]{1,0:T(8,128)}, bf16[512,1024]{1,0:T(8,128)(2,1)}, f32[512,1]{1,0:T(8,128)}, /*index=5*/bf16[512,4096]{1,0:T(8,128)(2,1)}) custom-call(bf16[512,1024]{1,0:T(8,128)(2,1)} %pad_maximum_fusion.2.x_ref, bf16[8,512,128]{2,1,0:T(8,128)(2,1)} %get-tuple-element.85.mixed_ref.rest_14_, ...), custom_call_target="tpu_custom_call" | custom-call | flops 9663676416 | bytes 29360128 | tf_op jit(solution)/shard_map/pallas_call | solution.py:332
  247.2 2.5 reshape.162
  252.3 9.5 %shard_map.152 = (bf16[8,512,128]{2,1,0:T(8,128)(2,1)}, bf16[2,8,512,128]{3,2,1,0:T(8,128)(2,1)}) custom-call(bf16[512,1024]{1,0:T(8,128)(2,1)} %get-tuple-element.88.x_ref, f32[3,1,1024]{2,1,0:T(1,128)} %reshape.171.b_ref, s32[2]{0:T(128)} %pad_add_fusion.1.place_ref, bf16[2,8,896,1024]{3,2,1,0:T(8,128)(2,1)} %bitcast.110, bf16[8,96,1024]{2,1,0:T(8,128)(2,1)} %copy-done.3, ...), custom_call_target="tpu_custom_call" | custom-call | flops 3221225472 | bytes 10485760 | tf_op jit(solution)/shard_map/pallas_call | solution.py:217
  266.4 1.3 copy-done.19
  267.7 19.8 %shard_map.153 = (bf16[8,512,128]{2,1,0:T(8,128)(2,1)}, bf16[8,2,1056,512]{3,2,1,0:T(8,128)(2,1)}, bf16[8,512,128]{2,1,0:T(8,128)(2,1)}) custom-call(bf16[8,512,128]{2,1,0:T(8,128)(2,1)} %get-tuple-element.90.q_ref.rest_11_, bf16[2,8,512,128]{3,2,1,0:T(8,128)(2,1)} %get-tuple-element.91.own_ref.rest_12_, bf16[1,2,8,512,128]{4,3,2,1,0:T(8,128)(2,1)} %bitcast.152, ...), custom_call_target="tpu_custom_call" | custom-call | flops 4429185024 | bytes 17301504 | tf_op jit(solution)/shard_map/pallas_call | solution.py:466
  287.5 3.6 all-gather.7.cloned.1.call-done
  291.2 1.3 collective-permute-start.10
  293.4 3.4 collective-permute-start.9
  297.3 21.5 %shard_map.154 = (bf16[128,1024]{1,0:T(8,128)(2,1)}, bf16[128,1024]{1,0:T(8,128)(2,1)}, bf16[128,1024]{1,0:T(8,128)(2,1)}, bf16[128,1024]{1,0:T(8,128)(2,1)}, bf...) custom-call(bf16[512,1024]{1,0:T(8,128)(2,1)} %get-tuple-element.88., ...), custom_call_target="tpu_custom_call" | custom-call | flops 9663676416 | bytes 29360128 | tf_op jit(solution)/shard_map/pallas_call | solution.py:332
  319.9 38.0 %shard_map.155 = (bf16[512,1024]{1,0:T(8,128)(2,1)}, bf16[8,512,128]{2,1,0:T(8,128)(2,1)}, bf16[2,8,512,128]{3,2,1,0:T(8,128)(2,1)}, bf16[1,2,8,512,128]{4,3,2,1,0:T(8,128)(2,1)}, f32[8,64,128]{2,1,0:T(8,128)}) custom-call(s32[2]{0:T(128)} %pad_add_fusion.1.place_ref, bf16[512,1024]{1,0:T(8,128)(2,1)} %pad_maximum_fusion.3.rest_0_, ...), custom_call_target="tpu_custom_call" | custom-call | flops 21743271936 | bytes 59244544 | tf_op jit(solution)/shard_map/pallas_call | solution.py:676
  357.9 4.5 collective-permute-start.16
  362.4 1.7 collective-permute-start.17
  364.2 1.5 collective-permute-start.18
  366.2 1.5 collective-permute-start.20
  367.7 1.4 copy-done.7
  369.1 44.4 %shard_map.156 = (bf16[512,1024]{1,0:T(8,128)(2,1)}, bf16[8,512,128]{2,1,0:T(8,128)(2,1)}, bf16[2,8,512,128]{3,2,1,0:T(8,128)(2,1)}, bf16[1,2,8,512,128]{4,3,2,1,0:T(8,128)(2,1)}, f32[8,64,128]{2,1,0:T(8,128)}) custom-call(s32[2]{0:T(128)} %pad_add_fusion.1.place_ref, bf16[512,1024]{1,0:T(8,128)(2,1)} %get-tuple-element.100.rest_0_, ...), custom_call_target="tpu_custom_call" | custom-call | flops 21743271936 | bytes 59244544 | tf_op jit(solution)/shard_map/pallas_call | solution.py:676
  413.6 4.0 collective-permute-start.21
  418.8 2.9 collective-permute-done.22
  422.8 1.2 copy-done.1
  424.1 1.2 copy-done.2
  425.3 6.7 %shard_map.157 = (bf16[144,1024]{1,0:T(8,128)(2,1)S(1)}, bf16[144,1024]{1,0:T(8,128)(2,1)S(1)}, bf16[144,1024]{1,0:T(8,128)(2,1)S(1)}, bf16[144,1024]{1,0:T(8,128)(2,1)S(1)}) custom-call(bf16[512,1024]{1,0:T(8,128)(2,1)S(1)} %copy-done.1, bf16[8,512,128]{2,1,0:T(8,128)(2,1)S(1)} %copy-done.2, bf16[2,8,512,128]{3,2,1,0:T(8,128)(2,1)S(1)} %copy-done, ...), custom_call_target="tpu_custom_call" | custom-call | flops 3221225472 | bytes 13631488 | tf_op jit(solution)/shard_map/pallas_call | solution.py:391
  432.1 2.9 collective-permute-start.24
  436.4 4.6 collective-permute-done.23
  441.0 8.9 %collective-permute-done.24 = bf16[144,1024]{1,0:T(8,128)(2,1)S(1)} collective-permute-done((bf16[144,1024]{1,0:T(8,128)(2,1)S(1)}, bf16[144,1024]{1,0:T(8,128)(2,1)S(1)}, u32[]{:S(2)}, u32[]{:S(2)}) %collective-permute-start.24) | collective-permute-done | bytes 294944 | tf_op jit(solution)/shard_map/ppermute | solution.py:998
  450.3 11.2 %collective-permute-start.27 = (bf16[4,128,1024]{2,1,0:T(8,128)(2,1)S(1)}, bf16[4,128,1024]{2,1,0:T(8,128)(2,1)S(1)}, u32[]{:S(2)}, u32[]{:S(2)}) collective-permute-start(bf16[4,128,1024]{2,1,0:T(8,128)(2,1)S(1)} %broadcast_select_fusion.5), channel_id=1, source_target_pairs={{0,16},{16,0},{1,17},{17,1},{2,18},{18,2},{3,19},{19,3},{4,20},{20... | collective-permute-start | bytes 3145736 | tf_op jit(solution)/shard_map/ppermute | solution.py:1027
  462.1 3.7 collective-permute-done.28
  465.9 1.2 collective-permute-done.29
  468.9 3.5 copy.63
  (159 shorter events, 30.4 us)
Async XLA Ops:
  7.2 5.2 %copy-start.16 = (bf16[1,20,128]{2,1,0:T(8,128)(2,1)S(1)}, bf16[1,20,128]{2,1,0:T(8,128)(2,1)}, u32[]{:S(2)}) copy-start(bf16[1,20,128]{2,1,0:T(8,128)(2,1)} %param.25) | copy-start | bytes 15364
  7.2 5.0 %copy-start.15 = (bf16[1,20,128]{2,1,0:T(8,128)(2,1)S(1)}, bf16[1,20,128]{2,1,0:T(8,128)(2,1)}, u32[]{:S(2)}) copy-start(bf16[1,20,128]{2,1,0:T(8,128)(2,1)} %param.24) | copy-start | bytes 15364
  7.2 4.7 copy-start.17
  7.2 4.8 copy-start.18
  7.2 178.6 %all-gather.5.cloned.1.call-start = ((), (), s32[]{:S(2)}) async-start(), calls=%async_computation | async-start | bytes 31195136 | tf_op jit(solution)/shard_map/all_gather | solution.py:852
  11.4 4.9 %copy-start.5 = (bf16[768,1024]{1,0:T(8,128)(2,1)S(1)}, bf16[768,1024]{1,0:T(8,128)(2,1)}, u32[]{:S(2)}) copy-start(bf16[768,1024]{1,0:T(8,128)(2,1)} %get-tuple-element.71) | copy-start | bytes 4718596
  11.4 3.8 collective-permute-start.1
  12.9 2.2 collective-permute-start.2
  17.8 273.2 %all-gather.7.cloned.1.call-start = ((), (), s32[]{:S(2)}) async-start(), calls=%async_computation.1 | async-start | bytes 20054016 | tf_op jit(solution)/shard_map/all_gather | solution.py:852
  21.7 1.7 copy-start.12
  21.7 1.7 copy-start.13
  21.7 1.9 copy-start.10
  23.0 3.2 collective-permute-start
  23.4 15.4 %collective-permute-start.3 = (bf16[8,1024]{1,0:T(8,128)(2,1)S(1)}, bf16[8,1024]{1,0:T(8,128)(2,1)S(1)}, u32[]{:S(2)}, u32[]{:S(2)}) collective-permute-start(bf16[8,1024]{1,0:T(8,128)(2,1)S(1)} %pad_maximum_fusion.7), channel_id=1, source_target_pairs={{0,16},{16,0},{1,17},{17,1},{2,18},{18,2},{3,19},{19,3},{4,20},{20... | collective-permute-start | bytes 49160 | tf_op jit(solution)/shard_map/ppermute | solution.py:794
  26.2 12.0 %copy-start.14 = (s32[1,512]{1,0:T(1,128)}, s32[1,512]{1,0:T(1,128)S(1)}, u32[]{:S(2)}) copy-start(s32[1,512]{1,0:T(1,128)S(1)} %get-tuple-element.83.sq_ref) | copy-start | bytes 6148
  30.4 15.0 %collective-permute-start.6 = (bf16[128,1024]{1,0:T(8,128)(2,1)}, bf16[128,1024]{1,0:T(8,128)(2,1)}, u32[]{:S(2)}, u32[]{:S(2)}) collective-permute-start(bf16[128,1024]{1,0:T(8,128)(2,1)} %get-tuple-element.168), channel_id=1, source_target_pairs={{0,1},{1,0},{2,3},{3,2},{4,17},{5,16},{6,19},{7,18},{16,5},{17,4},... | collective-permute-start | bytes 786440 | tf_op jit(solution)/shard_map/ppermute | solution.py:775
  33.0 12.4 %collective-permute-start.7 = (bf16[128,1024]{1,0:T(8,128)(2,1)}, bf16[128,1024]{1,0:T(8,128)(2,1)}, u32[]{:S(2)}, u32[]{:S(2)}) collective-permute-start(bf16[128,1024]{1,0:T(8,128)(2,1)} %get-tuple-element.169), channel_id=1, source_target_pairs={{0,0},{1,1},{2,2},{3,3},{4,16},{5,17},{6,18},{7,19},{16,4},{17,5},... | collective-permute-start | bytes 786440 | tf_op jit(solution)/shard_map/ppermute | solution.py:775
  36.6 15.0 %collective-permute-start.5 = (bf16[128,1024]{1,0:T(8,128)(2,1)}, bf16[128,1024]{1,0:T(8,128)(2,1)}, u32[]{:S(2)}, u32[]{:S(2)}) collective-permute-start(bf16[128,1024]{1,0:T(8,128)(2,1)} %get-tuple-element.170), channel_id=1, source_target_pairs={{0,2},{1,3},{2,0},{3,1},{4,18},{5,19},{6,16},{7,17},{16,6},{17,7},... | collective-permute-start | bytes 786440 | tf_op jit(solution)/shard_map/ppermute | solution.py:775
  38.2 24.2 %collective-permute-start.4 = (bf16[128,1024]{1,0:T(8,128)(2,1)S(1)}, bf16[128,1024]{1,0:T(8,128)(2,1)}, u32[]{:S(2)}, u32[]{:S(2)}) collective-permute-start(bf16[128,1024]{1,0:T(8,128)(2,1)S(1)} %get-tuple-element.171), channel_id=1, source_target_pairs={{0,3},{1,2},{2,1},{3,0},{4,19},{5,18},{6,17},{7,16},{16,7},{17,6},... | collective-permute-start | bytes 786440 | tf_op jit(solution)/shard_map/ppermute | solution.py:775
  188.7 9.8 %copy-start.9 = (bf16[2,8,16384]{2,1,0:T(8,128)(2,1)}, bf16[2,8,16384]{2,1,0:T(8,128)(2,1)S(1)}, u32[]{:S(2)}) copy-start(bf16[2,8,16384]{2,1,0:T(8,128)(2,1)S(1)} %reshape.158) | copy-start | bytes 1572868
  198.1 7.2 %collective-permute-start.13 = (bf16[2,8,512,128]{3,2,1,0:T(8,128)(2,1)}, bf16[2,8,512,128]{3,2,1,0:T(8,128)(2,1)}, u32[]{:S(2)}, u32[]{:S(2)}) collective-permute-start(bf16[2,8,512,128]{3,2,1,0:T(8,128)(2,1)} %get-tuple-element.82.own_ref.rest_18_), channel_id=1, source_target_pairs={{0,16},{16,0},{1,17},{17,1},{2,18},{18,2},{3,19},{19,3},{4,20},{20... | collective-permute-start | bytes 6291464 | tf_op jit(solution)/shard_map/ppermute | solution.py:948
  200.8 46.3 %collective-permute-start.12 = (bf16[8,96,1024]{2,1,0:T(8,128)(2,1)S(1)}, bf16[8,96,1024]{2,1,0:T(8,128)(2,1)S(1)}, u32[]{:S(2)}, u32[]{:S(2)}) collective-permute-start(bf16[8,96,1024]{2,1,0:T(8,128)(2,1)S(1)} %dynamic-slice_bitcast_fusion), channel_id=1, source_target_pairs={{0,8},{8,0},{1,9},{9,1},{2,10},{10,2},{3,11},{11,3},{4,12},{12,4},... | collective-permute-start | bytes 4718600 | tf_op jit(solution)/shard_map/ppermute | solution.py:966
  247.1 4.1 copy-start.3
  247.1 4.1 collective-permute-start.14
  261.9 4.5 collective-permute-start.15
  267.7 23.4 %copy-start.6 = (bf16[4,128,1024]{2,1,0:T(8,128)(2,1)S(1)}, bf16[4,128,1024]{2,1,0:T(8,128)(2,1)}, u32[]{:S(2)}) copy-start(bf16[4,128,1024]{2,1,0:T(8,128)(2,1)} %get-tuple-element.78) | copy-start | bytes 3145732
  291.2 27.6 %collective-permute-start.10 = (bf16[128,1024]{1,0:T(8,128)(2,1)S(1)}, bf16[128,1024]{1,0:T(8,128)(2,1)S(1)}, u32[]{:S(2)}, u32[]{:S(2)}) collective-permute-start(bf16[128,1024]{1,0:T(8,128)(2,1)S(1)} %get-tuple-element.160), channel_id=1, source_target_pairs={{0,1},{1,0},{2,3},{3,2},{4,17},{5,16},{6,19},{7,18},{16,5},{17,4},... | collective-permute-start | bytes 786440 | tf_op jit(solution)/shard_map/ppermute | solution.py:775
  292.5 26.3 %collective-permute-start.11 = (bf16[128,1024]{1,0:T(8,128)(2,1)S(1)}, bf16[128,1024]{1,0:T(8,128)(2,1)S(1)}, u32[]{:S(2)}, u32[]{:S(2)}) collective-permute-start(bf16[128,1024]{1,0:T(8,128)(2,1)S(1)} %get-tuple-element.161), channel_id=1, source_target_pairs={{0,0},{1,1},{2,2},{3,3},{4,16},{5,17},{6,18},{7,19},{16,4},{17,5},... | collective-permute-start | bytes 786440 | tf_op jit(solution)/shard_map/ppermute | solution.py:775
  293.4 25.4 %collective-permute-start.9 = (bf16[128,1024]{1,0:T(8,128)(2,1)S(1)}, bf16[128,1024]{1,0:T(8,128)(2,1)S(1)}, u32[]{:S(2)}, u32[]{:S(2)}) collective-permute-start(bf16[128,1024]{1,0:T(8,128)(2,1)S(1)} %get-tuple-element.162), channel_id=1, source_target_pairs={{0,2},{1,3},{2,0},{3,1},{4,18},{5,19},{6,16},{7,17},{16,6},{17,7},... | collective-permute-start | bytes 786440 | tf_op jit(solution)/shard_map/ppermute | solution.py:775
  296.8 22.0 %collective-permute-start.8 = (bf16[128,1024]{1,0:T(8,128)(2,1)S(1)}, bf16[128,1024]{1,0:T(8,128)(2,1)S(1)}, u32[]{:S(2)}, u32[]{:S(2)}) collective-permute-start(bf16[128,1024]{1,0:T(8,128)(2,1)S(1)} %get-tuple-element.163), channel_id=1, source_target_pairs={{0,3},{1,2},{2,1},{3,0},{4,19},{5,18},{6,17},{7,16},{16,7},{17,6},... | collective-permute-start | bytes 786440 | tf_op jit(solution)/shard_map/ppermute | solution.py:775
  319.9 45.7 %copy-start.21 = (bf16[128,1024]{1,0:T(8,128)(2,1)S(1)}, bf16[128,1024]{1,0:T(8,128)(2,1)}, u32[]{:S(2)}) copy-start(bf16[128,1024]{1,0:T(8,128)(2,1)} %get-tuple-element.122) | copy-start | bytes 786436
  319.9 46.3 %copy-start.20 = (bf16[128,1024]{1,0:T(8,128)(2,1)S(1)}, bf16[128,1024]{1,0:T(8,128)(2,1)}, u32[]{:S(2)}) copy-start(bf16[128,1024]{1,0:T(8,128)(2,1)} %get-tuple-element.123) | copy-start | bytes 786436
  357.9 9.8 %collective-permute-start.16 = (bf16[2,8,512,128]{3,2,1,0:T(8,128)(2,1)}, bf16[2,8,512,128]{3,2,1,0:T(8,128)(2,1)S(1)}, u32[]{:S(2)}, u32[]{:S(2)}) collective-permute-start(bf16[2,8,512,128]{3,2,1,0:T(8,128)(2,1)} %bitcast.155), channel_id=1, source_target_pairs={{0,16},{16,0},{1,17},{17,1},{2,18},{18,2},{3,19},{19,3},{4,20},{20... | collective-permute-start | bytes 6291464 | tf_op jit(solution)/shard_map/ppermute | solution.py:948
  362.4 51.1 %collective-permute-start.17 = (bf16[128,1024]{1,0:T(8,128)(2,1)}, bf16[128,1024]{1,0:T(8,128)(2,1)S(1)}, u32[]{:S(2)}, u32[]{:S(2)}) collective-permute-start(bf16[128,1024]{1,0:T(8,128)(2,1)} %get-tuple-element.120), channel_id=1, source_target_pairs={{0,0},{1,1},{2,2},{3,3},{4,16},{5,17},{6,18},{7,19},{16,4},{17,5},... | collective-permute-start | bytes 786440 | tf_op jit(solution)/shard_map/ppermute | solution.py:998
  364.2 49.4 %collective-permute-start.18 = (bf16[128,1024]{1,0:T(8,128)(2,1)}, bf16[128,1024]{1,0:T(8,128)(2,1)S(1)}, u32[]{:S(2)}, u32[]{:S(2)}) collective-permute-start(bf16[128,1024]{1,0:T(8,128)(2,1)} %get-tuple-element.121), channel_id=1, source_target_pairs={{0,1},{1,0},{2,3},{3,2},{4,17},{5,16},{6,19},{7,18},{16,5},{17,4},... | collective-permute-start | bytes 786440 | tf_op jit(solution)/shard_map/ppermute | solution.py:998
  365.7 47.9 %collective-permute-start.19 = (bf16[128,1024]{1,0:T(8,128)(2,1)S(1)}, bf16[128,1024]{1,0:T(8,128)(2,1)S(1)}, u32[]{:S(2)}, u32[]{:S(2)}) collective-permute-start(bf16[128,1024]{1,0:T(8,128)(2,1)S(1)} %copy-done.21), channel_id=1, source_target_pairs={{0,2},{1,3},{2,0},{3,1},{4,18},{5,19},{6,16},{7,17},{16,6},{17,7},... | collective-permute-start | bytes 786440 | tf_op jit(solution)/shard_map/ppermute | solution.py:998
  366.2 47.4 %collective-permute-start.20 = (bf16[128,1024]{1,0:T(8,128)(2,1)S(1)}, bf16[128,1024]{1,0:T(8,128)(2,1)S(1)}, u32[]{:S(2)}, u32[]{:S(2)}) collective-permute-start(bf16[128,1024]{1,0:T(8,128)(2,1)S(1)} %copy-done.20), channel_id=1, source_target_pairs={{0,3},{1,2},{2,1},{3,0},{4,19},{5,18},{6,17},{7,16},{16,7},{17,6},... | collective-permute-start | bytes 786440 | tf_op jit(solution)/shard_map/ppermute | solution.py:998
  369.1 48.5 %copy-start.8 = (f32[8,64,128]{2,1,0:T(8,128)S(1)}, f32[8,64,128]{2,1,0:T(8,128)}, u32[]{:S(2)}) copy-start(f32[8,64,128]{2,1,0:T(8,128)} %get-tuple-element.126) | copy-start | bytes 786436
  413.5 9.3 %copy-start = (bf16[2,8,512,128]{3,2,1,0:T(8,128)(2,1)S(1)}, bf16[2,8,512,128]{3,2,1,0:T(8,128)(2,1)}, u32[]{:S(2)}) copy-start(bf16[2,8,512,128]{3,2,1,0:T(8,128)(2,1)} %get-tuple-element.118.own_ref) | copy-start | bytes 6291460
  413.6 9.2 %collective-permute-start.21 = (bf16[2,8,512,128]{3,2,1,0:T(8,128)(2,1)}, bf16[2,8,512,128]{3,2,1,0:T(8,128)(2,1)S(1)}, u32[]{:S(2)}, u32[]{:S(2)}) collective-permute-start(bf16[2,8,512,128]{3,2,1,0:T(8,128)(2,1)} %bitcast.154), channel_id=1, source_target_pairs={{0,16},{16,0},{1,17},{17,1},{2,18},{18,2},{3,19},{19,3},{4,20},{20... | collective-permute-start | bytes 6291464 | tf_op jit(solution)/shard_map/ppermute | solution.py:948
  418.6 3.2 collective-permute-start.22
  432.0 9.0 %collective-permute-start.23 = (bf16[144,1024]{1,0:T(8,128)(2,1)S(1)}, bf16[144,1024]{1,0:T(8,128)(2,1)S(1)}, u32[]{:S(2)}, u32[]{:S(2)}) collective-permute-start(bf16[144,1024]{1,0:T(8,128)(2,1)S(1)} %get-tuple-element.127), channel_id=1, source_target_pairs={{0,3},{1,2},{2,1},{3,0},{4,19},{5,18},{6,17},{7,16},{16,7},{17,6},... | collective-permute-start | bytes 884744 | tf_op jit(solution)/shard_map/ppermute | solution.py:998
  432.1 17.8 %collective-permute-start.24 = (bf16[144,1024]{1,0:T(8,128)(2,1)S(1)}, bf16[144,1024]{1,0:T(8,128)(2,1)S(1)}, u32[]{:S(2)}, u32[]{:S(2)}) collective-permute-start(bf16[144,1024]{1,0:T(8,128)(2,1)S(1)} %get-tuple-element.128), channel_id=1, source_target_pairs={{0,2},{1,3},{2,0},{3,1},{4,18},{5,19},{6,16},{7,17},{16,6},{17,7},... | collective-permute-start | bytes 884744 | tf_op jit(solution)/shard_map/ppermute | solution.py:998
  435.0 14.9 %collective-permute-start.25 = (bf16[144,1024]{1,0:T(8,128)(2,1)S(1)}, bf16[144,1024]{1,0:T(8,128)(2,1)S(1)}, u32[]{:S(2)}, u32[]{:S(2)}) collective-permute-start(bf16[144,1024]{1,0:T(8,128)(2,1)S(1)} %get-tuple-element.129), channel_id=1, source_target_pairs={{0,1},{1,0},{2,3},{3,2},{4,17},{5,16},{6,19},{7,18},{16,5},{17,4},... | collective-permute-start | bytes 884744 | tf_op jit(solution)/shard_map/ppermute | solution.py:998
  435.6 14.3 %collective-permute-start.26 = (bf16[144,1024]{1,0:T(8,128)(2,1)S(1)}, bf16[144,1024]{1,0:T(8,128)(2,1)S(1)}, u32[]{:S(2)}, u32[]{:S(2)}) collective-permute-start(bf16[144,1024]{1,0:T(8,128)(2,1)S(1)} %get-tuple-element.130), channel_id=1, source_target_pairs={{0,0},{1,1},{2,2},{3,3},{4,16},{5,17},{6,18},{7,19},{16,4},{17,5},... | collective-permute-start | bytes 884744 | tf_op jit(solution)/shard_map/ppermute | solution.py:998
  450.3 18.1 %collective-permute-start.27 = (bf16[4,128,1024]{2,1,0:T(8,128)(2,1)S(1)}, bf16[4,128,1024]{2,1,0:T(8,128)(2,1)S(1)}, u32[]{:S(2)}, u32[]{:S(2)}) collective-permute-start(bf16[4,128,1024]{2,1,0:T(8,128)(2,1)S(1)} %broadcast_select_fusion.5), channel_id=1, source_target_pairs={{0,16},{16,0},{1,17},{17,1},{2,18},{18,2},{3,19},{19,3},{4,20},{20... | collective-permute-start | bytes 3145736 | tf_op jit(solution)/shard_map/ppermute | solution.py:1027
  461.5 4.3 collective-permute-start.28
  465.8 1.3 collective-permute-start.29
  (6 other events, 7.9 us)
Sparse Core Ops, SparseCore 0:
  18.0 167.8 all-gather.4
  187.4 103.6 all-gather.6

commit v5 on v4

--- a/solution.py
+++ b/solution.py
@@ -773,9 +773,9 @@
                 ]
                 part = lax.dynamic_index_in_dim(rows_here, low_rank ^ j, 0, keepdims=False)
                 parts.append(lax.ppermute(part, ("section", "tensor"), route))
-            return jnp.concatenate(ordered(parts), axis=0)
-
-        tokens = arrive(jnp.where(is_first, keep, got))
+            return parts
+
+        tokens = jnp.concatenate(ordered(arrive(jnp.where(is_first, keep, got))), axis=0)
         cotangent_rows = jnp.where(is_first, got, keep)
     else:
         if chips > 1:
@@ -972,7 +972,7 @@
         mixed, raised, inverse = attend(q, own, other, pk, pv, prefix_count, seg_q, seg_k)
         saved.append((mixed, inverse, raised, q, own, other, pk, pv))
         if layer == 1 and quick:
-            cotangent = arrive(after(cotangent_rows, late))
+            cotangent = arrive(after(cotangent_rows, mixed))
         x, *kept = feed(
             x, mixed, others, vectors[layer], u_bias, order, out_blocks if layer else 0
         )
@@ -981,6 +981,9 @@
             theirs, x = lax.optimization_barrier((theirs, x))
             theirs_too = lax.ppermute(theirs, "section", swap)
     outs = x
+    if quick:
+        cotangent, outs = lax.optimization_barrier((cotangent, outs))
+        cotangent = jnp.concatenate(ordered(cotangent), axis=0)
     kept_0, kept_1 = (entry[-1] for entry in saved)
     saved = [entry[:-1] for entry in saved]
     first, dq, down, dother, prefix_1 = backward(

time: 489 us -> 488 us (level)
  waiting for transfers between devices: 170 us -> 164 us
  starting transfers between devices: 47.6 us -> 53 us
  transfers between devices with their start and end apart: 32 -> 32, of which waited for: 12 -> 11; matrix products, arithmetic and copies ran while one was open for 8% -> 8% of each run, Pallas kernels for 30% -> 30%
where the time goes in v5:
time: 488 us; the launch traced here: 479 us
  Pallas kernels  194 us (40%)
  waiting for transfers between devices  164 us (34%)
  starting transfers between devices  53 us (11%)
  local copies, waits for them, and re-layouts  31.6 us (6%)
  other arithmetic  20.8 us (4%)
  between operations  14.9 us (3%)
    all_gather x2, waiting for transfers between devices, per_device(): lax.all_gather(jnp.concatenate(parts, axis=0), ('section', 'tensor'), axi...  120 us
    pallas_call x2, Pallas kernels, backward(): call(functools.partial(back_kernel, p_first, len(more), o_table[1], piece...  82.4 us
    pallas_call x2, Pallas kernels, feed(): call(functools.partial(feed_kernel, (o_table[1], pieces), len(arrays), bl...  43.2 us
    pallas_call x2, Pallas kernels, attend(): call(functools.partial(attend_kernel, prefix_count), [by_pair, pl.BlockSp...  39.9 us
    ppermute x8, waiting for transfers between devices, arrive(): parts.append(lax.ppermute(part, ('section', 'tensor'), route))  23 us
    pallas_call x2, Pallas kernels, project(): call(functools.partial(project_kernel, first), [IN_VMEM, IN_VMEM, IN_SMEM...  18.1 us
    ppermute x8, starting transfers between devices, arrive(): parts.append(lax.ppermute(part, ('section', 'tensor'), route))  17.3 us
    ppermute x1, starting transfers between devices, per_device(): got = lax.ppermute(jnp.where(is_first, outs, grads), 'section', swap)  14.9 us
  transfers between devices with their start and end apart: 32, of which 11 were waited for; matrix products, arithmetic and copies ran while one was open for 8% of the time, Pallas kernels for 30%

profile of v5, /device:TPU:0, one launch (start us, length us, event | category | flops | bytes accessed | tf_op | source)
XLA Modules:
  0.0 478.6 jit_solution(3921018887694865290)
XLA Ops:
  7.3 4.1 shard_map.148
  13.0 2.0 collective-permute-done.2
  16.4 1.4 pad_maximum_fusion.1
  17.9 3.8 broadcast_select_fusion
  21.7 1.3 copy.29
  23.6 2.5 copy.30
  26.2 3.2 bitcast_select_fusion
  30.4 2.6 collective-permute-start.6
  33.0 3.6 collective-permute-start.7
  36.6 1.6 collective-permute-start.5
  39.4 5.9 %collective-permute-done.6 = bf16[128,1024]{1,0:T(8,128)(2,1)} collective-permute-done((bf16[128,1024]{1,0:T(8,128)(2,1)}, bf16[128,1024]{1,0:T(8,128)(2,1)}, u32[]{:S(2)}, u32[]{:S(2)}) %collective-permute-start.6) | collective-permute-done | bytes 262176 | tf_op jit(solution)/shard_map/ppermute | solution.py:775
  45.4 6.2 %collective-permute-done.5 = bf16[128,1024]{1,0:T(8,128)(2,1)} collective-permute-done((bf16[128,1024]{1,0:T(8,128)(2,1)}, bf16[128,1024]{1,0:T(8,128)(2,1)}, u32[]{:S(2)}, u32[]{:S(2)}) %collective-permute-start.5) | collective-permute-done | bytes 262176 | tf_op jit(solution)/shard_map/ppermute | solution.py:775
  51.6 10.8 %collective-permute-done.4 = bf16[128,1024]{1,0:T(8,128)(2,1)} collective-permute-done((bf16[128,1024]{1,0:T(8,128)(2,1)S(1)}, bf16[128,1024]{1,0:T(8,128)(2,1)}, u32[]{:S(2)}, u32[]{:S(2)}) %collective-permute-start.4) | collective-permute-done | bytes 262176 | tf_op jit(solution)/shard_map/ppermute | solution.py:775
  62.4 1.3 broadcast_select_fusion.30
  64.8 1.2 slice_select_fusion
  65.9 119.9 %all-gather.5.cloned.1.call-done = bf16[14336,1024]{1,0:T(8,128)(2,1)} async-done(((bf16[896,1024]{1,0:T(8,128)(2,1)}), bf16[14336,1024]{1,0:T(8,128)(2,1)}) %all-gather.5.cloned.1.call-update) | async-done | bytes 29360144 | tf_op jit(solution)/shard_map/all_gather | solution.py:852
  186.4 2.1 fusion.3
  189.5 8.6 %shard_map.149 = (bf16[8,512,128]{2,1,0:T(8,128)(2,1)}, bf16[2,8,512,128]{3,2,1,0:T(8,128)(2,1)}) custom-call(bf16[512,1024]{1,0:T(8,128)(2,1)} %pad_maximum_fusion.2.x_ref, f32[3,1,1024]{2,1,0:T(1,128)} %reshape.169.b_ref, s32[2]{0:T(128)} %pad_add_fusion.1.place_ref, bf16[2,8,896,1024]{3,2,1,0:T(8,128)(2,1)} %bitcast.106), custom_call_target="tpu_custom_call" | custom-call | flops 3221225472 | bytes 10485760 | tf_op jit(solution)/shard_map/pallas_call | solution.py:217
  199.2 1.6 dynamic-slice_bitcast_fusion
  200.8 1.6 collective-permute-start.8
  205.3 20.1 %shard_map.150 = (bf16[8,512,128]{2,1,0:T(8,128)(2,1)}, bf16[8,2,1056,512]{3,2,1,0:T(8,128)(2,1)}, bf16[8,512,128]{2,1,0:T(8,128)(2,1)}) custom-call(bf16[8,512,128]{2,1,0:T(8,128)(2,1)} %get-tuple-element.86.q_ref.rest_17_, bf16[2,8,512,128]{3,2,1,0:T(8,128)(2,1)} %get-tuple-element.87.own_ref.rest_18_, ...), custom_call_target="tpu_custom_call" | custom-call | flops 4429185024 | bytes 17301504 | tf_op jit(solution)/shard_map/pallas_call | solution.py:466
  225.4 21.7 %shard_map.151 = (bf16[512,1024]{1,0:T(8,128)(2,1)}, bf16[512,1024]{1,0:T(8,128)(2,1)}, f32[512,1]{1,0:T(8,128)}, bf16[512,1024]{1,0:T(8,128)(2,1)}, f32[512,1]{1,0:T(8,128)}, /*index=5*/bf16[512,4096]{1,0:T(8,128)(2,1)}) custom-call(bf16[512,1024]{1,0:T(8,128)(2,1)} %pad_maximum_fusion.2.x_ref, bf16[8,512,128]{2,1,0:T(8,128)(2,1)} %get-tuple-element.90.mixed_ref.rest_14_, ...), custom_call_target="tpu_custom_call" | custom-call | flops 9663676416 | bytes 29360128 | tf_op jit(solution)/shard_map/pallas_call | solution.py:332
  247.2 2.5 reshape.161
  252.3 9.5 %shard_map.152 = (bf16[8,512,128]{2,1,0:T(8,128)(2,1)}, bf16[2,8,512,128]{3,2,1,0:T(8,128)(2,1)}) custom-call(bf16[512,1024]{1,0:T(8,128)(2,1)} %get-tuple-element.93.x_ref, f32[3,1,1024]{2,1,0:T(1,128)} %reshape.171.b_ref, s32[2]{0:T(128)} %pad_add_fusion.1.place_ref, bf16[2,8,896,1024]{3,2,1,0:T(8,128)(2,1)} %bitcast.110, bf16[8,96,1024]{2,1,0:T(8,128)(2,1)} %copy-done.3, ...), custom_call_target="tpu_custom_call" | custom-call | flops 3221225472 | bytes 10485760 | tf_op jit(solution)/shard_map/pallas_call | solution.py:217
  266.4 1.3 copy-done.19
  267.7 19.8 %shard_map.153 = (bf16[8,512,128]{2,1,0:T(8,128)(2,1)}, bf16[8,2,1056,512]{3,2,1,0:T(8,128)(2,1)}, bf16[8,512,128]{2,1,0:T(8,128)(2,1)}) custom-call(bf16[8,512,128]{2,1,0:T(8,128)(2,1)} %get-tuple-element.95.q_ref.rest_11_, bf16[2,8,512,128]{3,2,1,0:T(8,128)(2,1)} %get-tuple-element.96.own_ref.rest_12_, bf16[1,2,8,512,128]{4,3,2,1,0:T(8,128)(2,1)} %bitcast.152, ...), custom_call_target="tpu_custom_call" | custom-call | flops 4429185024 | bytes 17301504 | tf_op jit(solution)/shard_map/pallas_call | solution.py:466
  287.6 7.7 %collective-permute-start.15 = (bf16[128,1024]{1,0:T(8,128)(2,1)S(1)}, bf16[128,1024]{1,0:T(8,128)(2,1)S(1)}, u32[]{:S(2)}, u32[]{:S(2)}) collective-permute-start(bf16[128,1024]{1,0:T(8,128)(2,1)S(1)} %get-tuple-element.176), channel_id=1, source_target_pairs={{0,3},{1,2},{2,1},{3,0},{4,19},{5,18},{6,17},{7,16},{16,7},{17,6},... | collective-permute-start | bytes 786440 | tf_op jit(solution)/shard_map/ppermute | solution.py:775
  297.1 21.5 %shard_map.154 = (bf16[128,1024]{1,0:T(8,128)(2,1)}, bf16[128,1024]{1,0:T(8,128)(2,1)}, bf16[128,1024]{1,0:T(8,128)(2,1)}, bf16[128,1024]{1,0:T(8,128)(2,1)}, bf...) custom-call(bf16[512,1024]{1,0:T(8,128)(2,1)} %get-tuple-element.93., ...), custom_call_target="tpu_custom_call" | custom-call | flops 9663676416 | bytes 29360128 | tf_op jit(solution)/shard_map/pallas_call | solution.py:332
  319.8 38.0 %shard_map.155 = (bf16[512,1024]{1,0:T(8,128)(2,1)}, bf16[8,512,128]{2,1,0:T(8,128)(2,1)}, bf16[2,8,512,128]{3,2,1,0:T(8,128)(2,1)}, bf16[1,2,8,512,128]{4,3,2,1,0:T(8,128)(2,1)}, f32[8,64,128]{2,1,0:T(8,128)}) custom-call(s32[2]{0:T(128)} %pad_add_fusion.1.place_ref, bf16[512,1024]{1,0:T(8,128)(2,1)} %pad_maximum_fusion.3.rest_0_, ...), custom_call_target="tpu_custom_call" | custom-call | flops 21743271936 | bytes 59244544 | tf_op jit(solution)/shard_map/pallas_call | solution.py:676
  357.8 2.8 collective-permute-start.16
  360.5 1.7 collective-permute-start.17
  362.3 1.5 collective-permute-start.18
  363.8 2.3 collective-permute-start.19
  366.6 1.4 copy-done.7
  368.0 44.4 %shard_map.156 = (bf16[512,1024]{1,0:T(8,128)(2,1)}, bf16[8,512,128]{2,1,0:T(8,128)(2,1)}, bf16[2,8,512,128]{3,2,1,0:T(8,128)(2,1)}, bf16[1,2,8,512,128]{4,3,2,1,0:T(8,128)(2,1)}, f32[8,64,128]{2,1,0:T(8,128)}) custom-call(s32[2]{0:T(128)} %pad_add_fusion.1.place_ref, bf16[512,1024]{1,0:T(8,128)(2,1)} %get-tuple-element.116.rest_0_, ...), custom_call_target="tpu_custom_call" | custom-call | flops 21743271936 | bytes 59244544 | tf_op jit(solution)/shard_map/pallas_call | solution.py:676
  412.5 3.3 collective-permute-start.21
  417.0 2.9 collective-permute-done.22
  421.0 1.2 copy-done.1
  422.3 1.2 copy-done.2
  423.5 6.7 %shard_map.157 = (bf16[144,1024]{1,0:T(8,128)(2,1)S(1)}, bf16[144,1024]{1,0:T(8,128)(2,1)S(1)}, bf16[144,1024]{1,0:T(8,128)(2,1)S(1)}, bf16[144,1024]{1,0:T(8,128)(2,1)S(1)}) custom-call(bf16[512,1024]{1,0:T(8,128)(2,1)S(1)} %copy-done.1, bf16[8,512,128]{2,1,0:T(8,128)(2,1)S(1)} %copy-done.2, bf16[2,8,512,128]{3,2,1,0:T(8,128)(2,1)S(1)} %copy-done, ...), custom_call_target="tpu_custom_call" | custom-call | flops 3221225472 | bytes 13631488 | tf_op jit(solution)/shard_map/pallas_call | solution.py:391
  430.2 1.4 collective-permute-start.23
  431.6 1.5 collective-permute-start.24
  434.6 4.6 collective-permute-done.23
  439.2 6.2 %collective-permute-done.24 = bf16[144,1024]{1,0:T(8,128)(2,1)S(1)} collective-permute-done((bf16[144,1024]{1,0:T(8,128)(2,1)S(1)}, bf16[144,1024]{1,0:T(8,128)(2,1)S(1)}, u32[]{:S(2)}, u32[]{:S(2)}) %collective-permute-start.24) | collective-permute-done | bytes 294944 | tf_op jit(solution)/shard_map/ppermute | solution.py:1001
  445.8 14.9 %collective-permute-start.27 = (bf16[4,128,1024]{2,1,0:T(8,128)(2,1)S(1)}, bf16[4,128,1024]{2,1,0:T(8,128)(2,1)S(1)}, u32[]{:S(2)}, u32[]{:S(2)}) collective-permute-start(bf16[4,128,1024]{2,1,0:T(8,128)(2,1)S(1)} %broadcast_select_fusion.5), channel_id=1, source_target_pairs={{0,16},{16,0},{1,17},{17,1},{2,18},{18,2},{3,19},{19,3},{4,20},{20... | collective-permute-start | bytes 3145736 | tf_op jit(solution)/shard_map/ppermute | solution.py:1030
  461.3 3.7 collective-permute-done.28
  465.1 1.2 collective-permute-done.29
  468.1 3.5 copy.63
  (159 shorter events, 29.7 us)
Async XLA Ops:
  7.2 5.2 %copy-start.16 = (bf16[1,20,128]{2,1,0:T(8,128)(2,1)S(1)}, bf16[1,20,128]{2,1,0:T(8,128)(2,1)}, u32[]{:S(2)}) copy-start(bf16[1,20,128]{2,1,0:T(8,128)(2,1)} %param.25) | copy-start | bytes 15364
  7.2 5.0 %copy-start.15 = (bf16[1,20,128]{2,1,0:T(8,128)(2,1)S(1)}, bf16[1,20,128]{2,1,0:T(8,128)(2,1)}, u32[]{:S(2)}) copy-start(bf16[1,20,128]{2,1,0:T(8,128)(2,1)} %param.24) | copy-start | bytes 15364
  7.2 4.7 copy-start.17
  7.2 4.8 copy-start.18
  7.2 178.6 %all-gather.5.cloned.1.call-start = ((), (), s32[]{:S(2)}) async-start(), calls=%async_computation | async-start | bytes 31195136 | tf_op jit(solution)/shard_map/all_gather | solution.py:852
  11.4 4.9 %copy-start.5 = (bf16[768,1024]{1,0:T(8,128)(2,1)S(1)}, bf16[768,1024]{1,0:T(8,128)(2,1)}, u32[]{:S(2)}) copy-start(bf16[768,1024]{1,0:T(8,128)(2,1)} %get-tuple-element.77) | copy-start | bytes 4718596
  11.4 3.8 collective-permute-start.1
  12.9 2.2 collective-permute-start.2
  17.8 279.3 %all-gather.7.cloned.1.call-start = ((), (), s32[]{:S(2)}) async-start(), calls=%async_computation.1 | async-start | bytes 20054016 | tf_op jit(solution)/shard_map/all_gather | solution.py:852
  21.7 1.7 copy-start.12
  21.7 1.7 copy-start.13
  21.7 1.9 copy-start.10
  23.0 3.2 collective-permute-start
  23.4 15.4 %collective-permute-start.3 = (bf16[8,1024]{1,0:T(8,128)(2,1)S(1)}, bf16[8,1024]{1,0:T(8,128)(2,1)S(1)}, u32[]{:S(2)}, u32[]{:S(2)}) collective-permute-start(bf16[8,1024]{1,0:T(8,128)(2,1)S(1)} %pad_maximum_fusion.7), channel_id=1, source_target_pairs={{0,16},{16,0},{1,17},{17,1},{2,18},{18,2},{3,19},{19,3},{4,20},{20... | collective-permute-start | bytes 49160 | tf_op jit(solution)/shard_map/ppermute | solution.py:794
  26.2 12.0 %copy-start.14 = (s32[1,512]{1,0:T(1,128)}, s32[1,512]{1,0:T(1,128)S(1)}, u32[]{:S(2)}) copy-start(s32[1,512]{1,0:T(1,128)S(1)} %get-tuple-element.88.sq_ref) | copy-start | bytes 6148
  30.4 15.0 %collective-permute-start.6 = (bf16[128,1024]{1,0:T(8,128)(2,1)}, bf16[128,1024]{1,0:T(8,128)(2,1)}, u32[]{:S(2)}, u32[]{:S(2)}) collective-permute-start(bf16[128,1024]{1,0:T(8,128)(2,1)} %get-tuple-element.184), channel_id=1, source_target_pairs={{0,1},{1,0},{2,3},{3,2},{4,17},{5,16},{6,19},{7,18},{16,5},{17,4},... | collective-permute-start | bytes 786440 | tf_op jit(solution)/shard_map/ppermute | solution.py:775
  33.0 12.4 %collective-permute-start.7 = (bf16[128,1024]{1,0:T(8,128)(2,1)}, bf16[128,1024]{1,0:T(8,128)(2,1)}, u32[]{:S(2)}, u32[]{:S(2)}) collective-permute-start(bf16[128,1024]{1,0:T(8,128)(2,1)} %get-tuple-element.185), channel_id=1, source_target_pairs={{0,0},{1,1},{2,2},{3,3},{4,16},{5,17},{6,18},{7,19},{16,4},{17,5},... | collective-permute-start | bytes 786440 | tf_op jit(solution)/shard_map/ppermute | solution.py:775
  36.6 15.0 %collective-permute-start.5 = (bf16[128,1024]{1,0:T(8,128)(2,1)}, bf16[128,1024]{1,0:T(8,128)(2,1)}, u32[]{:S(2)}, u32[]{:S(2)}) collective-permute-start(bf16[128,1024]{1,0:T(8,128)(2,1)} %get-tuple-element.186), channel_id=1, source_target_pairs={{0,2},{1,3},{2,0},{3,1},{4,18},{5,19},{6,16},{7,17},{16,6},{17,7},... | collective-permute-start | bytes 786440 | tf_op jit(solution)/shard_map/ppermute | solution.py:775
  38.2 24.2 %collective-permute-start.4 = (bf16[128,1024]{1,0:T(8,128)(2,1)S(1)}, bf16[128,1024]{1,0:T(8,128)(2,1)}, u32[]{:S(2)}, u32[]{:S(2)}) collective-permute-start(bf16[128,1024]{1,0:T(8,128)(2,1)S(1)} %get-tuple-element.187), channel_id=1, source_target_pairs={{0,3},{1,2},{2,1},{3,0},{4,19},{5,18},{6,17},{7,16},{16,7},{17,6},... | collective-permute-start | bytes 786440 | tf_op jit(solution)/shard_map/ppermute | solution.py:775
  188.7 9.8 %copy-start.9 = (bf16[2,8,16384]{2,1,0:T(8,128)(2,1)}, bf16[2,8,16384]{2,1,0:T(8,128)(2,1)S(1)}, u32[]{:S(2)}) copy-start(bf16[2,8,16384]{2,1,0:T(8,128)(2,1)S(1)} %reshape.157) | copy-start | bytes 1572868
  198.1 7.2 %collective-permute-start.9 = (bf16[2,8,512,128]{3,2,1,0:T(8,128)(2,1)}, bf16[2,8,512,128]{3,2,1,0:T(8,128)(2,1)}, u32[]{:S(2)}, u32[]{:S(2)}) collective-permute-start(bf16[2,8,512,128]{3,2,1,0:T(8,128)(2,1)} %get-tuple-element.87.own_ref.rest_18_), channel_id=1, source_target_pairs={{0,16},{16,0},{1,17},{17,1},{2,18},{18,2},{3,19},{19,3},{4,20},{20... | collective-permute-start | bytes 6291464 | tf_op jit(solution)/shard_map/ppermute | solution.py:948
  200.8 46.3 %collective-permute-start.8 = (bf16[8,96,1024]{2,1,0:T(8,128)(2,1)S(1)}, bf16[8,96,1024]{2,1,0:T(8,128)(2,1)S(1)}, u32[]{:S(2)}, u32[]{:S(2)}) collective-permute-start(bf16[8,96,1024]{2,1,0:T(8,128)(2,1)S(1)} %dynamic-slice_bitcast_fusion), channel_id=1, source_target_pairs={{0,8},{8,0},{1,9},{9,1},{2,10},{10,2},{3,11},{11,3},{4,12},{12,4},... | collective-permute-start | bytes 4718600 | tf_op jit(solution)/shard_map/ppermute | solution.py:966
  247.1 4.1 copy-start.3
  247.1 4.1 collective-permute-start.10
  261.9 4.5 collective-permute-start.11
  267.7 19.8 %copy-start.6 = (bf16[4,128,1024]{2,1,0:T(8,128)(2,1)S(1)}, bf16[4,128,1024]{2,1,0:T(8,128)(2,1)}, u32[]{:S(2)}) copy-start(bf16[4,128,1024]{2,1,0:T(8,128)(2,1)} %get-tuple-element.98) | copy-start | bytes 3145732
  287.6 31.1 %collective-permute-start.15 = (bf16[128,1024]{1,0:T(8,128)(2,1)S(1)}, bf16[128,1024]{1,0:T(8,128)(2,1)S(1)}, u32[]{:S(2)}, u32[]{:S(2)}) collective-permute-start(bf16[128,1024]{1,0:T(8,128)(2,1)S(1)} %get-tuple-element.176), channel_id=1, source_target_pairs={{0,3},{1,2},{2,1},{3,0},{4,19},{5,18},{6,17},{7,16},{16,7},{17,6},... | collective-permute-start | bytes 786440 | tf_op jit(solution)/shard_map/ppermute | solution.py:775
  295.3 23.4 %collective-permute-start.14 = (bf16[128,1024]{1,0:T(8,128)(2,1)S(1)}, bf16[128,1024]{1,0:T(8,128)(2,1)S(1)}, u32[]{:S(2)}, u32[]{:S(2)}) collective-permute-start(bf16[128,1024]{1,0:T(8,128)(2,1)S(1)} %get-tuple-element.177), channel_id=1, source_target_pairs={{0,2},{1,3},{2,0},{3,1},{4,18},{5,19},{6,16},{7,17},{16,6},{17,7},... | collective-permute-start | bytes 786440 | tf_op jit(solution)/shard_map/ppermute | solution.py:775
  295.3 23.4 %collective-permute-start.13 = (bf16[128,1024]{1,0:T(8,128)(2,1)S(1)}, bf16[128,1024]{1,0:T(8,128)(2,1)S(1)}, u32[]{:S(2)}, u32[]{:S(2)}) collective-permute-start(bf16[128,1024]{1,0:T(8,128)(2,1)S(1)} %get-tuple-element.178), channel_id=1, source_target_pairs={{0,1},{1,0},{2,3},{3,2},{4,17},{5,16},{6,19},{7,18},{16,5},{17,4},... | collective-permute-start | bytes 786440 | tf_op jit(solution)/shard_map/ppermute | solution.py:775
  296.2 22.5 %collective-permute-start.12 = (bf16[128,1024]{1,0:T(8,128)(2,1)S(1)}, bf16[128,1024]{1,0:T(8,128)(2,1)S(1)}, u32[]{:S(2)}, u32[]{:S(2)}) collective-permute-start(bf16[128,1024]{1,0:T(8,128)(2,1)S(1)} %get-tuple-element.179), channel_id=1, source_target_pairs={{0,0},{1,1},{2,2},{3,3},{4,16},{5,17},{6,18},{7,19},{16,4},{17,5},... | collective-permute-start | bytes 786440 | tf_op jit(solution)/shard_map/ppermute | solution.py:775
  319.8 44.0 %copy-start.21 = (bf16[128,1024]{1,0:T(8,128)(2,1)S(1)}, bf16[128,1024]{1,0:T(8,128)(2,1)}, u32[]{:S(2)}) copy-start(bf16[128,1024]{1,0:T(8,128)(2,1)} %get-tuple-element.138) | copy-start | bytes 786436
  319.8 46.3 %copy-start.20 = (bf16[128,1024]{1,0:T(8,128)(2,1)S(1)}, bf16[128,1024]{1,0:T(8,128)(2,1)}, u32[]{:S(2)}) copy-start(bf16[128,1024]{1,0:T(8,128)(2,1)} %get-tuple-element.139) | copy-start | bytes 786436
  357.8 8.9 %collective-permute-start.16 = (bf16[2,8,512,128]{3,2,1,0:T(8,128)(2,1)}, bf16[2,8,512,128]{3,2,1,0:T(8,128)(2,1)S(1)}, u32[]{:S(2)}, u32[]{:S(2)}) collective-permute-start(bf16[2,8,512,128]{3,2,1,0:T(8,128)(2,1)} %bitcast.155), channel_id=1, source_target_pairs={{0,16},{16,0},{1,17},{17,1},{2,18},{18,2},{3,19},{19,3},{4,20},{20... | collective-permute-start | bytes 6291464 | tf_op jit(solution)/shard_map/ppermute | solution.py:948
  360.5 51.9 %collective-permute-start.17 = (bf16[128,1024]{1,0:T(8,128)(2,1)}, bf16[128,1024]{1,0:T(8,128)(2,1)S(1)}, u32[]{:S(2)}, u32[]{:S(2)}) collective-permute-start(bf16[128,1024]{1,0:T(8,128)(2,1)} %get-tuple-element.136), channel_id=1, source_target_pairs={{0,0},{1,1},{2,2},{3,3},{4,16},{5,17},{6,18},{7,19},{16,4},{17,5},... | collective-permute-start | bytes 786440 | tf_op jit(solution)/shard_map/ppermute | solution.py:1001
  362.3 50.2 %collective-permute-start.18 = (bf16[128,1024]{1,0:T(8,128)(2,1)}, bf16[128,1024]{1,0:T(8,128)(2,1)S(1)}, u32[]{:S(2)}, u32[]{:S(2)}) collective-permute-start(bf16[128,1024]{1,0:T(8,128)(2,1)} %get-tuple-element.137), channel_id=1, source_target_pairs={{0,1},{1,0},{2,3},{3,2},{4,17},{5,16},{6,19},{7,18},{16,5},{17,4},... | collective-permute-start | bytes 786440 | tf_op jit(solution)/shard_map/ppermute | solution.py:1001
  363.8 48.7 %collective-permute-start.19 = (bf16[128,1024]{1,0:T(8,128)(2,1)S(1)}, bf16[128,1024]{1,0:T(8,128)(2,1)S(1)}, u32[]{:S(2)}, u32[]{:S(2)}) collective-permute-start(bf16[128,1024]{1,0:T(8,128)(2,1)S(1)} %copy-done.21), channel_id=1, source_target_pairs={{0,2},{1,3},{2,0},{3,1},{4,18},{5,19},{6,16},{7,17},{16,6},{17,7},... | collective-permute-start | bytes 786440 | tf_op jit(solution)/shard_map/ppermute | solution.py:1001
  366.1 46.3 %collective-permute-start.20 = (bf16[128,1024]{1,0:T(8,128)(2,1)S(1)}, bf16[128,1024]{1,0:T(8,128)(2,1)S(1)}, u32[]{:S(2)}, u32[]{:S(2)}) collective-permute-start(bf16[128,1024]{1,0:T(8,128)(2,1)S(1)} %copy-done.20), channel_id=1, source_target_pairs={{0,3},{1,2},{2,1},{3,0},{4,19},{5,18},{6,17},{7,16},{16,7},{17,6},... | collective-permute-start | bytes 786440 | tf_op jit(solution)/shard_map/ppermute | solution.py:1001
  368.0 47.8 %copy-start.8 = (f32[8,64,128]{2,1,0:T(8,128)S(1)}, f32[8,64,128]{2,1,0:T(8,128)}, u32[]{:S(2)}) copy-start(f32[8,64,128]{2,1,0:T(8,128)} %get-tuple-element.142) | copy-start | bytes 786436
  412.4 8.6 %copy-start = (bf16[2,8,512,128]{3,2,1,0:T(8,128)(2,1)S(1)}, bf16[2,8,512,128]{3,2,1,0:T(8,128)(2,1)}, u32[]{:S(2)}) copy-start(bf16[2,8,512,128]{3,2,1,0:T(8,128)(2,1)} %get-tuple-element.134.own_ref) | copy-start | bytes 6291460
  412.5 8.5 %collective-permute-start.21 = (bf16[2,8,512,128]{3,2,1,0:T(8,128)(2,1)}, bf16[2,8,512,128]{3,2,1,0:T(8,128)(2,1)S(1)}, u32[]{:S(2)}, u32[]{:S(2)}) collective-permute-start(bf16[2,8,512,128]{3,2,1,0:T(8,128)(2,1)} %bitcast.154), channel_id=1, source_target_pairs={{0,16},{16,0},{1,17},{17,1},{2,18},{18,2},{3,19},{19,3},{4,20},{20... | collective-permute-start | bytes 6291464 | tf_op jit(solution)/shard_map/ppermute | solution.py:948
  416.8 3.2 collective-permute-start.22
  430.2 9.0 %collective-permute-start.23 = (bf16[144,1024]{1,0:T(8,128)(2,1)S(1)}, bf16[144,1024]{1,0:T(8,128)(2,1)S(1)}, u32[]{:S(2)}, u32[]{:S(2)}) collective-permute-start(bf16[144,1024]{1,0:T(8,128)(2,1)S(1)} %get-tuple-element.143), channel_id=1, source_target_pairs={{0,3},{1,2},{2,1},{3,0},{4,19},{5,18},{6,17},{7,16},{16,7},{17,6},... | collective-permute-start | bytes 884744 | tf_op jit(solution)/shard_map/ppermute | solution.py:1001
  431.6 13.8 %collective-permute-start.24 = (bf16[144,1024]{1,0:T(8,128)(2,1)S(1)}, bf16[144,1024]{1,0:T(8,128)(2,1)S(1)}, u32[]{:S(2)}, u32[]{:S(2)}) collective-permute-start(bf16[144,1024]{1,0:T(8,128)(2,1)S(1)} %get-tuple-element.144), channel_id=1, source_target_pairs={{0,2},{1,3},{2,0},{3,1},{4,18},{5,19},{6,16},{7,17},{16,6},{17,7},... | collective-permute-start | bytes 884744 | tf_op jit(solution)/shard_map/ppermute | solution.py:1001
  433.2 12.3 %collective-permute-start.25 = (bf16[144,1024]{1,0:T(8,128)(2,1)S(1)}, bf16[144,1024]{1,0:T(8,128)(2,1)S(1)}, u32[]{:S(2)}, u32[]{:S(2)}) collective-permute-start(bf16[144,1024]{1,0:T(8,128)(2,1)S(1)} %get-tuple-element.145), channel_id=1, source_target_pairs={{0,1},{1,0},{2,3},{3,2},{4,17},{5,16},{6,19},{7,18},{16,5},{17,4},... | collective-permute-start | bytes 884744 | tf_op jit(solution)/shard_map/ppermute | solution.py:1001
  433.8 11.7 %collective-permute-start.26 = (bf16[144,1024]{1,0:T(8,128)(2,1)S(1)}, bf16[144,1024]{1,0:T(8,128)(2,1)S(1)}, u32[]{:S(2)}, u32[]{:S(2)}) collective-permute-start(bf16[144,1024]{1,0:T(8,128)(2,1)S(1)} %get-tuple-element.146), channel_id=1, source_target_pairs={{0,0},{1,1},{2,2},{3,3},{4,16},{5,17},{6,18},{7,19},{16,4},{17,5},... | collective-permute-start | bytes 884744 | tf_op jit(solution)/shard_map/ppermute | solution.py:1001
  445.8 21.8 %collective-permute-start.27 = (bf16[4,128,1024]{2,1,0:T(8,128)(2,1)S(1)}, bf16[4,128,1024]{2,1,0:T(8,128)(2,1)S(1)}, u32[]{:S(2)}, u32[]{:S(2)}) collective-permute-start(bf16[4,128,1024]{2,1,0:T(8,128)(2,1)S(1)} %broadcast_select_fusion.5), channel_id=1, source_target_pairs={{0,16},{16,0},{1,17},{17,1},{2,18},{18,2},{3,19},{19,3},{4,20},{20... | collective-permute-start | bytes 3145736 | tf_op jit(solution)/shard_map/ppermute | solution.py:1030
  460.7 4.3 collective-permute-start.28
  465.1 1.3 collective-permute-start.29
  (6 other events, 7.9 us)
Sparse Core Ops, SparseCore 0:
  18.0 167.8 all-gather.4
  187.4 103.6 all-gather.6
